TPU v7x, 32 devices: a whole 2x2x4 slice. The times are simulated.
32 devices in a mesh: wide: 8 (over y, x, core), narrow: 4 (over z).
Axes of the slice: x: 2, y: 2, z: 4, core: 2. Of those that a mesh axis runs over, the one named last changes fastest.
Arguments:
- embeddings: bfloat16 [8192, 32, 192], P(('wide', 'narrow')), may hold values from -6 to 6
- upstream: bfloat16 [8192, 16, 192], P(('wide', 'narrow')), may hold values from -6 to 6
- factor_machine_projection: bfloat16 [32, 16], replicated, may hold values from -0.078125 to 0.078125
- w_first: bfloat16 [512, 2048], replicated, may hold values from -0.25 to 0.25
- w_second: bfloat16 [2048, 1536], replicated, may hold values from -0.125 to 0.125
- compress: bfloat16 [8, 32], replicated, may hold values from -1 to 1
- norm_gain: float32 [192], replicated, may hold values from 0.5 to 2
- hot_index: int32 [8192, 16], P(('wide', 'narrow')), may hold values from 0 to 127
- cold_row: int32 [8192, 16], P(('wide', 'narrow')), may hold values from 0 to 255
- cold_owner: int32 [8192, 16, 1], P(('wide', 'narrow')), may hold values from 0 to 7; in each aligned block of 4096 rows (0 to 4095, 4096 to 8191, ..., all dimensions but the last counted through in order) at most 1024 rows name the same one
Outputs:
- grad_first: float32 [512, 2048], P(('wide', 'narrow'))
- grad_second: float32 [2048, 1536], P(('wide', 'narrow'))
- grad_proj: float32 [32, 16], replicated
- compress_gradient: float32 [8, 32], replicated
- grad_gain: float32 [192], replicated
- hot_grad: float32 [16, 128, 192], replicated
- cold_grad: float32 [16, 2048, 192], P(None, 'wide')
Inputs may be any that keep to these rules, and one draw needn't show every extreme that they name: `cold_owner`: within the 256 samples of one device (aligned blocks), no owner is named by more than 1024 cold lookups, a bound that some block reaches.
All inputs are finite; a program needn't handle non-finite values.
Results may differ from a plain program's by a relative error of at most 0.0066.
Values sent between devices are 32-bit elements; how exact they have to be, the bound alone decides.
No kernel may reach another device: no remote copies, remote signals or barrier semaphores. Data moves between devices by JAX's collectives and lax.ppermute only.
A program may use at most 128 MiB of HBM per device.

v0:
```python
import functools

import jax
import jax.numpy as jnp
from jax import lax
from jax.experimental import pallas as pl
from jax.experimental.pallas import tpu as pltpu
from jax.sharding import PartitionSpec as P

D = 192
RANK = 16
HOT_TABLES = 16
COLD_TABLES = 16
FM_OUT = 8
LC_OUT = 8
HOT_ROWS = 128
COLD_ROWS_DEV = 256
TABLES = 32
LANES = 128


NT = (((1,), (1,)), ((), ()))
NN = (((1,), (0,)), ((), ()))
GROUP = 16
OCTET = 8
VMEM = 60 * 1024 * 1024


def mm(a, b, dims=NN):
    return lax.dot_general(a, b, dims, preferred_element_type=jnp.float32)


def iota(shape, dim):
    return lax.broadcasted_iota(jnp.int32, shape, dim)


def ones_where(mask):
    return mask.astype(jnp.float32).astype(jnp.bfloat16)


def eye(size):
    return ones_where(iota((size, size), 0) == iota((size, size), 1))


def same_sample(rows, columns):
    return ones_where(
        lax.rem(iota((rows, columns), 0), GROUP) == lax.rem(iota((rows, columns), 1), GROUP)
    )


def spread_rows(count):
    return ones_where(
        lax.div(iota((count * GROUP, count), 0), GROUP) == iota((count * GROUP, count), 1)
    )


def spread_columns(count):
    return ones_where(
        lax.div(iota((count, count * GROUP), 1), GROUP) == iota((count, count * GROUP), 0)
    )


def expand(matrix):
    rows, columns = matrix.shape
    tall = mm(spread_rows(rows), matrix).astype(jnp.bfloat16)
    full = mm(tall, spread_columns(columns)).astype(jnp.bfloat16)
    return full * same_sample(rows * GROUP, columns * GROUP)


def expand_t(matrix):
    rows, columns = matrix.shape
    tall = mm(spread_rows(columns), matrix, NT).astype(jnp.bfloat16)
    full = mm(tall, spread_columns(rows)).astype(jnp.bfloat16)
    return full * same_sample(columns * GROUP, rows * GROUP)


def pick_rank():
    shape = (RANK * GROUP, OCTET * RANK)
    return ones_where(lax.div(iota(shape, 0), GROUP) == lax.rem(iota(shape, 1), RANK))


def same_table():
    shape = (OCTET * GROUP, OCTET * RANK)
    return ones_where(lax.div(iota(shape, 0), GROUP) == lax.div(iota(shape, 1), RANK))


def mlp_kernel(
    core,
    x,
    up,
    proj,
    w_first,
    w_second,
    comp,
    gain,
    second_keep,
    second_send,
    first_keep,
    first_send,
    xs,
    inner,
    d_pair,
    d_lc,
    grad_gain,
    flat,
    flat_t,
    hidden,
    hidden_t,
    slope,
    lc_out,
    d_fm,
    d_pre,
):
    step = pl.program_id(0)
    samples = x.shape[2]
    hidden_size = w_first.shape[1]
    groups = samples // GROUP

    @pl.when(step == 0)
    def _():
        unit = eye(samples)
        for n in range(TABLES):
            xs[n] = mm(unit, x[n], NT).astype(jnp.bfloat16)
        comp_rows = expand(comp[...])
        for b in range(D // GROUP):
            block = x[:, GROUP * b : GROUP * (b + 1), :].reshape(TABLES * GROUP, samples)
            lc_out[:, GROUP * b : GROUP * (b + 1), :] = mm(comp_rows, block).reshape(
                LC_OUT, GROUP, samples
            )
        proj_t = expand_t(proj[...])
        samples_match = same_sample(TABLES * GROUP, RANK * GROUP).astype(jnp.float32)
        rank_of = pick_rank()
        table_match = same_table().astype(jnp.float32)

        def group(g, carry):
            rows = pl.ds(pl.multiple_of(g * GROUP, GROUP), GROUP)
            xg = xs[:, rows, :].reshape(TABLES * GROUP, D)
            inner_g = mm(proj_t, xg).astype(jnp.bfloat16)
            inner[:, rows, :] = inner_g.reshape(RANK, GROUP, D)
            pair = (mm(xg, inner_g, NT) * samples_match).astype(jnp.bfloat16)
            for j in range(TABLES // OCTET):
                part = pair[OCTET * GROUP * j : OCTET * GROUP * (j + 1)]
                wide_part = mm(part, rank_of) * table_match
                flat[rows, OCTET * RANK * j : OCTET * RANK * (j + 1)] = jnp.sum(
                    wide_part.reshape(OCTET, GROUP, OCTET * RANK), axis=0
                ).astype(jnp.bfloat16)
            return carry

        lax.fori_loop(0, groups, group, 0)
        pairs = flat.shape[1]
        block = 256
        unit_b = eye(block)
        for b in range(pairs // block):
            at = slice(block * b, block * (b + 1))
            flat_t[at] = mm(unit_b, flat[:, at], NT).astype(jnp.bfloat16)
        for b in range(hidden_size // block):
            at = slice(block * b, block * (b + 1))
            pre = mm(flat[...], w_first[:, at])
            sigmoid_v = 1.0 / (1.0 + jnp.exp(-pre))
            slope[:, at] = sigmoid_v * (1.0 + pre * (1.0 - sigmoid_v))
            hidden_b = (pre * sigmoid_v).astype(jnp.bfloat16)
            hidden[:, at] = hidden_b
            hidden_t[at] = mm(unit_b, hidden_b, NT).astype(jnp.bfloat16)
        gain_column = jnp.sum(
            jnp.where(iota((D, D), 0) == iota((D, D), 1), gain[...], 0.0), axis=1, keepdims=True
        )
        scale = 1.0 / D
        gain_sum = jnp.zeros((D, samples), jnp.float32)

        def norm(joined, o, gain_sum):
            mean = jnp.sum(joined, axis=0, keepdims=True) * scale
            centered = joined - mean
            variance = jnp.sum(centered * centered, axis=0, keepdims=True) * scale
            inv_std = lax.rsqrt(variance + 1e-05)
            normed = centered * inv_std
            cotangent = up[o].astype(jnp.float32)
            gain_sum = gain_sum + cotangent * normed
            d_norm = cotangent * gain_column
            mean_d = jnp.sum(d_norm, axis=0, keepdims=True) * scale
            mean_n = jnp.sum(d_norm * normed, axis=0, keepdims=True) * scale
            return (inv_std * (d_norm - mean_d - normed * mean_n)).astype(jnp.bfloat16), gain_sum

        for c in range(FM_OUT // 2):
            at = slice(2 * D * c, 2 * D * (c + 1))
            fm_t = mm(hidden[...], w_second[:, at]).T
            low, gain_sum = norm(fm_t[:D], 2 * c, gain_sum)
            high, gain_sum = norm(fm_t[D:], 2 * c + 1, gain_sum)
            both = jnp.concatenate([low, high], axis=0)
            d_fm[:, at] = mm(unit, both, NT).astype(jnp.bfloat16)
        for o in range(LC_OUT):
            d_joined, gain_sum = norm(lc_out[o], FM_OUT + o, gain_sum)
            d_lc[o] = mm(unit, d_joined, NT).astype(jnp.bfloat16)
        gain_row = jnp.sum(gain_sum, axis=1, keepdims=True)
        grad_gain[...] = jnp.broadcast_to(gain_row, grad_gain.shape)
        for b in range(hidden_size // block):
            at = slice(block * b, block * (b + 1))
            d_pre[:, at] = (mm(d_fm[...], w_second[at], NT) * slope[:, at]).astype(jnp.bfloat16)
        d_pair[...] = mm(d_pre[...], w_first[...], NT).astype(jnp.bfloat16)

    mine = core[0]
    second_rows, first_rows = second_keep.shape[1], first_keep.shape[1]
    for which, second, first in ((mine, second_keep, first_keep), (1 - mine, second_send, first_send)):
        w = 2 * step + which
        rows = pl.ds(pl.multiple_of(w * second_rows, second_rows), second_rows)
        second[0] = mm(hidden_t[rows], d_fm[...])
        rows = pl.ds(pl.multiple_of(w * first_rows, first_rows), first_rows)
        first[0] = mm(flat_t[rows], d_pre[...])


def whole(shape):
    zeros = (0,) * len(shape)
    return pl.BlockSpec(shape, lambda j, c: zeros, pipeline_mode=pl.Buffered(1))


def mlp(core, x, up, proj, w_first, w_second, comp, gain, wide):
    samples = x.shape[2]
    pairs, hidden_size = w_first.shape
    outs = w_second.shape[1]
    half, second_rows, first_rows = wide // 2, hidden_size // wide, pairs // wide
    second = jax.ShapeDtypeStruct((half, second_rows, outs), jnp.float32)
    first = jax.ShapeDtypeStruct((half, first_rows, hidden_size), jnp.float32)
    rest = [
        jax.ShapeDtypeStruct((TABLES, samples, D), jnp.bfloat16),
        jax.ShapeDtypeStruct((RANK, samples, D), jnp.bfloat16),
        jax.ShapeDtypeStruct((samples, pairs), jnp.bfloat16),
        jax.ShapeDtypeStruct((LC_OUT, samples, D), jnp.bfloat16),
        jax.ShapeDtypeStruct((D, LANES), jnp.float32),
    ]

    def by_step(shape):
        return pl.BlockSpec((1,) + shape.shape[1:], lambda j, c: (j, 0, 0))

    bf16, f32 = jnp.bfloat16, jnp.float32
    return pl.pallas_call(
        mlp_kernel,
        grid_spec=pltpu.PrefetchScalarGridSpec(
            num_scalar_prefetch=1,
            grid=(half,),
            in_specs=[whole(a.shape) for a in (x, up, proj, w_first, w_second, comp, gain)],
            out_specs=[by_step(second)] * 2 + [by_step(first)] * 2 + [whole(r.shape) for r in rest],
            scratch_shapes=[
                pltpu.VMEM((samples, pairs), bf16),
                pltpu.VMEM((pairs, samples), bf16),
                pltpu.VMEM((samples, hidden_size), bf16),
                pltpu.VMEM((hidden_size, samples), bf16),
                pltpu.VMEM((samples, hidden_size), f32),
                pltpu.VMEM((LC_OUT, D, samples), f32),
                pltpu.VMEM((samples, outs), bf16),
                pltpu.VMEM((samples, hidden_size), bf16),
            ],
        ),
        out_shape=[second, second, first, first] + rest,
        compiler_params=pltpu.CompilerParams(vmem_limit_bytes=VMEM),
        cost_estimate=pl.CostEstimate(
            flops=16_000_000_000, bytes_accessed=32_000_000, transcendentals=600_000
        ),
    )(core, x, up, proj, w_first, w_second, comp, gain)


def rows_kernel(
    narrow, here, xs, inner, d_pair, d_lc, proj, comp, hot_ids, *refs
):
    colds, (hot, sums, d_rows, totals) = refs[:narrow], refs[narrow:]
    samples = xs.shape[1]
    share = COLD_TABLES // narrow
    proj_rows, comp_rows = expand(proj[...]), expand_t(comp[...])
    match = same_sample(OCTET * GROUP, RANK * GROUP)
    match_t = same_sample(RANK * GROUP, OCTET * GROUP)
    rank_of, table_match = pick_rank(), same_table()
    totals[...] = jnp.zeros_like(totals)

    def group(g, carry):
        rows = pl.ds(pl.multiple_of(g * GROUP, GROUP), GROUP)
        xg = xs[:, rows, :].reshape(TABLES * GROUP, D)
        inner_g = inner[:, rows, :].reshape(RANK * GROUP, D)
        d_lc_g = d_lc[:, rows, :].reshape(LC_OUT * GROUP, D)
        parts, parts_t = [], []
        for j in range(TABLES // OCTET):
            own = d_pair[rows, OCTET * RANK * j : OCTET * RANK * (j + 1)]
            spread = jnp.concatenate([own] * OCTET, axis=0) * table_match
            parts.append(mm(spread, rank_of, NT).astype(jnp.bfloat16) * match)
            parts_t.append(mm(rank_of, spread, NT).astype(jnp.bfloat16) * match_t)
        d_pairs = jnp.concatenate(parts, axis=0)
        d_pairs_t = jnp.concatenate(parts_t, axis=1)
        d_inner = mm(d_pairs_t, xg).astype(jnp.bfloat16)
        d_embed = mm(d_pairs, inner_g) + mm(proj_rows, d_inner) + mm(comp_rows, d_lc_g)
        d_rows[:, rows, :] = d_embed.astype(jnp.bfloat16).reshape(TABLES, GROUP, D)
        totals[...] += mm(jnp.concatenate([d_inner, d_lc_g], axis=0), xg, NT)
        return carry

    lax.fori_loop(0, samples // GROUP, group, 0)
    unit = eye(D)
    for step in range(narrow):
        target = lax.rem(here[0] + step, narrow)
        for i in range(share):
            colds[step][i] = mm(unit, d_rows[HOT_TABLES + target * share + i], NT)
    for t in range(HOT_TABLES):
        values = mm(unit, d_rows[t], NT).astype(jnp.bfloat16)
        onehot = ones_where(iota((HOT_ROWS, samples), 0) == hot_ids[t : t + 1, :])
        hot[t] = mm(values, onehot, NT)
    sums_shape = totals.shape
    own = lax.rem(iota(sums_shape, 0), GROUP) == lax.rem(iota(sums_shape, 1), GROUP)
    masked = jnp.where(own, totals[...], 0.0)
    folded = jnp.sum(masked.reshape(RANK + LC_OUT, GROUP, sums_shape[1]), axis=1)
    sums[...] = lax.dot_general(
        folded,
        spread_rows(TABLES).astype(jnp.float32),
        NN,
        precision=lax.Precision.HIGHEST,
        preferred_element_type=jnp.float32,
    )


def row_gradients(here, xs, inner, d_pair, d_lc, proj, comp, hot_ids, narrow):
    samples = xs.shape[1]
    share = COLD_TABLES // narrow
    vmem = pl.BlockSpec(memory_space=pltpu.VMEM)
    return pl.pallas_call(
        functools.partial(rows_kernel, narrow),
        in_specs=[pl.BlockSpec(memory_space=pltpu.SMEM)] + [vmem] * 7,
        out_specs=[vmem] * (narrow + 2),
        out_shape=[jax.ShapeDtypeStruct((share, D, samples), jnp.float32)] * narrow
        + [
            jax.ShapeDtypeStruct((HOT_TABLES, D, HOT_ROWS), jnp.float32),
            jax.ShapeDtypeStruct((RANK + LC_OUT, TABLES), jnp.float32),
        ],
        scratch_shapes=[
            pltpu.VMEM((TABLES, samples, D), jnp.bfloat16),
            pltpu.VMEM(((RANK + LC_OUT) * GROUP, TABLES * GROUP), jnp.float32),
        ],
        compiler_params=pltpu.CompilerParams(vmem_limit_bytes=VMEM),
        cost_estimate=pl.CostEstimate(
            flops=8_000_000_000, bytes_accessed=12_000_000, transcendentals=0
        ),
    )(here, xs, inner, d_pair, d_lc, proj, comp, hot_ids)


def bits_of(axis):
    return (lax.axis_size(axis) - 1).bit_length()


def flip(value, axis, bit):
    return lax.ppermute(value, axis, [(i, i ^ (1 << bit)) for i in range(lax.axis_size(axis))])


def my_bit(axis, bit):
    return (lax.axis_index(axis) >> bit) & 1


def halve(value, dims, axis, bit):
    dim = dims.index((axis, bit))
    me = my_bit(axis, bit)
    send = lax.dynamic_index_in_dim(value, 1 - me, dim, keepdims=False)
    keep = lax.dynamic_index_in_dim(value, me, dim, keepdims=False)
    return keep + flip(send, axis, bit), dims[:dim] + dims[dim + 1 :]


def scatter_sum(value, dims, order):
    for axis, bit in order:
        value, dims = halve(value, dims, axis, bit)
    return value


def gather_back(value, order):
    for axis, bit in reversed(order):
        got = flip(value, axis, bit)
        me = my_bit(axis, bit)
        value = jnp.stack(
            [jnp.where(me == 0, value, got), jnp.where(me == 0, got, value)], axis=0
        )
    return value


def add_rows_kernel(blocks, rows, parts, *refs):
    ids, values, out = refs[:parts], refs[parts : 2 * parts], refs[2 * parts]
    table_ids = jnp.concatenate([r[0] for r in ids], axis=1)
    table_values = jnp.concatenate([r[0].astype(jnp.bfloat16) for r in values], axis=1)
    for b in range(blocks):
        at = lax.broadcasted_iota(jnp.int32, (rows, table_ids.shape[1]), 0) + b * rows
        onehot = (at == table_ids).astype(jnp.float32).astype(jnp.bfloat16)
        out[b, 0] = lax.dot_general(
            table_values, onehot, (((1,), (1,)), ((), ())), preferred_element_type=jnp.float32
        )


def add_rows(values, ids, blocks, rows):
    tables, depth, samples = values[0].shape
    parts = len(values)
    return pl.pallas_call(
        functools.partial(add_rows_kernel, blocks, rows, parts),
        grid=(tables,),
        in_specs=[pl.BlockSpec((1, 1, samples), lambda t: (t, 0, 0))] * parts
        + [pl.BlockSpec((1, depth, samples), lambda t: (t, 0, 0))] * parts,
        out_specs=pl.BlockSpec((blocks, 1, depth, rows), lambda t: (0, t, 0, 0)),
        out_shape=jax.ShapeDtypeStruct((blocks, tables, depth, rows), jnp.float32),
        compiler_params=pltpu.CompilerParams(vmem_limit_bytes=48 * 1024 * 1024),
        cost_estimate=pl.CostEstimate(
            flops=2 * tables * depth * samples * parts * blocks * rows,
            bytes_accessed=4 * tables * depth * (samples * parts + blocks * rows),
            transcendentals=0,
        ),
    )(*ids, *values)


def local(
    embeddings,
    upstream,
    factor_machine_projection,
    w_first,
    w_second,
    compress,
    norm_gain,
    hot_index,
    cold_row,
    cold_owner,
):
    wide, narrow = lax.axis_size("wide"), lax.axis_size("narrow")
    wide_bits = [("wide", b) for b in range(bits_of("wide"))]
    narrow_bits = [("narrow", b) for b in range(bits_of("narrow"))]
    w_dims, n_dims = wide_bits[::-1], narrow_bits[::-1]
    links = wide_bits[1:]
    order_a = wide_bits[:1] + links + narrow_bits
    order_b = wide_bits[:1] + links[::-1] + narrow_bits

    sample_count = embeddings.shape[0]
    here = lax.axis_index("narrow")
    x = jnp.transpose(embeddings, (1, 2, 0))
    up = jnp.transpose(upstream, (1, 2, 0))
    core = my_bit("wide", 0).reshape(1)
    second_keep, second_send, first_keep, first_send, xs, inner, d_pair, d_lc, gain_sum = mlp(
        core,
        x,
        up,
        factor_machine_projection,
        w_first,
        w_second,
        compress,
        norm_gain.reshape(1, D),
        wide,
    )
    *cold_values, hot_local, sums = row_gradients(
        here.reshape(1),
        xs,
        inner,
        d_pair,
        d_lc,
        factor_machine_projection,
        compress,
        hot_index.T,
        narrow,
    )
    grad_gain = gain_sum[:, 0]
    grad_proj, compress_gradient = sums[:RANK].T, sums[RANK:]

    share = COLD_TABLES // narrow
    cold_ids = (cold_owner[:, :, 0] * COLD_ROWS_DEV + cold_row).T.reshape(
        narrow, share, 1, sample_count
    )
    got_ids, got_values = [], []
    for step in range(narrow):
        target = (here + step) % narrow
        ids = lax.dynamic_index_in_dim(cold_ids, target, 0, keepdims=False)
        values = cold_values[step]
        if step:
            ring = [(i, (i + step) % narrow) for i in range(narrow)]
            ids, values = lax.ppermute(ids, "narrow", ring), lax.ppermute(values, "narrow", ring)
        got_ids.append(ids)
        got_values.append(values)
    cold_dense = add_rows(got_values, got_ids, wide, COLD_ROWS_DEV)
    half = share // 2
    cold_dense = cold_dense.reshape([2] * len(w_dims) + [2, half, D, COLD_ROWS_DEV])
    lead = (slice(None),) * len(w_dims)
    cold_pieces = []
    for piece, order in ((0, order_a), (1, order_b)):
        value = scatter_sum(cold_dense[lead + (piece,)], w_dims, order[: len(w_dims)])
        cold_pieces.append(value)
    cold_mine = jnp.concatenate(cold_pieces, axis=0)
    cold_grad = jnp.zeros((narrow, share, D, COLD_ROWS_DEV), jnp.float32)
    ring = [(i, (i + 1) % narrow) for i in range(narrow)]
    value = cold_mine
    for step in range(narrow):
        if step:
            value = lax.ppermute(value, "narrow", ring)
        cold_grad = lax.dynamic_update_index_in_dim(
            cold_grad, value, (here - step) % narrow, 0
        )
    cold_grad = jnp.transpose(
        cold_grad.reshape(COLD_TABLES, D, COLD_ROWS_DEV), (0, 2, 1)
    )

    dims = w_dims + n_dims
    devices = wide * narrow

    def reduce_matrix(keep, send):
        got = flip(send, "wide", 0)
        own, columns = keep.shape[1] // narrow, keep.shape[2]
        left = dims[: len(w_dims) - 1] + n_dims
        if own % 16:
            pieces = [(slice(None), order_a)]
        else:
            pieces = [(slice(0, own // 2), order_a), (slice(own // 2, own), order_b)]
        done = []
        for rows, order in pieces:
            lead = (slice(None),) * len(left)
            size = [2] * len(left) + [own, columns]
            value = keep.reshape(size)[lead + (rows,)] + got.reshape(size)[lead + (rows,)]
            done.append(scatter_sum(value, left, order[1:]))
        return jnp.concatenate(done, axis=0)

    grad_second = reduce_matrix(second_keep, second_send)
    grad_first = reduce_matrix(first_keep, first_send)

    hot_rows = hot_local.size // LANES
    small = jnp.concatenate([grad_proj.reshape(-1), compress_gradient.reshape(-1), grad_gain])
    small = jnp.pad(small, (0, -small.size % LANES)).reshape(-1, LANES)
    shared = jnp.concatenate([hot_local.reshape(hot_rows, LANES), small], axis=0)
    shared = jnp.pad(shared, ((0, -shared.shape[0] % (8 * devices)), (0, 0)))
    order = order_a
    shared = shared.reshape([2] * len(dims) + [-1, LANES])
    mine = scatter_sum(shared, order, order)
    shared = gather_back(mine, order).reshape(-1, LANES)
    hot_grad = jnp.transpose(shared[:hot_rows].reshape(HOT_TABLES, D, HOT_ROWS), (0, 2, 1))
    small = shared[hot_rows:].reshape(-1)
    n_proj, n_compress = TABLES * RANK, LC_OUT * TABLES
    grad_proj = small[:n_proj].reshape(TABLES, RANK)
    compress_gradient = small[n_proj : n_proj + n_compress].reshape(LC_OUT, TABLES)
    grad_gain = small[n_proj + n_compress : n_proj + n_compress + D]
    return (grad_first, grad_second, grad_proj, compress_gradient, grad_gain, hot_grad, cold_grad)


def solution(mesh):
    placed = (
        P(("wide", "narrow"), None, None),
        P(("wide", "narrow"), None, None),
        P(),
        P(),
        P(),
        P(),
        P(),
        P(("wide", "narrow"), None),
        P(("wide", "narrow"), None),
        P(("wide", "narrow"), None, None),
    )
    return jax.shard_map(
        local,
        mesh=mesh,
        in_specs=placed,
        out_specs=(
            P(("wide", "narrow"), None),
            P(("wide", "narrow"), None),
            P(),
            P(),
            P(),
            P(),
            P(None, "wide", None),
        ),
        check_vma=False,
    )
```

profile of v0, /device:TPU:0, one launch (start us, length us, event | category | flops | bytes accessed | tf_op | source)
XLA Modules:
  0.0 341.1 jit_solution(16491553097917291636)
XLA Ops:
  2.0 37.0 %shard_map.153 = (f32[4,256,1536]{2,1,0:T(8,128)}, f32[4,256,1536]{2,1,0:T(8,128)}, f32[4,64,2048]{2,1,0:T(8,128)}, f32[4,64,2048]{2,1,0:T(8,128)}, bf16[32,256,...) custom-call(s32[1]{0:T(128)} %bitcast.core, ...), custom_call_target="tpu_custom_call" | custom-call | flops 16000000000 | bytes 32000000 | tf_op jit(solution)/shard_map/pallas_call | solution.py:234
  39.0 24.7 %shard_map.154 = (f32[4,192,256]{2,1,0:T(8,128)}, f32[4,192,256]{2,1,0:T(8,128)}, f32[4,192,256]{2,1,0:T(8,128)}, f32[4,192,256]{2,1,0:T(8,128)}, f32[16,192,128]{2,1,0:T(8,128)}, /*index=5*/f32[24,32]{1,0:T(8,128)}) custom-call(s32[1]{0:T(128)} %bitcast.40.here, bf16[32,256,192]{2,1,0:T(8,128)(2,1)} %get-tuple-element.26.xs, ...), custom_call_target="tpu_custom_call" | custom-call | flops 8000000000 | bytes 12000000 | tf_op jit(solution)/shard_map/pallas_call | solution.py:318
  78.9 4.9 %collective-permute-done.19 = f32[2,2,2,104,128]{4,3,2,1,0:T(8,128)} collective-permute-done((f32[2,2,2,104,128]{4,3,2,1,0:T(8,128)}, f32[2,2,2,104,128]{4,3,2,1,0:T(8,128)}, u32[]{:S(2)}, u32[]{:S(2)}) %collective-permute-start.19) | collective-permute-done | bytes 426016 | tf_op jit(solution)/shard_map/ppermute | solution.py:343
  86.9 5.0 %collective-permute-done.20 = f32[2,2,104,128]{3,2,1,0:T(8,128)S(1)} collective-permute-done((f32[2,2,104,128]{3,2,1,0:T(8,128)S(1)}, f32[2,2,104,128]{3,2,1,0:T(8,128)S(1)}, u32[]{:S(2)}, u32[]{:S(2)}) %collective-permute-start.20) | collective-permute-done | bytes 213024 | tf_op jit(solution)/shard_map/ppermute | solution.py:343
  93.5 37.3 %collective-permute-done.21 = f32[2,104,128]{2,1,0:T(8,128)} collective-permute-done((f32[2,104,128]{2,1,0:T(8,128)S(1)}, f32[2,104,128]{2,1,0:T(8,128)}, u32[]{:S(2)}, u32[]{:S(2)}) %collective-permute-start.21) | collective-permute-done | bytes 106528 | tf_op jit(solution)/shard_map/ppermute | solution.py:343
  132.5 5.5 %collective-permute-done.28.refs_1_ = s32[4,1,256]{2,1,0:T(1,128)S(1)} collective-permute-done((s32[4,1,256]{2,1,0:T(1,128)S(1)}, s32[4,1,256]{2,1,0:T(1,128)S(1)}, u32[]{:S(2)}, u32[]{:S(2)}) %collective-permute-start.28) | collective-permute-done | bytes 4128 | tf_op jit(solution)/shard_map/ppermute | solution.py:466
  138.0 10.4 %collective-permute-start.29 = (s32[4,1,256]{2,1,0:T(1,128)S(1)}, s32[4,1,256]{2,1,0:T(1,128)S(1)}, u32[]{:S(2)}, u32[]{:S(2)}) collective-permute-start(s32[4,1,256]{2,1,0:T(1,128)S(1)} %get-tuple-element.61), channel_id=1, source_target_pairs={{0,2},{1,3},{2,0},{3,1},{4,6},{5,7},{6,4},{7,5},{8,10},{9,11},{10,... | collective-permute-start | bytes 12296 | tf_op jit(solution)/shard_map/ppermute | solution.py:466
  153.0 7.3 %shard_map.155 = f32[8,4,192,256]{3,2,1,0:T(8,128)} custom-call(s32[4,1,256]{2,1,0:T(1,128)S(1)} %get-tuple-element.63.refs_0_, s32[4,1,256]{2,1,0:T(1,128)S(1)} %collective-permute-done.28.refs_1_, s32[4,1,256]{2,1,0:T(1,128)S(1)} %collective-permute-done.29.refs_2_, s32[4,1,256]{2,1,0:T(1,128)S(1)} %collective-permute-done.30.refs_3_, ...), custom_call_target="tpu_custom_call" | custom-call | flops 3221225472 | bytes 9437184 | tf_op jit(solution)/shard_map/pallas_call | solution.py:389
  162.7 3.4 %fusion.6 = (f32[2,2,2,1,2,192,256]{6,5,4,3,2,1,0:T(8,128)S(1)}, f32[2,2,2,1,2,192,256]{6,5,4,3,2,1,0:T(8,128)S(1)}) fusion(f32[2,2,2,2,2,192,256]{6,5,4,3,2,1,0:T(8,128)} %bitcast.182), kind=kLoop, calls=%fused_computation.100 | loop fusion | bytes 12582912 | tf_op jit(solution)/shard_map/slice | solution.py:475
  182.6 4.4 %collective-permute-done.26 = f32[2,2,2,104,128]{4,3,2,1,0:T(8,128)S(1)} collective-permute-done((f32[2,2,2,104,128]{4,3,2,1,0:T(8,128)S(1)}, f32[2,2,2,104,128]{4,3,2,1,0:T(8,128)S(1)}, u32[]{:S(2)}, u32[]{:S(2)}) %collective-permute-start.26) | collective-permute-done | bytes 426016 | tf_op jit(solution)/shard_map/ppermute | solution.py:343
  187.7 4.1 %collective-permute-done.5 = f32[2,2,2,8,2048]{4,3,2,1,0:T(8,128)S(1)} collective-permute-done((f32[2,2,2,8,2048]{4,3,2,1,0:T(8,128)S(1)}, f32[2,2,2,8,2048]{4,3,2,1,0:T(8,128)S(1)}, u32[]{:S(2)}, u32[]{:S(2)}) %collective-permute-start.5) | collective-permute-done | bytes 524320 | tf_op jit(solution)/shard_map/ppermute | solution.py:343
  191.9 6.3 %collective-permute-done.1 = f32[2,2,2,8,2048]{4,3,2,1,0:T(8,128)S(1)} collective-permute-done((f32[2,2,2,8,2048]{4,3,2,1,0:T(8,128)S(1)}, f32[2,2,2,8,2048]{4,3,2,1,0:T(8,128)S(1)}, u32[]{:S(2)}, u32[]{:S(2)}) %collective-permute-start.1) | collective-permute-done | bytes 524320 | tf_op jit(solution)/shard_map/ppermute | solution.py:343
  198.9 18.7 %collective-permute-done.6 = f32[2,2,8,2048]{3,2,1,0:T(8,128)S(1)} collective-permute-done((f32[2,2,8,2048]{3,2,1,0:T(8,128)S(1)}, f32[2,2,8,2048]{3,2,1,0:T(8,128)S(1)}, u32[]{:S(2)}, u32[]{:S(2)}) %collective-permute-start.6) | collective-permute-done | bytes 262176 | tf_op jit(solution)/shard_map/ppermute | solution.py:343
  218.8 5.1 %collective-permute-done.2 = f32[2,2,8,2048]{3,2,1,0:T(8,128)S(1)} collective-permute-done((f32[2,2,8,2048]{3,2,1,0:T(8,128)S(1)}, f32[2,2,8,2048]{3,2,1,0:T(8,128)S(1)}, u32[]{:S(2)}, u32[]{:S(2)}) %collective-permute-start.2) | collective-permute-done | bytes 262176 | tf_op jit(solution)/shard_map/ppermute | solution.py:343
  225.1 4.1 %collective-permute-done.7 = f32[2,8,2048]{2,1,0:T(8,128)S(1)} collective-permute-done((f32[2,8,2048]{2,1,0:T(8,128)S(1)}, f32[2,8,2048]{2,1,0:T(8,128)S(1)}, u32[]{:S(2)}, u32[]{:S(2)}) %collective-permute-start.7) | collective-permute-done | bytes 131104 | tf_op jit(solution)/shard_map/ppermute | solution.py:343
  230.4 4.4 %collective-permute-done.3 = f32[2,8,2048]{2,1,0:T(8,128)S(1)} collective-permute-done((f32[2,8,2048]{2,1,0:T(8,128)S(1)}, f32[2,8,2048]{2,1,0:T(8,128)S(1)}, u32[]{:S(2)}, u32[]{:S(2)}) %collective-permute-start.3) | collective-permute-done | bytes 131104 | tf_op jit(solution)/shard_map/ppermute | solution.py:343
  242.0 3.9 %collective-permute-done.39 = f32[2,192,256]{2,1,0:T(8,128)S(1)} collective-permute-done((f32[2,192,256]{2,1,0:T(8,128)S(1)}, f32[2,192,256]{2,1,0:T(8,128)S(1)}, u32[]{:S(2)}, u32[]{:S(2)}) %collective-permute-start.39) | collective-permute-done | bytes 393248 | tf_op jit(solution)/shard_map/ppermute | solution.py:343
  251.1 19.5 %collective-permute-done.40 = f32[4,192,256]{2,1,0:T(8,128)} collective-permute-done((f32[4,192,256]{2,1,0:T(8,128)S(1)}, f32[4,192,256]{2,1,0:T(8,128)}, u32[]{:S(2)}, u32[]{:S(2)}) %collective-permute-start.40) | collective-permute-done | bytes 786464 | tf_op jit(solution)/shard_map/ppermute | solution.py:483
  270.7 4.2 %slice_add_fusion.1 = (f32[2,2,2,2,32,1536]{5,4,3,2,1,0:T(8,128)S(1)}, f32[2,2,2,2,32,1536]{5,4,3,2,1,0:T(8,128)S(1)}) fusion(f32[2,2,2,2,64,1536]{5,4,3,2,1,0:T(8,128)} %bitcast.23, f32[2,2,2,2,64,1536]{5,4,3,2,1,0:T(8,128)S(1)} %bitcast.185), kind=kLoop, calls=%fused_computation.1 | loop fusion | flops 1572864 | bytes 18874368 | tf_op jit(solution)/shard_map/add | solution.py:506
  287.1 5.5 %collective-permute-done.41 = f32[4,192,256]{2,1,0:T(8,128)} collective-permute-done((f32[4,192,256]{2,1,0:T(8,128)}, f32[4,192,256]{2,1,0:T(8,128)}, u32[]{:S(2)}, u32[]{:S(2)}) %collective-permute-start.41) | collective-permute-done | bytes 786464 | tf_op jit(solution)/shard_map/ppermute | solution.py:483
  293.8 11.7 %collective-permute-done.14 = f32[2,2,2,32,1536]{4,3,2,1,0:T(8,128)} collective-permute-done((f32[2,2,2,32,1536]{4,3,2,1,0:T(8,128)}, f32[2,2,2,32,1536]{4,3,2,1,0:T(8,128)}, u32[]{:S(2)}, u32[]{:S(2)}) %collective-permute-start.14) | collective-permute-done | bytes 1572896 | tf_op jit(solution)/shard_map/ppermute | solution.py:343
  310.7 8.6 %collective-permute-done.15 = f32[2,2,32,1536]{3,2,1,0:T(8,128)S(1)} collective-permute-done((f32[2,2,32,1536]{3,2,1,0:T(8,128)S(1)}, f32[2,2,32,1536]{3,2,1,0:T(8,128)S(1)}, u32[]{:S(2)}, u32[]{:S(2)}) %collective-permute-start.15) | collective-permute-done | bytes 786464 | tf_op jit(solution)/shard_map/ppermute | solution.py:343
  321.8 5.5 %collective-permute-done.16 = f32[2,32,1536]{2,1,0:T(8,128)S(1)} collective-permute-done((f32[2,32,1536]{2,1,0:T(8,128)S(1)}, f32[2,32,1536]{2,1,0:T(8,128)S(1)}, u32[]{:S(2)}, u32[]{:S(2)}) %collective-permute-start.16) | collective-permute-done | bytes 393248 | tf_op jit(solution)/shard_map/ppermute | solution.py:343
  336.1 4.2 %collective-permute-done.13 = f32[32,1536]{1,0:T(8,128)S(1)} collective-permute-done((f32[32,1536]{1,0:T(8,128)S(1)}, f32[32,1536]{1,0:T(8,128)S(1)}, u32[]{:S(2)}, u32[]{:S(2)}) %collective-permute-start.13) | collective-permute-done | bytes 196640 | tf_op jit(solution)/shard_map/ppermute | solution.py:343
  (192 shorter events, 94.0 us)
Async XLA Ops:
  70.5 13.3 %collective-permute-start.19 = (f32[2,2,2,104,128]{4,3,2,1,0:T(8,128)}, f32[2,2,2,104,128]{4,3,2,1,0:T(8,128)}, u32[]{:S(2)}, u32[]{:S(2)}) collective-permute-start(f32[2,2,2,104,128]{4,3,2,1,0:T(8,128)} %dynamic-slice_bitcast_fusion.11), channel_id=1, source_target_pairs={{0,8},{4,12},{8,0},{12,4},{16,24},{20,28},{24,16},{28,20},{1,9},{5... | collective-permute-start | bytes 1277960 | tf_op jit(solution)/shard_map/ppermute | solution.py:343
  73.3 79.6 %collective-permute-start.31 = (f32[4,192,256]{2,1,0:T(8,128)}, f32[4,192,256]{2,1,0:T(8,128)S(1)}, u32[]{:S(2)}, u32[]{:S(2)}) collective-permute-start(f32[4,192,256]{2,1,0:T(8,128)} %get-tuple-element.34), channel_id=1, source_target_pairs={{0,1},{1,2},{2,3},{3,0},{4,5},{5,6},{6,7},{7,4},{8,9},{9,10},{10,1... | collective-permute-start | bytes 2359304 | tf_op jit(solution)/shard_map/ppermute | solution.py:466
  74.9 78.0 %collective-permute-start.32 = (f32[4,192,256]{2,1,0:T(8,128)}, f32[4,192,256]{2,1,0:T(8,128)S(1)}, u32[]{:S(2)}, u32[]{:S(2)}) collective-permute-start(f32[4,192,256]{2,1,0:T(8,128)} %get-tuple-element.35), channel_id=1, source_target_pairs={{0,2},{1,3},{2,0},{3,1},{4,6},{5,7},{6,4},{7,5},{8,10},{9,11},{10,... | collective-permute-start | bytes 2359304 | tf_op jit(solution)/shard_map/ppermute | solution.py:466
  77.5 75.4 %collective-permute-start.33 = (f32[4,192,256]{2,1,0:T(8,128)}, f32[4,192,256]{2,1,0:T(8,128)S(1)}, u32[]{:S(2)}, u32[]{:S(2)}) collective-permute-start(f32[4,192,256]{2,1,0:T(8,128)} %get-tuple-element.36), channel_id=1, source_target_pairs={{0,3},{1,0},{2,1},{3,2},{4,7},{5,4},{6,5},{7,6},{8,11},{9,8},{10,9... | collective-permute-start | bytes 2359304 | tf_op jit(solution)/shard_map/ppermute | solution.py:466
  91.9 38.9 %collective-permute-start.21 = (f32[2,104,128]{2,1,0:T(8,128)S(1)}, f32[2,104,128]{2,1,0:T(8,128)}, u32[]{:S(2)}, u32[]{:S(2)}) collective-permute-start(f32[2,104,128]{2,1,0:T(8,128)S(1)} %dynamic-slice_bitcast_fusion.23), channel_id=1, source_target_pairs={{0,1},{1,0},{2,3},{3,2},{4,5},{5,4},{6,7},{7,6},{8,9},{9,8},{10,11... | collective-permute-start | bytes 319496 | tf_op jit(solution)/shard_map/ppermute | solution.py:343
  131.8 16.7 %collective-permute-start.22 = (f32[104,128]{1,0:T(8,128)S(1)}, f32[104,128]{1,0:T(8,128)S(1)}, u32[]{:S(2)}, u32[]{:S(2)}) collective-permute-start(f32[104,128]{1,0:T(8,128)S(1)} %dynamic-slice_bitcast_fusion.26), channel_id=1, source_target_pairs={{0,2},{1,3},{2,0},{3,1},{4,6},{5,7},{6,4},{7,5},{8,10},{9,11},{10,... | collective-permute-start | bytes 159752 | tf_op jit(solution)/shard_map/ppermute | solution.py:343
  138.0 12.0 %collective-permute-start.29 = (s32[4,1,256]{2,1,0:T(1,128)S(1)}, s32[4,1,256]{2,1,0:T(1,128)S(1)}, u32[]{:S(2)}, u32[]{:S(2)}) collective-permute-start(s32[4,1,256]{2,1,0:T(1,128)S(1)} %get-tuple-element.61), channel_id=1, source_target_pairs={{0,2},{1,3},{2,0},{3,1},{4,6},{5,7},{6,4},{7,5},{8,10},{9,11},{10,... | collective-permute-start | bytes 12296 | tf_op jit(solution)/shard_map/ppermute | solution.py:466
  150.0 24.8 %collective-permute-start = (f32[4,64,2048]{2,1,0:T(8,128)}, f32[4,64,2048]{2,1,0:T(8,128)}, u32[]{:S(2)}, u32[]{:S(2)}) collective-permute-start(f32[4,64,2048]{2,1,0:T(8,128)} %get-tuple-element.23), channel_id=1, source_target_pairs={{0,4},{4,0},{8,12},{12,8},{16,20},{20,16},{24,28},{28,24},{1,5},{5... | collective-permute-start | bytes 6291464 | tf_op jit(solution)/shard_map/ppermute | solution.py:343
  169.8 100.8 %collective-permute-start.9 = (f32[4,256,1536]{2,1,0:T(8,128)}, f32[4,256,1536]{2,1,0:T(8,128)}, u32[]{:S(2)}, u32[]{:S(2)}) collective-permute-start(f32[4,256,1536]{2,1,0:T(8,128)} %get-tuple-element.25), channel_id=1, source_target_pairs={{0,4},{4,0},{8,12},{12,8},{16,20},{20,16},{24,28},{28,24},{1,5},{5... | collective-permute-start | bytes 18874376 | tf_op jit(solution)/shard_map/ppermute | solution.py:343
  174.2 12.8 %collective-permute-start.26 = (f32[2,2,2,104,128]{4,3,2,1,0:T(8,128)S(1)}, f32[2,2,2,104,128]{4,3,2,1,0:T(8,128)S(1)}, u32[]{:S(2)}, u32[]{:S(2)}) collective-permute-start(f32[2,2,2,104,128]{4,3,2,1,0:T(8,128)S(1)} %pad_maximum_fusion.3), channel_id=1, source_target_pairs={{0,8},{4,12},{8,0},{12,4},{16,24},{20,28},{24,16},{28,20},{1,9},{5... | collective-permute-start | bytes 1277960 | tf_op jit(solution)/shard_map/ppermute | solution.py:343
  176.9 14.9 %collective-permute-start.5 = (f32[2,2,2,8,2048]{4,3,2,1,0:T(8,128)S(1)}, f32[2,2,2,8,2048]{4,3,2,1,0:T(8,128)S(1)}, u32[]{:S(2)}, u32[]{:S(2)}) collective-permute-start(f32[2,2,2,8,2048]{4,3,2,1,0:T(8,128)S(1)} %dynamic-slice_bitcast_fusion.9), channel_id=1, source_target_pairs={{0,16},{4,20},{8,24},{12,28},{16,0},{20,4},{24,8},{28,12},{1,17},{... | collective-permute-start | bytes 1572872 | tf_op jit(solution)/shard_map/ppermute | solution.py:343
  178.5 19.7 %collective-permute-start.1 = (f32[2,2,2,8,2048]{4,3,2,1,0:T(8,128)S(1)}, f32[2,2,2,8,2048]{4,3,2,1,0:T(8,128)S(1)}, u32[]{:S(2)}, u32[]{:S(2)}) collective-permute-start(f32[2,2,2,8,2048]{4,3,2,1,0:T(8,128)S(1)} %dynamic-slice_bitcast_fusion.10), channel_id=1, source_target_pairs={{0,8},{4,12},{8,0},{12,4},{16,24},{20,28},{24,16},{28,20},{1,9},{5... | collective-permute-start | bytes 1572872 | tf_op jit(solution)/shard_map/ppermute | solution.py:343
  181.8 54.0 %collective-permute-start.38 = (f32[2,2,192,256]{3,2,1,0:T(8,128)S(1)}, f32[2,2,192,256]{3,2,1,0:T(8,128)S(1)}, u32[]{:S(2)}, u32[]{:S(2)}) collective-permute-start(f32[2,2,192,256]{3,2,1,0:T(8,128)S(1)} %dynamic-slice_bitcast_fusion.5), channel_id=1, source_target_pairs={{0,16},{4,20},{8,24},{12,28},{16,0},{20,4},{24,8},{28,12},{1,17},{... | collective-permute-start | bytes 2359304 | tf_op jit(solution)/shard_map/ppermute | solution.py:343
  187.0 51.0 %collective-permute-start.35 = (f32[2,2,192,256]{3,2,1,0:T(8,128)S(1)}, f32[2,2,192,256]{3,2,1,0:T(8,128)S(1)}, u32[]{:S(2)}, u32[]{:S(2)}) collective-permute-start(f32[2,2,192,256]{3,2,1,0:T(8,128)S(1)} %dynamic-slice_bitcast_fusion.6), channel_id=1, source_target_pairs={{0,8},{4,12},{8,0},{12,4},{16,24},{20,28},{24,16},{28,20},{1,9},{5... | collective-permute-start | bytes 2359304 | tf_op jit(solution)/shard_map/ppermute | solution.py:343
  191.8 59.0 %collective-permute-start.27 = (f32[2,2,2,2,104,128]{5,4,3,2,1,0:T(8,128)S(1)}, f32[2,2,2,2,104,128]{5,4,3,2,1,0:T(8,128)S(1)}, u32[]{:S(2)}, u32[]{:S(2)}) collective-permute-start(f32[2,2,2,2,104,128]{5,4,3,2,1,0:T(8,128)S(1)} %pad_maximum_fusion.1), channel_id=1, source_target_pairs={{0,4},{4,0},{8,12},{12,8},{16,20},{20,16},{24,28},{28,24},{1,5},{5... | collective-permute-start | bytes 2555912 | tf_op jit(solution)/shard_map/ppermute | solution.py:343
  198.2 19.3 %collective-permute-start.6 = (f32[2,2,8,2048]{3,2,1,0:T(8,128)S(1)}, f32[2,2,8,2048]{3,2,1,0:T(8,128)S(1)}, u32[]{:S(2)}, u32[]{:S(2)}) collective-permute-start(f32[2,2,8,2048]{3,2,1,0:T(8,128)S(1)} %dynamic-slice_bitcast_fusion.16), channel_id=1, source_target_pairs={{0,8},{4,12},{8,0},{12,4},{16,24},{20,28},{24,16},{28,20},{1,9},{5... | collective-permute-start | bytes 786440 | tf_op jit(solution)/shard_map/ppermute | solution.py:343
  235.7 14.4 %collective-permute-start.4 = (f32[8,2048]{1,0:T(8,128)S(1)}, f32[8,2048]{1,0:T(8,128)S(1)}, u32[]{:S(2)}, u32[]{:S(2)}) collective-permute-start(f32[8,2048]{1,0:T(8,128)S(1)} %dynamic-slice_bitcast_fusion.25), channel_id=1, source_target_pairs={{0,2},{1,3},{2,0},{3,1},{4,6},{5,7},{6,4},{7,5},{8,10},{9,11},{10,... | collective-permute-start | bytes 196616 | tf_op jit(solution)/shard_map/ppermute | solution.py:343
  250.0 20.6 %collective-permute-start.40 = (f32[4,192,256]{2,1,0:T(8,128)S(1)}, f32[4,192,256]{2,1,0:T(8,128)}, u32[]{:S(2)}, u32[]{:S(2)}) collective-permute-start(f32[4,192,256]{2,1,0:T(8,128)S(1)} %pad_maximum_fusion.2), channel_id=1, source_target_pairs={{0,1},{1,2},{2,3},{3,0},{4,5},{5,6},{6,7},{7,4},{8,9},{9,10},{10,1... | collective-permute-start | bytes 2359304 | tf_op jit(solution)/shard_map/ppermute | solution.py:483
  270.6 21.9 %collective-permute-start.41 = (f32[4,192,256]{2,1,0:T(8,128)}, f32[4,192,256]{2,1,0:T(8,128)}, u32[]{:S(2)}, u32[]{:S(2)}) collective-permute-start(f32[4,192,256]{2,1,0:T(8,128)} %collective-permute-done.40), channel_id=1, source_target_pairs={{0,1},{1,2},{2,3},{3,0},{4,5},{5,6},{6,7},{7,4},{8,9},{9,10},{10,1... | collective-permute-start | bytes 2359304 | tf_op jit(solution)/shard_map/ppermute | solution.py:483
  276.4 29.2 %collective-permute-start.14 = (f32[2,2,2,32,1536]{4,3,2,1,0:T(8,128)}, f32[2,2,2,32,1536]{4,3,2,1,0:T(8,128)}, u32[]{:S(2)}, u32[]{:S(2)}) collective-permute-start(f32[2,2,2,32,1536]{4,3,2,1,0:T(8,128)} %dynamic-slice_bitcast_fusion.2), channel_id=1, source_target_pairs={{0,16},{4,20},{8,24},{12,28},{16,0},{20,4},{24,8},{28,12},{1,17},{... | collective-permute-start | bytes 4718600 | tf_op jit(solution)/shard_map/ppermute | solution.py:343
  277.7 30.1 %collective-permute-start.10 = (f32[2,2,2,32,1536]{4,3,2,1,0:T(8,128)}, f32[2,2,2,32,1536]{4,3,2,1,0:T(8,128)}, u32[]{:S(2)}, u32[]{:S(2)}) collective-permute-start(f32[2,2,2,32,1536]{4,3,2,1,0:T(8,128)} %dynamic-slice_bitcast_fusion.3), channel_id=1, source_target_pairs={{0,8},{4,12},{8,0},{12,4},{16,24},{20,28},{24,16},{28,20},{1,9},{5... | collective-permute-start | bytes 4718600 | tf_op jit(solution)/shard_map/ppermute | solution.py:343
  292.6 18.1 %collective-permute-start.42 = (f32[4,192,256]{2,1,0:T(8,128)}, f32[4,192,256]{2,1,0:T(8,128)S(1)}, u32[]{:S(2)}, u32[]{:S(2)}) collective-permute-start(f32[4,192,256]{2,1,0:T(8,128)} %collective-permute-done.41), channel_id=1, source_target_pairs={{0,1},{1,2},{2,3},{3,0},{4,5},{5,6},{6,7},{7,4},{8,9},{9,10},{10,1... | collective-permute-start | bytes 2359304 | tf_op jit(solution)/shard_map/ppermute | solution.py:483
  307.3 12.1 %collective-permute-start.15 = (f32[2,2,32,1536]{3,2,1,0:T(8,128)S(1)}, f32[2,2,32,1536]{3,2,1,0:T(8,128)S(1)}, u32[]{:S(2)}, u32[]{:S(2)}) collective-permute-start(f32[2,2,32,1536]{3,2,1,0:T(8,128)S(1)} %dynamic-slice_bitcast_fusion.7), channel_id=1, source_target_pairs={{0,8},{4,12},{8,0},{12,4},{16,24},{20,28},{24,16},{28,20},{1,9},{5... | collective-permute-start | bytes 2359304 | tf_op jit(solution)/shard_map/ppermute | solution.py:343
  309.5 12.1 %collective-permute-start.11 = (f32[2,2,32,1536]{3,2,1,0:T(8,128)S(1)}, f32[2,2,32,1536]{3,2,1,0:T(8,128)S(1)}, u32[]{:S(2)}, u32[]{:S(2)}) collective-permute-start(f32[2,2,32,1536]{3,2,1,0:T(8,128)S(1)} %dynamic-slice_bitcast_fusion.8), channel_id=1, source_target_pairs={{0,16},{4,20},{8,24},{12,28},{16,0},{20,4},{24,8},{28,12},{1,17},{... | collective-permute-start | bytes 2359304 | tf_op jit(solution)/shard_map/ppermute | solution.py:343
  (34 other events, 385.1 us)
where the time goes:
time: 342 us; the launch traced here: 341 us
  waiting for transfers between devices  178 us (52%)
  Pallas kernels  69 us (20%)
  starting transfers between devices  50.1 us (15%)
  local copies, waits for them, and re-layouts  23.1 us (7%)
  other arithmetic  19.8 us (6%)
    ppermute x34, waiting for transfers between devices, flip(): lax.ppermute(value, axis, [(i, i ^ 1 << bit) for i in range(lax.axis_size...  145 us
    pallas_call x1, Pallas kernels, mlp(): pl.pallas_call(mlp_kernel, grid_spec=pltpu.PrefetchScalarGridSpec(num_sca...  37 us
    ppermute x34, starting transfers between devices, flip(): lax.ppermute(value, axis, [(i, i ^ 1 << bit) for i in range(lax.axis_size...  33.2 us
    ppermute x3, waiting for transfers between devices, local(): value = lax.ppermute(value, 'narrow', ring)  25.1 us
    pallas_call x1, Pallas kernels, row_gradients(): pl.pallas_call(functools.partial(rows_kernel, narrow), in_specs=[pl.Block...  24.7 us
    ppermute x3, starting transfers between devices, local(): lax.ppermute(ids, 'narrow', ring)  11.3 us
    ppermute x3, waiting for transfers between devices, local(): lax.ppermute(ids, 'narrow', ring)  8.25 us
    add x27, other arithmetic, halve(): return (keep + flip(send, axis, bit), dims[:dim] + dims[dim + 1:])  8.21 us
  transfers between devices with their start and end apart: 43, of which 27 were waited for; matrix products, arithmetic and copies ran while one was open for 10% of the time, Pallas kernels for 2%

commit v1 on v0

--- a/solution.py
+++ b/solution.py
@@ -17,6 +17,8 @@
 COLD_ROWS_DEV = 256
 TABLES = 32
 LANES = 128
+COLUMNS = 512
+ID_ROWS = 8
 
 
 NT = (((1,), (1,)), ((), ()))
@@ -85,6 +87,7 @@
 
 
 def mlp_kernel(
+    wide,
     core,
     x,
     up,
@@ -93,10 +96,8 @@
     w_second,
     comp,
     gain,
-    second_keep,
-    second_send,
-    first_keep,
-    first_send,
+    keep,
+    send,
     xs,
     inner,
     d_pair,
@@ -146,7 +147,7 @@
                 ).astype(jnp.bfloat16)
             return carry
 
-        lax.fori_loop(0, groups, group, 0)
+        lax.fori_loop(0, groups, group, 0, unroll=2)
         pairs = flat.shape[1]
         block = 256
         unit_b = eye(block)
@@ -198,13 +199,24 @@
         d_pair[...] = mm(d_pre[...], w_first[...], NT).astype(jnp.bfloat16)
 
     mine = core[0]
-    second_rows, first_rows = second_keep.shape[1], first_keep.shape[1]
-    for which, second, first in ((mine, second_keep, first_keep), (1 - mine, second_send, first_send)):
+    narrow = keep.shape[1]
+    second_rows = hidden_t.shape[0] // wide
+    first_rows = flat_t.shape[0] // wide
+    own_second, own_first = second_rows // narrow, first_rows // narrow
+    second_cuts, first_cuts = d_fm.shape[1] // COLUMNS, hidden_size // COLUMNS
+    for which, out in ((1 - mine, send), (mine, keep)):
         w = 2 * step + which
         rows = pl.ds(pl.multiple_of(w * second_rows, second_rows), second_rows)
-        second[0] = mm(hidden_t[rows], d_fm[...])
+        for c in range(second_cuts):
+            part = mm(hidden_t[rows], d_fm[:, COLUMNS * c : COLUMNS * (c + 1)])
+            out[0, :, own_second * c : own_second * (c + 1), :] = part.reshape(
+                narrow, own_second, COLUMNS
+            )
         rows = pl.ds(pl.multiple_of(w * first_rows, first_rows), first_rows)
-        first[0] = mm(flat_t[rows], d_pre[...])
+        for c in range(first_cuts):
+            part = mm(flat_t[rows], d_pre[:, COLUMNS * c : COLUMNS * (c + 1)])
+            at = own_second * second_cuts + own_first * c
+            out[0, :, at : at + own_first, :] = part.reshape(narrow, own_first, COLUMNS)
 
 
 def whole(shape):
@@ -212,13 +224,13 @@
     return pl.BlockSpec(shape, lambda j, c: zeros, pipeline_mode=pl.Buffered(1))
 
 
-def mlp(core, x, up, proj, w_first, w_second, comp, gain, wide):
+def mlp(core, x, up, proj, w_first, w_second, comp, gain, wide, narrow):
     samples = x.shape[2]
     pairs, hidden_size = w_first.shape
     outs = w_second.shape[1]
-    half, second_rows, first_rows = wide // 2, hidden_size // wide, pairs // wide
-    second = jax.ShapeDtypeStruct((half, second_rows, outs), jnp.float32)
-    first = jax.ShapeDtypeStruct((half, first_rows, hidden_size), jnp.float32)
+    half = wide // 2
+    chunk = (w_first.size + w_second.size) // (wide * narrow * COLUMNS)
+    sums = jax.ShapeDtypeStruct((half, narrow, chunk, COLUMNS), jnp.float32)
     rest = [
         jax.ShapeDtypeStruct((TABLES, samples, D), jnp.bfloat16),
         jax.ShapeDtypeStruct((RANK, samples, D), jnp.bfloat16),
@@ -228,16 +240,16 @@
     ]
 
     def by_step(shape):
-        return pl.BlockSpec((1,) + shape.shape[1:], lambda j, c: (j, 0, 0))
+        return pl.BlockSpec((1,) + shape.shape[1:], lambda j, c: (j, 0, 0, 0))
 
     bf16, f32 = jnp.bfloat16, jnp.float32
     return pl.pallas_call(
-        mlp_kernel,
+        functools.partial(mlp_kernel, wide),
         grid_spec=pltpu.PrefetchScalarGridSpec(
             num_scalar_prefetch=1,
             grid=(half,),
             in_specs=[whole(a.shape) for a in (x, up, proj, w_first, w_second, comp, gain)],
-            out_specs=[by_step(second)] * 2 + [by_step(first)] * 2 + [whole(r.shape) for r in rest],
+            out_specs=[by_step(sums)] * 2 + [whole(r.shape) for r in rest],
             scratch_shapes=[
                 pltpu.VMEM((samples, pairs), bf16),
                 pltpu.VMEM((pairs, samples), bf16),
@@ -249,7 +261,7 @@
                 pltpu.VMEM((samples, hidden_size), bf16),
             ],
         ),
-        out_shape=[second, second, first, first] + rest,
+        out_shape=[sums, sums] + rest,
         compiler_params=pltpu.CompilerParams(vmem_limit_bytes=VMEM),
         cost_estimate=pl.CostEstimate(
             flops=16_000_000_000, bytes_accessed=32_000_000, transcendentals=600_000
@@ -258,7 +270,7 @@
 
 
 def rows_kernel(
-    narrow, here, xs, inner, d_pair, d_lc, proj, comp, hot_ids, *refs
+    narrow, here, xs, inner, d_pair, d_lc, proj, comp, hot_ids, cold_ids, *refs
 ):
     colds, (hot, sums, d_rows, totals) = refs[:narrow], refs[narrow:]
     samples = xs.shape[1]
@@ -288,12 +300,18 @@
         totals[...] += mm(jnp.concatenate([d_inner, d_lc_g], axis=0), xg, NT)
         return carry
 
-    lax.fori_loop(0, samples // GROUP, group, 0)
+    lax.fori_loop(0, samples // GROUP, group, 0, unroll=2)
     unit = eye(D)
     for step in range(narrow):
         target = lax.rem(here[0] + step, narrow)
         for i in range(share):
-            colds[step][i] = mm(unit, d_rows[HOT_TABLES + target * share + i], NT)
+            colds[step][D * i : D * (i + 1)] = mm(
+                unit, d_rows[HOT_TABLES + target * share + i], NT
+            )
+        for i in range(ID_ROWS):
+            colds[step][D * share + i : D * share + i + 1] = cold_ids[
+                pl.ds(target * share + min(i, share - 1), 1)
+            ]
     for t in range(HOT_TABLES):
         values = mm(unit, d_rows[t], NT).astype(jnp.bfloat16)
         onehot = ones_where(iota((HOT_ROWS, samples), 0) == hot_ids[t : t + 1, :])
@@ -311,15 +329,15 @@
     )
 
 
-def row_gradients(here, xs, inner, d_pair, d_lc, proj, comp, hot_ids, narrow):
+def row_gradients(here, xs, inner, d_pair, d_lc, proj, comp, hot_ids, cold_ids, narrow):
     samples = xs.shape[1]
     share = COLD_TABLES // narrow
     vmem = pl.BlockSpec(memory_space=pltpu.VMEM)
     return pl.pallas_call(
         functools.partial(rows_kernel, narrow),
-        in_specs=[pl.BlockSpec(memory_space=pltpu.SMEM)] + [vmem] * 7,
+        in_specs=[pl.BlockSpec(memory_space=pltpu.SMEM)] + [vmem] * 8,
         out_specs=[vmem] * (narrow + 2),
-        out_shape=[jax.ShapeDtypeStruct((share, D, samples), jnp.float32)] * narrow
+        out_shape=[jax.ShapeDtypeStruct((share * D + ID_ROWS, samples), jnp.float32)] * narrow
         + [
             jax.ShapeDtypeStruct((HOT_TABLES, D, HOT_ROWS), jnp.float32),
             jax.ShapeDtypeStruct((RANK + LC_OUT, TABLES), jnp.float32),
@@ -332,7 +350,7 @@
         cost_estimate=pl.CostEstimate(
             flops=8_000_000_000, bytes_accessed=12_000_000, transcendentals=0
         ),
-    )(here, xs, inner, d_pair, d_lc, proj, comp, hot_ids)
+    )(here, xs, inner, d_pair, d_lc, proj, comp, hot_ids, cold_ids)
 
 
 def bits_of(axis):
@@ -347,59 +365,116 @@
     return (lax.axis_index(axis) >> bit) & 1
 
 
-def halve(value, dims, axis, bit):
-    dim = dims.index((axis, bit))
-    me = my_bit(axis, bit)
+def split(value, dims, label):
+    dim = dims.index(label)
+    me = my_bit(*label)
     send = lax.dynamic_index_in_dim(value, 1 - me, dim, keepdims=False)
     keep = lax.dynamic_index_in_dim(value, me, dim, keepdims=False)
-    return keep + flip(send, axis, bit), dims[:dim] + dims[dim + 1 :]
-
-
-def scatter_sum(value, dims, order):
-    for axis, bit in order:
-        value, dims = halve(value, dims, axis, bit)
-    return value
-
-
-def gather_back(value, order):
-    for axis, bit in reversed(order):
-        got = flip(value, axis, bit)
-        me = my_bit(axis, bit)
-        value = jnp.stack(
-            [jnp.where(me == 0, value, got), jnp.where(me == 0, got, value)], axis=0
-        )
-    return value
-
-
-def add_rows_kernel(blocks, rows, parts, *refs):
-    ids, values, out = refs[:parts], refs[parts : 2 * parts], refs[2 * parts]
-    table_ids = jnp.concatenate([r[0] for r in ids], axis=1)
-    table_values = jnp.concatenate([r[0].astype(jnp.bfloat16) for r in values], axis=1)
-    for b in range(blocks):
-        at = lax.broadcasted_iota(jnp.int32, (rows, table_ids.shape[1]), 0) + b * rows
-        onehot = (at == table_ids).astype(jnp.float32).astype(jnp.bfloat16)
-        out[b, 0] = lax.dot_general(
-            table_values, onehot, (((1,), (1,)), ((), ())), preferred_element_type=jnp.float32
-        )
-
-
-def add_rows(values, ids, blocks, rows):
-    tables, depth, samples = values[0].shape
+    return send, keep, dims[:dim] + dims[dim + 1 :]
+
+
+def join(value, label):
+    got = flip(value, *label)
+    me = my_bit(*label)
+    return jnp.stack([jnp.where(me == 0, value, got), jnp.where(me == 0, got, value)], axis=0)
+
+
+def nothing(*refs):
+    pass
+
+
+def gate(values, after=()):
+    values, after = list(values), list(after)
+    return pl.pallas_call(
+        nothing,
+        in_specs=[pl.BlockSpec(memory_space=pl.ANY)] * (len(values) + len(after)),
+        out_specs=[pl.BlockSpec(memory_space=pl.ANY)] * len(values),
+        out_shape=[jax.ShapeDtypeStruct(v.shape, v.dtype) for v in values],
+        input_output_aliases={i: i for i in range(len(values))},
+    )(*values, *after)
+
+
+def start(parts, labels):
+    return [split(value, dims, label) for (value, dims), label in zip(parts, labels)]
+
+
+def finish(cuts, labels):
+    return [(keep + flip(send, *label), dims) for (send, keep, dims), label in zip(cuts, labels)]
+
+
+def ordered(cuts, after=()):
+    sends = gate([cut[0] for cut in cuts], after)
+    return [(send, cut[1], cut[2]) for send, cut in zip(sends, cuts)]
+
+
+def combine_kernel(bits, *refs):
+    sums = [refs[2 * i][...] + refs[2 * i + 1][...] for i in range(4)]
+    for value, out in zip(sums, refs[8:]):
+        out[...] = value
+
+
+def combine(bits, keep, got):
+    blocks, n, rows, columns = keep.shape
+    half = blocks // 2
+    shape = (1, n, rows // 2, columns)
+
+    def spec(piece, other):
+        if piece == 0:
+            return pl.BlockSpec(shape, lambda i, b: (2 * i + (b[0] ^ other), 0, 0, 0))
+        return pl.BlockSpec(shape, lambda i, b: (half * (b[1] ^ other) + i, 0, 1, 0))
+
+    specs = [spec(piece, other) for piece in (0, 1) for other in (1, 0)]
+    out = jax.ShapeDtypeStruct((half, n, rows // 2, columns), keep.dtype)
+    return pl.pallas_call(
+        combine_kernel,
+        grid_spec=pltpu.PrefetchScalarGridSpec(
+            num_scalar_prefetch=1,
+            grid=(half,),
+            in_specs=[s for s in specs for _ in range(2)],
+            out_specs=[pl.BlockSpec(shape, lambda i, b: (i, 0, 0, 0))] * 4,
+        ),
+        out_shape=[out] * 4,
+        compiler_params=pltpu.CompilerParams(vmem_limit_bytes=VMEM),
+        cost_estimate=pl.CostEstimate(
+            flops=keep.size, bytes_accessed=12 * keep.size, transcendentals=0
+        ),
+    )(bits, *[keep, got] * 4)
+
+
+def add_rows_kernel(rows, parts, core, *refs):
+    ids, values, (keep, send) = refs[:parts], refs[parts : 2 * parts], refs[-2:]
+    table = pl.program_id(0)
+    numbers = jnp.concatenate([r[pl.ds(table, 1)] for r in ids], axis=1).astype(jnp.int32)
+    owners, at = lax.div(numbers, rows), lax.rem(numbers, rows)
+    values = jnp.concatenate([r[...].astype(jnp.bfloat16) for r in values], axis=1)
+    onehot = ones_where(iota((rows, numbers.shape[1]), 0) == at)
+    for which, out in ((1 - core[0], send), (core[0], keep)):
+        for b in range(out.shape[0]):
+            out[b, 0] = mm(values * ones_where(owners == 2 * b + which), onehot, NT)
+
+
+def add_rows(core, values, tables, blocks, rows):
+    samples = values[0].shape[1]
     parts = len(values)
+    out = jax.ShapeDtypeStruct((blocks // 2, tables, D, rows), jnp.float32)
     return pl.pallas_call(
-        functools.partial(add_rows_kernel, blocks, rows, parts),
-        grid=(tables,),
-        in_specs=[pl.BlockSpec((1, 1, samples), lambda t: (t, 0, 0))] * parts
-        + [pl.BlockSpec((1, depth, samples), lambda t: (t, 0, 0))] * parts,
-        out_specs=pl.BlockSpec((blocks, 1, depth, rows), lambda t: (0, t, 0, 0)),
-        out_shape=jax.ShapeDtypeStruct((blocks, tables, depth, rows), jnp.float32),
-        compiler_params=pltpu.CompilerParams(vmem_limit_bytes=48 * 1024 * 1024),
+        functools.partial(add_rows_kernel, rows, parts),
+        grid_spec=pltpu.PrefetchScalarGridSpec(
+            num_scalar_prefetch=1,
+            grid=(tables,),
+            in_specs=[
+                pl.BlockSpec((ID_ROWS, samples), lambda t, c: (tables * D // ID_ROWS, 0))
+            ]
+            * parts
+            + [pl.BlockSpec((D, samples), lambda t, c: (t, 0))] * parts,
+            out_specs=[pl.BlockSpec((blocks // 2, 1, D, rows), lambda t, c: (0, t, 0, 0))] * 2,
+        ),
+        out_shape=[out] * 2,
+        compiler_params=pltpu.CompilerParams(vmem_limit_bytes=VMEM),
         cost_estimate=pl.CostEstimate(
-            flops=2 * tables * depth * samples * parts * blocks * rows,
-            bytes_accessed=4 * tables * depth * (samples * parts + blocks * rows),
-            transcendentals=0,
-        ),
-    )(*ids, *values)
+            flops=1, bytes_accessed=1, transcendentals=0
+        ),
+    )(core, *values, *values)
 
 
 def local(
@@ -415,19 +490,18 @@
     cold_owner,
 ):
     wide, narrow = lax.axis_size("wide"), lax.axis_size("narrow")
+    devices = wide * narrow
     wide_bits = [("wide", b) for b in range(bits_of("wide"))]
     narrow_bits = [("narrow", b) for b in range(bits_of("narrow"))]
-    w_dims, n_dims = wide_bits[::-1], narrow_bits[::-1]
-    links = wide_bits[1:]
-    order_a = wide_bits[:1] + links + narrow_bits
-    order_b = wide_bits[:1] + links[::-1] + narrow_bits
+    core_bit, links = wide_bits[0], wide_bits[1:]
+    left_dims = links[::-1] + narrow_bits[::-1]
 
     sample_count = embeddings.shape[0]
     here = lax.axis_index("narrow")
     x = jnp.transpose(embeddings, (1, 2, 0))
     up = jnp.transpose(upstream, (1, 2, 0))
     core = my_bit("wide", 0).reshape(1)
-    second_keep, second_send, first_keep, first_send, xs, inner, d_pair, d_lc, gain_sum = mlp(
+    mlp_keep, mlp_send, xs, inner, d_pair, d_lc, gain_sum = mlp(
         core,
         x,
         up,
@@ -437,6 +511,7 @@
         compress,
         norm_gain.reshape(1, D),
         wide,
+        narrow,
     )
     *cold_values, hot_local, sums = row_gradients(
         here.reshape(1),
@@ -447,84 +522,138 @@
         factor_machine_projection,
         compress,
         hot_index.T,
+        (cold_owner[:, :, 0] * COLD_ROWS_DEV + cold_row).T.astype(jnp.float32),
         narrow,
     )
     grad_gain = gain_sum[:, 0]
     grad_proj, compress_gradient = sums[:RANK].T, sums[RANK:]
 
     share = COLD_TABLES // narrow
-    cold_ids = (cold_owner[:, :, 0] * COLD_ROWS_DEV + cold_row).T.reshape(
-        narrow, share, 1, sample_count
-    )
-    got_ids, got_values = [], []
-    for step in range(narrow):
-        target = (here + step) % narrow
-        ids = lax.dynamic_index_in_dim(cold_ids, target, 0, keepdims=False)
-        values = cold_values[step]
-        if step:
-            ring = [(i, (i + step) % narrow) for i in range(narrow)]
-            ids, values = lax.ppermute(ids, "narrow", ring), lax.ppermute(values, "narrow", ring)
-        got_ids.append(ids)
-        got_values.append(values)
-    cold_dense = add_rows(got_values, got_ids, wide, COLD_ROWS_DEV)
-    half = share // 2
-    cold_dense = cold_dense.reshape([2] * len(w_dims) + [2, half, D, COLD_ROWS_DEV])
-    lead = (slice(None),) * len(w_dims)
-    cold_pieces = []
-    for piece, order in ((0, order_a), (1, order_b)):
-        value = scatter_sum(cold_dense[lead + (piece,)], w_dims, order[: len(w_dims)])
-        cold_pieces.append(value)
-    cold_mine = jnp.concatenate(cold_pieces, axis=0)
-    cold_grad = jnp.zeros((narrow, share, D, COLD_ROWS_DEV), jnp.float32)
-    ring = [(i, (i + 1) % narrow) for i in range(narrow)]
-    value = cold_mine
-    for step in range(narrow):
-        if step:
-            value = lax.ppermute(value, "narrow", ring)
-        cold_grad = lax.dynamic_update_index_in_dim(
-            cold_grad, value, (here - step) % narrow, 0
-        )
-    cold_grad = jnp.transpose(
-        cold_grad.reshape(COLD_TABLES, D, COLD_ROWS_DEV), (0, 2, 1)
-    )
-
-    dims = w_dims + n_dims
-    devices = wide * narrow
-
-    def reduce_matrix(keep, send):
-        got = flip(send, "wide", 0)
-        own, columns = keep.shape[1] // narrow, keep.shape[2]
-        left = dims[: len(w_dims) - 1] + n_dims
-        if own % 16:
-            pieces = [(slice(None), order_a)]
-        else:
-            pieces = [(slice(0, own // 2), order_a), (slice(own // 2, own), order_b)]
-        done = []
-        for rows, order in pieces:
-            lead = (slice(None),) * len(left)
-            size = [2] * len(left) + [own, columns]
-            value = keep.reshape(size)[lead + (rows,)] + got.reshape(size)[lead + (rows,)]
-            done.append(scatter_sum(value, left, order[1:]))
-        return jnp.concatenate(done, axis=0)
-
-    grad_second = reduce_matrix(second_keep, second_send)
-    grad_first = reduce_matrix(first_keep, first_send)
+
+    def go_round(value, step):
+        return lax.ppermute(value, "narrow", [(i, (i + step) % narrow) for i in range(narrow)])
+
+    got_values = [cold_values[0], go_round(cold_values[1], 1)]
 
     hot_rows = hot_local.size // LANES
     small = jnp.concatenate([grad_proj.reshape(-1), compress_gradient.reshape(-1), grad_gain])
     small = jnp.pad(small, (0, -small.size % LANES)).reshape(-1, LANES)
     shared = jnp.concatenate([hot_local.reshape(hot_rows, LANES), small], axis=0)
     shared = jnp.pad(shared, ((0, -shared.shape[0] % (8 * devices)), (0, 0)))
-    order = order_a
-    shared = shared.reshape([2] * len(dims) + [-1, LANES])
-    mine = scatter_sum(shared, order, order)
-    shared = gather_back(mine, order).reshape(-1, LANES)
+    hot_order = [core_bit] + links + narrow_bits
+    shared = shared.reshape([2] * len(hot_order) + [-1, LANES])
+    hot = (shared, hot_order)
+
+    def halve(part, label):
+        (part,) = finish(start([part], [label]), [label])
+        return part
+
+    hot = halve(halve(hot, core_bit), links[0])
+
+    (mlp_got,) = gate([flip(mlp_send, *core_bit)], [cold_values[0]])
+    link_bits = jnp.stack([my_bit(*links[0]), my_bit(*links[-1])])
+
+    def first_cuts(keep, got):
+        a_send, a_keep, b_send, b_keep = combine(link_bits, keep, got)
+        dims = links[::-1]
+        return [
+            (a_send, a_keep, dims[:-1]),
+            (b_send, b_keep, dims[1:]),
+        ]
+
+    def unfold(parts, tail):
+        return [(value.reshape([2] * len(dims) + tail), dims) for value, dims in parts]
+
+    chunk = mlp_keep.shape[2]
+    cuts = first_cuts(mlp_keep, mlp_got)
+    later = list(cold_values[2:])
+    sends = gate([cut[0] for cut in cuts] + later, [hot[0], got_values[1]])
+    cuts = [(send, cut[1], cut[2]) for send, cut in zip(sends, cuts)]
+    got_values += [go_round(value, step + 2) for step, value in enumerate(sends[2:])]
+    mlp_parts = unfold(
+        finish(cuts, [links[0], links[-1]]), [2] * len(narrow_bits) + [chunk // 2, COLUMNS]
+    )
+    mlp_parts = [(value, dims + narrow_bits[::-1]) for value, dims in mlp_parts]
+    for turn in range(1, len(links)):
+        labels = [links[turn], links[-1 - turn]]
+        cuts = start(mlp_parts, labels)
+        if turn == len(links) - 1:
+            (hot_cut,) = start([hot], narrow_bits[:1])
+            sends = gate([cut[0] for cut in cuts] + [hot_cut[0]] + got_values)
+            cuts = [(send, cut[1], cut[2]) for send, cut in zip(sends, cuts)]
+            (hot,) = finish([(sends[2], hot_cut[1], hot_cut[2])], narrow_bits[:1])
+            got_values = sends[3:]
+        mlp_parts = finish(cuts, labels)
+
+    cold_keep, cold_send = add_rows(core, got_values, share, wide, COLD_ROWS_DEV)
+    low, high = narrow_bits
+    ready = start([hot, mlp_parts[0]], [high, low])
+    cold_send, *sends = gate([cold_send] + [cut[0] for cut in ready], [mlp_parts[1][0]])
+    ready = [(send, cut[1], cut[2]) for send, cut in zip(sends, ready)]
+    hot, mlp_first = finish(ready, [high, low])
+    mlp_second = mlp_parts[1]
+    cuts = first_cuts(cold_keep, flip(cold_send, *core_bit))
+    half = D // 2
+    parts = []
+    for turn in range(len(links)):
+        labels = [links[turn], links[-1 - turn]]
+        moving = list(parts)
+        if turn == 0:
+            moving, labels = [mlp_second, mlp_first, hot], labels + [low, high, links[1]]
+        elif turn == len(links) - 1:
+            moving, labels = moving + [mlp_second], labels + [high]
+        first = cuts if turn == 0 else []
+        ready = first + start(moving, labels[len(first) :])
+        if turn == len(links) - 1:
+            *sends, hot_value = gate([cut[0] for cut in ready] + [hot[0]])
+            ready = [(send, cut[1], cut[2]) for send, cut in zip(sends, ready)]
+            hot_value = join(hot_value, high)
+        else:
+            ready = ordered(ready)
+        moved = finish(ready, labels)
+        parts = moved[:2]
+        if turn == 0:
+            parts = unfold(parts, [share, half, COLD_ROWS_DEV])
+            mlp_second, mlp_first, hot = moved[2:]
+            for label in links[2:]:
+                hot = halve(hot, label)
+        elif turn == len(links) - 1:
+            mlp_second = moved[2]
+    mlp_parts = [mlp_first, mlp_second]
+
+    cold_grad = jnp.zeros((narrow, share, D, COLD_ROWS_DEV), jnp.float32)
+    moving = jnp.concatenate([parts[0][0], parts[1][0]], axis=1)
+    joins = [narrow_bits[:1], links[:0:-1]] + [[]] * (narrow - 4) + [links[:1]]
+    for step in range(narrow):
+        cold_grad = lax.dynamic_update_index_in_dim(cold_grad, moving, (here - step) % narrow, 0)
+        if step == narrow - 1:
+            break
+        after = [] if step else [value for value, _ in mlp_parts]
+        moving, hot_value = gate([moving, hot_value], after)
+        moving = go_round(moving, 1)
+        for label in joins[step]:
+            hot_value = join(hot_value, label)
+    (hot_value,) = gate([hot_value], [moving])
+    shared = join(hot_value, core_bit).reshape(-1, LANES)
+    cold_grad = jnp.transpose(
+        cold_grad.reshape(COLD_TABLES, D, COLD_ROWS_DEV), (0, 2, 1)
+    )
     hot_grad = jnp.transpose(shared[:hot_rows].reshape(HOT_TABLES, D, HOT_ROWS), (0, 2, 1))
     small = shared[hot_rows:].reshape(-1)
     n_proj, n_compress = TABLES * RANK, LC_OUT * TABLES
     grad_proj = small[:n_proj].reshape(TABLES, RANK)
     compress_gradient = small[n_proj : n_proj + n_compress].reshape(LC_OUT, TABLES)
     grad_gain = small[n_proj + n_compress : n_proj + n_compress + D]
+
+    done = jnp.concatenate([value for value, _ in mlp_parts], axis=0)
+    own_second, own_first = w_first.shape[1] // devices, TABLES * RANK // devices
+    cut = own_second * FM_OUT * D // COLUMNS
+
+    def side_by_side(blocks, rows):
+        return jnp.transpose(blocks.reshape(-1, rows, COLUMNS), (1, 0, 2)).reshape(rows, -1)
+
+    grad_second = side_by_side(done[:cut], own_second)
+    grad_first = side_by_side(done[cut:], own_first)
     return (grad_first, grad_second, grad_proj, compress_gradient, grad_gain, hot_grad, cold_grad)
 
 

time: 342 us -> 326 us (0.953)
  waiting for transfers between devices: 178 us -> 146 us
  Pallas kernels: 69 us -> 82.7 us
  starting transfers between devices: 50.1 us -> 38 us
  other arithmetic: 19.8 us -> 28 us
  local copies, waits for them, and re-layouts: 23.1 us -> 29.3 us
    ppermute x34 -> x24, waiting for transfers between devices: 145 us -> 126 us  [flip(): lax.ppermute(value, axis, [(i, i ^ 1 << bit) for i in range(lax.axis_size...]
    pallas_call x2 -> x14, Pallas kernels: 44.3 us -> 59.7 us  [the longest x1 35.5 us: mlp(): pl.pallas_call(functools.partial(mlp_kernel, wide), grid_spec=pltpu.Prefe...]
    ppermute x9 -> x6, waiting for transfers between devices: 33.3 us -> 19.6 us  [go_round(): lax.ppermute(value, 'narrow', [(i, (i + step) % narrow) for i in range(na...]
    ppermute x9 -> x6, starting transfers between devices: 16.9 us -> 7.35 us  [go_round(): lax.ppermute(value, 'narrow', [(i, (i + step) % narrow) for i in range(na...]
    unnamed x32 -> x53, local copies, waits for them, and re-layouts: 2.85 us -> 9.36 us
    another operation x10 -> x11, other arithmetic: 2.21 us -> 6.84 us  [the longest x10 6.26 us: join(): jnp.stack([jnp.where(me == 0, value, got), jnp.where(me == 0, got, value)...]
    squeeze x28 -> x12, local copies, waits for them, and re-layouts: 5.76 us -> 9.78 us  [split(): send = lax.dynamic_index_in_dim(value, 1 - me, dim, keepdims=False)]
    slice x1 -> x2, local copies, waits for them, and re-layouts: 3.43 us -> 0.01 us  [local(): grad_first = side_by_side(done[cut:], own_first)]
  transfers between devices with their start and end apart: 43 -> 30, of which waited for: 27 -> 14; matrix products, arithmetic and copies ran while one was open for 10% -> 12% of each run, Pallas kernels for 2% -> 13%
where the time goes in v1:
time: 326 us; the launch traced here: 325 us
  waiting for transfers between devices  146 us (45%)
  Pallas kernels  82.7 us (25%)
  starting transfers between devices  38 us (12%)
  local copies, waits for them, and re-layouts  29.3 us (9%)
  other arithmetic  28 us (9%)
    ppermute x24, waiting for transfers between devices, flip(): lax.ppermute(value, axis, [(i, i ^ 1 << bit) for i in range(lax.axis_size...  126 us
    pallas_call x1, Pallas kernels, mlp(): pl.pallas_call(functools.partial(mlp_kernel, wide), grid_spec=pltpu.Prefe...  35.5 us
    ppermute x24, starting transfers between devices, flip(): lax.ppermute(value, axis, [(i, i ^ 1 << bit) for i in range(lax.axis_size...  30.7 us
    pallas_call x1, Pallas kernels, row_gradients(): pl.pallas_call(functools.partial(rows_kernel, narrow), in_specs=[pl.Block...  23 us
    ppermute x6, waiting for transfers between devices, go_round(): lax.ppermute(value, 'narrow', [(i, (i + step) % narrow) for i in range(na...  19.6 us
    add x17, other arithmetic, finish(): keep + flip(send, *label)  17.1 us
    pallas_call x2, Pallas kernels, combine(): pl.pallas_call(combine_kernel, grid_spec=pltpu.PrefetchScalarGridSpec(num...  15.4 us
    squeeze x12, local copies, waits for them, and re-layouts, split(): send = lax.dynamic_index_in_dim(value, 1 - me, dim, keepdims=False)  9.78 us
  transfers between devices with their start and end apart: 30, of which 14 were waited for; matrix products, arithmetic and copies ran while one was open for 12% of the time, Pallas kernels for 13%

profile of v1, /device:TPU:0, one launch (start us, length us, event | category | flops | bytes accessed | tf_op | source)
XLA Modules:
  0.0 325.1 jit_solution(13988106334508619035)
XLA Ops:
  2.0 35.5 %shard_map.153 = (f32[4,4,256,512]{3,2,1,0:T(8,128)}, f32[4,4,256,512]{3,2,1,0:T(8,128)}, bf16[32,256,192]{2,1,0:T(8,128)(2,1)}, bf16[16,256,192]{2,1,0:T(8,128)...) custom-call(s32[1]{0:T(128)} %bitcast.2.core, bf16[32,192,256]{2,1,0:T(8,128)(2,1)} %bitcast.139, ...), custom_call_target="tpu_custom_call" | custom-call | flops 16000000000 | bytes 32000000 | tf_op jit(solution)/shard_map/pallas_call | solution.py:246
  38.5 23.0 %shard_map.154 = (f32[776,256]{1,0:T(8,128)}, f32[776,256]{1,0:T(8,128)}, f32[776,256]{1,0:T(8,128)}, f32[776,256]{1,0:T(8,128)}, f32[16,192,128]{2,1,0:T(8,128)}, /*index=5*/f32[24,32]{1,0:T(8,128)}) custom-call(s32[1]{0:T(128)} %bitcast.6.here, bf16[32,256,192]{2,1,0:T(8,128)(2,1)} %get-tuple-element.61.xs, bf16[16,256,192]{2,1,0:T(8,128)(2,1)} %get-tuple-element.62.inner, ...), custom_call_target="tpu_custom_call" | custom-call | flops 8000000000 | bytes 12000000 | tf_op jit(solution)/shard_map/pallas_call | solution.py:336
  65.0 3.0 collective-permute-start.3
  72.1 9.8 %collective-permute-done.2 = f32[2,2,2,104,128]{4,3,2,1,0:T(8,128)S(1)} collective-permute-done((f32[2,2,2,104,128]{4,3,2,1,0:T(8,128)S(1)}, f32[2,2,2,104,128]{4,3,2,1,0:T(8,128)S(1)}, u32[]{:S(2)}, u32[]{:S(2)}) %collective-permute-start.2) | collective-permute-done | bytes 426016 | tf_op jit(solution)/shard_map/ppermute | solution.py:361
  82.7 10.5 %shard_map.156 = (f32[2,4,128,512]{3,2,1,0:T(8,128)}, f32[2,4,128,512]{3,2,1,0:T(8,128)}, f32[2,4,128,512]{3,2,1,0:T(8,128)}, f32[2,4,128,512]{3,2,1,0:T(8,128)}) custom-call(s32[2]{0:T(128)} %pad_add_fusion.bits, f32[4,4,256,512]{3,2,1,0:T(8,128)} %get-tuple-element.59.refs_0_.refs_2_.refs_4_.refs_6_, ...), custom_call_target="tpu_custom_call" | custom-call | flops 2097152 | bytes 25165824 | tf_op jit(solution)/shard_map/pallas_call | solution.py:428
  97.4 2.6 collective-permute-start.6
  102.0 39.6 %collective-permute-done.5 = f32[2,4,128,512]{3,2,1,0:T(8,128)S(1)} collective-permute-done((f32[2,4,128,512]{3,2,1,0:T(8,128)}, f32[2,4,128,512]{3,2,1,0:T(8,128)S(1)}, u32[]{:S(2)}, u32[]{:S(2)}) %collective-permute-start.5) | collective-permute-done | bytes 2097184 | tf_op jit(solution)/shard_map/ppermute | solution.py:361
  143.0 3.0 add.155
  155.6 8.8 %shard_map.159 = (f32[4,4,192,256]{3,2,1,0:T(8,128)}, f32[4,4,192,256]{3,2,1,0:T(8,128)}) custom-call(s32[1]{0:T(128)} %bitcast.2.core, f32[776,256]{1,0:T(8,128)} %get-tuple-element.81.refs_0_.refs_4_, f32[776,256]{1,0:T(8,128)} %get-tuple-element.82.refs_1_.refs_5_, f32[776,256]{1,0:T(8,128)} %get-tuple-element.83.refs_2_.refs_6_, ...), custom_call_target="tpu_custom_call" | custom-call | flops 1 | bytes 1 | tf_op jit(solution)/shard_map/pallas_call | solution.py:460
  165.1 10.3 %collective-permute-done.10 = f32[2,2,128,512]{3,2,1,0:T(8,128)} collective-permute-done((f32[2,2,128,512]{3,2,1,0:T(8,128)}, f32[2,2,128,512]{3,2,1,0:T(8,128)}, u32[]{:S(2)}, u32[]{:S(2)}) %collective-permute-start.10) | collective-permute-done | bytes 1048608 | tf_op jit(solution)/shard_map/ppermute | solution.py:361
  177.8 2.4 bitcast_add_fusion.1.refs_3_
  180.2 2.9 collective-permute-start.12
  183.1 3.3 %collective-permute-start.13 = (f32[2,104,128]{2,1,0:T(8,128)}, f32[2,104,128]{2,1,0:T(8,128)S(1)}, u32[]{:S(2)}, u32[]{:S(2)}) collective-permute-start(f32[2,104,128]{2,1,0:T(8,128)} %get-tuple-element.93), channel_id=1, source_target_pairs={{0,2},{1,3},{2,0},{3,1},{4,6},{5,7},{6,4},{7,5},{8,10},{9,11},{10,... | collective-permute-start | bytes 319496 | tf_op jit(solution)/shard_map/ppermute | solution.py:361
  188.3 9.3 %collective-permute-done.13 = f32[2,104,128]{2,1,0:T(8,128)S(1)} collective-permute-done((f32[2,104,128]{2,1,0:T(8,128)}, f32[2,104,128]{2,1,0:T(8,128)S(1)}, u32[]{:S(2)}, u32[]{:S(2)}) %collective-permute-start.13) | collective-permute-done | bytes 106528 | tf_op jit(solution)/shard_map/ppermute | solution.py:361
  202.1 4.9 %shard_map.161 = (f32[2,4,96,256]{3,2,1,0:T(8,128)}, f32[2,4,96,256]{3,2,1,0:T(8,128)}, f32[2,4,96,256]{3,2,1,0:T(8,128)}, f32[2,4,96,256]{3,2,1,0:T(8,128)}) custom-call(s32[2]{0:T(128)} %pad_add_fusion.bits, f32[4,4,192,256]{3,2,1,0:T(8,128)} %get-tuple-element.85.refs_0_.refs_2_.refs_4_.refs_6_, f32[4,4,192,256]{3,2,1,0:T(8,128)} %copy-done, ...), custom_call_target="tpu_custom_call" | custom-call | flops 786432 | bytes 9437184 | tf_op jit(solution)/shard_map/pallas_call | solution.py:428
  207.0 3.9 %collective-permute-start.14 = (f32[2,128,512]{2,1,0:T(8,128)}, f32[2,128,512]{2,1,0:T(8,128)S(1)}, u32[]{:S(2)}, u32[]{:S(2)}) collective-permute-start(f32[2,128,512]{2,1,0:T(8,128)} %get-tuple-element.94), channel_id=1, source_target_pairs={{0,1},{1,0},{2,3},{3,2},{4,5},{5,4},{6,7},{7,6},{8,9},{9,8},{10,11... | collective-permute-start | bytes 1572872 | tf_op jit(solution)/shard_map/ppermute | solution.py:361
  214.7 16.7 %collective-permute-done.17 = f32[104,128]{1,0:T(8,128)S(1)} collective-permute-done((f32[104,128]{1,0:T(8,128)}, f32[104,128]{1,0:T(8,128)S(1)}, u32[]{:S(2)}, u32[]{:S(2)}) %collective-permute-start.17) | collective-permute-done | bytes 53280 | tf_op jit(solution)/shard_map/ppermute | solution.py:361
  241.6 7.1 %collective-permute-done.22 = f32[104,128]{1,0:T(8,128)S(1)} collective-permute-done((f32[104,128]{1,0:T(8,128)}, f32[104,128]{1,0:T(8,128)S(1)}, u32[]{:S(2)}, u32[]{:S(2)}) %collective-permute-start.22) | collective-permute-done | bytes 53280 | tf_op jit(solution)/shard_map/ppermute | solution.py:361
  250.2 3.5 %collective-permute-done.18 = f32[128,512]{1,0:T(8,128)S(1)} collective-permute-done((f32[128,512]{1,0:T(8,128)}, f32[128,512]{1,0:T(8,128)S(1)}, u32[]{:S(2)}, u32[]{:S(2)}) %collective-permute-start.18) | collective-permute-done | bytes 262176 | tf_op jit(solution)/shard_map/ppermute | solution.py:361
  258.6 17.9 %collective-permute-done.24 = f32[2,104,128]{2,1,0:T(8,128)S(1)} collective-permute-done((f32[2,104,128]{2,1,0:T(8,128)}, f32[2,104,128]{2,1,0:T(8,128)S(1)}, u32[]{:S(2)}, u32[]{:S(2)}) %collective-permute-start.24) | collective-permute-done | bytes 106528 | tf_op jit(solution)/shard_map/ppermute | solution.py:361
  280.0 5.0 %collective-permute-done.26 = f32[2,2,104,128]{3,2,1,0:T(8,128)S(1)} collective-permute-done((f32[2,2,104,128]{3,2,1,0:T(8,128)}, f32[2,2,104,128]{3,2,1,0:T(8,128)S(1)}, u32[]{:S(2)}, u32[]{:S(2)}) %collective-permute-start.26) | collective-permute-done | bytes 213024 | tf_op jit(solution)/shard_map/ppermute | solution.py:361
  286.8 10.6 %collective-permute-done.25.refs_0_ = f32[4,192,256]{2,1,0:T(8,128)S(1)} collective-permute-done((f32[4,192,256]{2,1,0:T(8,128)}, f32[4,192,256]{2,1,0:T(8,128)S(1)}, u32[]{:S(2)}, u32[]{:S(2)}) %collective-permute-start.25) | collective-permute-done | bytes 786464 | tf_op jit(solution)/shard_map/ppermute | solution.py:534
  299.9 7.1 %collective-permute-done.27 = f32[2,2,2,104,128]{4,3,2,1,0:T(8,128)S(1)} collective-permute-done((f32[2,2,2,104,128]{4,3,2,1,0:T(8,128)}, f32[2,2,2,104,128]{4,3,2,1,0:T(8,128)S(1)}, u32[]{:S(2)}, u32[]{:S(2)}) %collective-permute-start.27) | collective-permute-done | bytes 426016 | tf_op jit(solution)/shard_map/ppermute | solution.py:361
  309.0 8.7 %collective-permute-done.28.refs_1_ = f32[4,192,256]{2,1,0:T(8,128)S(1)} collective-permute-done((f32[4,192,256]{2,1,0:T(8,128)}, f32[4,192,256]{2,1,0:T(8,128)S(1)}, u32[]{:S(2)}, u32[]{:S(2)}) %collective-permute-start.28) | collective-permute-done | bytes 786464 | tf_op jit(solution)/shard_map/ppermute | solution.py:534
  (171 shorter events, 74.7 us)
Async XLA Ops:
  37.5 45.2 %collective-permute-start = (f32[4,4,256,512]{3,2,1,0:T(8,128)}, f32[4,4,256,512]{3,2,1,0:T(8,128)}, u32[]{:S(2)}, u32[]{:S(2)}) collective-permute-start(f32[4,4,256,512]{3,2,1,0:T(8,128)} %get-tuple-element.60), channel_id=1, source_target_pairs={{0,4},{4,0},{8,12},{12,8},{16,20},{20,16},{24,28},{28,24},{1,5},{5... | collective-permute-start | bytes 25165832 | tf_op jit(solution)/shard_map/ppermute | solution.py:361
  65.0 28.2 %collective-permute-start.3 = (f32[776,256]{1,0:T(8,128)}, f32[776,256]{1,0:T(8,128)S(1)}, u32[]{:S(2)}, u32[]{:S(2)}) collective-permute-start(f32[776,256]{1,0:T(8,128)} %get-tuple-element.74), channel_id=1, source_target_pairs={{0,1},{1,2},{2,3},{3,0},{4,5},{5,6},{6,7},{7,4},{8,9},{9,10},{10,1... | collective-permute-start | bytes 2383880 | tf_op jit(solution)/shard_map/ppermute | solution.py:534
  69.4 12.5 %collective-permute-start.2 = (f32[2,2,2,104,128]{4,3,2,1,0:T(8,128)S(1)}, f32[2,2,2,104,128]{4,3,2,1,0:T(8,128)S(1)}, u32[]{:S(2)}, u32[]{:S(2)}) collective-permute-start(f32[2,2,2,104,128]{4,3,2,1,0:T(8,128)S(1)} %dynamic-slice_bitcast_fusion.5), channel_id=1, source_target_pairs={{0,8},{4,12},{8,0},{12,4},{16,24},{20,28},{24,16},{28,20},{1,9},{5... | collective-permute-start | bytes 1277960 | tf_op jit(solution)/shard_map/ppermute | solution.py:361
  94.1 47.5 %collective-permute-start.5 = (f32[2,4,128,512]{3,2,1,0:T(8,128)}, f32[2,4,128,512]{3,2,1,0:T(8,128)S(1)}, u32[]{:S(2)}, u32[]{:S(2)}) collective-permute-start(f32[2,4,128,512]{3,2,1,0:T(8,128)} %get-tuple-element.77), channel_id=1, source_target_pairs={{0,8},{4,12},{8,0},{12,4},{16,24},{20,28},{24,16},{28,20},{1,9},{5... | collective-permute-start | bytes 6291464 | tf_op jit(solution)/shard_map/ppermute | solution.py:361
  95.9 50.1 %collective-permute-start.4 = (f32[2,4,128,512]{3,2,1,0:T(8,128)}, f32[2,4,128,512]{3,2,1,0:T(8,128)}, u32[]{:S(2)}, u32[]{:S(2)}) collective-permute-start(f32[2,4,128,512]{3,2,1,0:T(8,128)} %get-tuple-element.75), channel_id=1, source_target_pairs={{0,16},{4,20},{8,24},{12,28},{16,0},{20,4},{24,8},{28,12},{1,17},{... | collective-permute-start | bytes 6291464 | tf_op jit(solution)/shard_map/ppermute | solution.py:361
  97.4 52.7 %collective-permute-start.6 = (f32[776,256]{1,0:T(8,128)}, f32[776,256]{1,0:T(8,128)S(1)}, u32[]{:S(2)}, u32[]{:S(2)}) collective-permute-start(f32[776,256]{1,0:T(8,128)} %get-tuple-element.78), channel_id=1, source_target_pairs={{0,2},{1,3},{2,0},{3,1},{4,6},{5,7},{6,4},{7,5},{8,10},{9,11},{10,... | collective-permute-start | bytes 2383880 | tf_op jit(solution)/shard_map/ppermute | solution.py:534
  100.0 50.1 %collective-permute-start.7 = (f32[776,256]{1,0:T(8,128)}, f32[776,256]{1,0:T(8,128)}, u32[]{:S(2)}, u32[]{:S(2)}) collective-permute-start(f32[776,256]{1,0:T(8,128)} %get-tuple-element.79), channel_id=1, source_target_pairs={{0,3},{1,0},{2,1},{3,2},{4,7},{5,4},{6,5},{7,6},{8,11},{9,8},{10,9... | collective-permute-start | bytes 2383880 | tf_op jit(solution)/shard_map/ppermute | solution.py:534
  151.0 24.4 %collective-permute-start.10 = (f32[2,2,128,512]{3,2,1,0:T(8,128)}, f32[2,2,128,512]{3,2,1,0:T(8,128)}, u32[]{:S(2)}, u32[]{:S(2)}) collective-permute-start(f32[2,2,128,512]{3,2,1,0:T(8,128)} %get-tuple-element.88), channel_id=1, source_target_pairs={{0,16},{4,20},{8,24},{12,28},{16,0},{20,4},{24,8},{28,12},{1,17},{... | collective-permute-start | bytes 3145736 | tf_op jit(solution)/shard_map/ppermute | solution.py:361
  152.5 25.3 %collective-permute-start.8 = (f32[2,2,128,512]{3,2,1,0:T(8,128)}, f32[2,2,128,512]{3,2,1,0:T(8,128)}, u32[]{:S(2)}, u32[]{:S(2)}) collective-permute-start(f32[2,2,128,512]{3,2,1,0:T(8,128)} %get-tuple-element.80), channel_id=1, source_target_pairs={{0,8},{4,12},{8,0},{12,4},{16,24},{20,28},{24,16},{28,20},{1,9},{5... | collective-permute-start | bytes 3145736 | tf_op jit(solution)/shard_map/ppermute | solution.py:361
  180.2 20.2 %collective-permute-start.11 = (f32[4,4,192,256]{3,2,1,0:T(8,128)}, f32[4,4,192,256]{3,2,1,0:T(8,128)S(1)}, u32[]{:S(2)}, u32[]{:S(2)}) collective-permute-start(f32[4,4,192,256]{3,2,1,0:T(8,128)} %get-tuple-element.89), channel_id=1, source_target_pairs={{0,4},{4,0},{8,12},{12,8},{16,20},{20,16},{24,28},{28,24},{1,5},{5... | collective-permute-start | bytes 9437192 | tf_op jit(solution)/shard_map/ppermute | solution.py:361
  180.2 18.1 %collective-permute-start.12 = (f32[2,128,512]{2,1,0:T(8,128)}, f32[2,128,512]{2,1,0:T(8,128)}, u32[]{:S(2)}, u32[]{:S(2)}) collective-permute-start(f32[2,128,512]{2,1,0:T(8,128)} %get-tuple-element.92), channel_id=1, source_target_pairs={{0,1},{1,0},{2,3},{3,2},{4,5},{5,4},{6,7},{7,6},{8,9},{9,8},{10,11... | collective-permute-start | bytes 1572872 | tf_op jit(solution)/shard_map/ppermute | solution.py:361
  183.1 14.5 %collective-permute-start.13 = (f32[2,104,128]{2,1,0:T(8,128)}, f32[2,104,128]{2,1,0:T(8,128)S(1)}, u32[]{:S(2)}, u32[]{:S(2)}) collective-permute-start(f32[2,104,128]{2,1,0:T(8,128)} %get-tuple-element.93), channel_id=1, source_target_pairs={{0,2},{1,3},{2,0},{3,1},{4,6},{5,7},{6,4},{7,5},{8,10},{9,11},{10,... | collective-permute-start | bytes 319496 | tf_op jit(solution)/shard_map/ppermute | solution.py:361
  207.0 25.0 %collective-permute-start.14 = (f32[2,128,512]{2,1,0:T(8,128)}, f32[2,128,512]{2,1,0:T(8,128)S(1)}, u32[]{:S(2)}, u32[]{:S(2)}) collective-permute-start(f32[2,128,512]{2,1,0:T(8,128)} %get-tuple-element.94), channel_id=1, source_target_pairs={{0,1},{1,0},{2,3},{3,2},{4,5},{5,4},{6,7},{7,6},{8,9},{9,8},{10,11... | collective-permute-start | bytes 1572872 | tf_op jit(solution)/shard_map/ppermute | solution.py:361
  210.9 21.9 %collective-permute-start.16 = (f32[2,4,96,256]{3,2,1,0:T(8,128)}, f32[2,4,96,256]{3,2,1,0:T(8,128)}, u32[]{:S(2)}, u32[]{:S(2)}) collective-permute-start(f32[2,4,96,256]{3,2,1,0:T(8,128)} %get-tuple-element.98), channel_id=1, source_target_pairs={{0,16},{4,20},{8,24},{12,28},{16,0},{20,4},{24,8},{28,12},{1,17},{... | collective-permute-start | bytes 2359304 | tf_op jit(solution)/shard_map/ppermute | solution.py:361
  211.4 22.6 %collective-permute-start.15 = (f32[2,4,96,256]{3,2,1,0:T(8,128)}, f32[2,4,96,256]{3,2,1,0:T(8,128)}, u32[]{:S(2)}, u32[]{:S(2)}) collective-permute-start(f32[2,4,96,256]{3,2,1,0:T(8,128)} %get-tuple-element.96), channel_id=1, source_target_pairs={{0,8},{4,12},{8,0},{12,4},{16,24},{20,28},{24,16},{28,20},{1,9},{5... | collective-permute-start | bytes 2359304 | tf_op jit(solution)/shard_map/ppermute | solution.py:361
  212.0 19.4 %collective-permute-start.17 = (f32[104,128]{1,0:T(8,128)}, f32[104,128]{1,0:T(8,128)S(1)}, u32[]{:S(2)}, u32[]{:S(2)}) collective-permute-start(f32[104,128]{1,0:T(8,128)} %get-tuple-element.99), channel_id=1, source_target_pairs={{0,16},{4,20},{8,24},{12,28},{16,0},{20,4},{24,8},{28,12},{1,17},{... | collective-permute-start | bytes 159752 | tf_op jit(solution)/shard_map/ppermute | solution.py:361
  213.5 24.5 %collective-permute-start.19 = (f32[128,512]{1,0:T(8,128)}, f32[128,512]{1,0:T(8,128)S(1)}, u32[]{:S(2)}, u32[]{:S(2)}) collective-permute-start(f32[128,512]{1,0:T(8,128)} %get-tuple-element.101), channel_id=1, source_target_pairs={{0,2},{1,3},{2,0},{3,1},{4,6},{5,7},{6,4},{7,5},{8,10},{9,11},{10,... | collective-permute-start | bytes 786440 | tf_op jit(solution)/shard_map/ppermute | solution.py:361
  238.7 15.7 %collective-permute-start.20 = (f32[4,96,256]{2,1,0:T(8,128)}, f32[4,96,256]{2,1,0:T(8,128)S(1)}, u32[]{:S(2)}, u32[]{:S(2)}) collective-permute-start(f32[4,96,256]{2,1,0:T(8,128)} %get-tuple-element.102), channel_id=1, source_target_pairs={{0,16},{4,20},{8,24},{12,28},{16,0},{20,4},{24,8},{28,12},{1,17},{... | collective-permute-start | bytes 1179656 | tf_op jit(solution)/shard_map/ppermute | solution.py:361
  239.2 15.2 %collective-permute-start.21 = (f32[4,96,256]{2,1,0:T(8,128)}, f32[4,96,256]{2,1,0:T(8,128)S(1)}, u32[]{:S(2)}, u32[]{:S(2)}) collective-permute-start(f32[4,96,256]{2,1,0:T(8,128)} %get-tuple-element.103), channel_id=1, source_target_pairs={{0,8},{4,12},{8,0},{12,4},{16,24},{20,28},{24,16},{28,20},{1,9},{5... | collective-permute-start | bytes 1179656 | tf_op jit(solution)/shard_map/ppermute | solution.py:361
  239.8 13.9 %collective-permute-start.18 = (f32[128,512]{1,0:T(8,128)}, f32[128,512]{1,0:T(8,128)S(1)}, u32[]{:S(2)}, u32[]{:S(2)}) collective-permute-start(f32[128,512]{1,0:T(8,128)} %get-tuple-element.100), channel_id=1, source_target_pairs={{0,2},{1,3},{2,0},{3,1},{4,6},{5,7},{6,4},{7,5},{8,10},{9,11},{10,... | collective-permute-start | bytes 786440 | tf_op jit(solution)/shard_map/ppermute | solution.py:361
  255.4 22.0 %collective-permute-start.23 = (f32[4,192,256]{2,1,0:T(8,128)}, f32[4,192,256]{2,1,0:T(8,128)S(1)}, u32[]{:S(2)}, u32[]{:S(2)}) collective-permute-start(f32[4,192,256]{2,1,0:T(8,128)} %get-tuple-element.105), channel_id=1, source_target_pairs={{0,1},{1,2},{2,3},{3,0},{4,5},{5,6},{6,7},{7,4},{8,9},{9,10},{10,1... | collective-permute-start | bytes 2359304 | tf_op jit(solution)/shard_map/ppermute | solution.py:534
  255.5 21.0 %collective-permute-start.24 = (f32[2,104,128]{2,1,0:T(8,128)}, f32[2,104,128]{2,1,0:T(8,128)S(1)}, u32[]{:S(2)}, u32[]{:S(2)}) collective-permute-start(f32[2,104,128]{2,1,0:T(8,128)} %get-tuple-element.106), channel_id=1, source_target_pairs={{0,1},{1,0},{2,3},{3,2},{4,5},{5,4},{6,7},{7,6},{8,9},{9,8},{10,11... | collective-permute-start | bytes 319496 | tf_op jit(solution)/shard_map/ppermute | solution.py:361
  278.6 18.8 %collective-permute-start.25 = (f32[4,192,256]{2,1,0:T(8,128)}, f32[4,192,256]{2,1,0:T(8,128)S(1)}, u32[]{:S(2)}, u32[]{:S(2)}) collective-permute-start(f32[4,192,256]{2,1,0:T(8,128)} %get-tuple-element.107), channel_id=1, source_target_pairs={{0,1},{1,2},{2,3},{3,0},{4,5},{5,6},{6,7},{7,4},{8,9},{9,10},{10,1... | collective-permute-start | bytes 2359304 | tf_op jit(solution)/shard_map/ppermute | solution.py:534
  299.9 17.9 %collective-permute-start.28 = (f32[4,192,256]{2,1,0:T(8,128)}, f32[4,192,256]{2,1,0:T(8,128)S(1)}, u32[]{:S(2)}, u32[]{:S(2)}) collective-permute-start(f32[4,192,256]{2,1,0:T(8,128)} %get-tuple-element.110), channel_id=1, source_target_pairs={{0,1},{1,2},{2,3},{3,0},{4,5},{5,6},{6,7},{7,4},{8,9},{9,10},{10,1... | collective-permute-start | bytes 2359304 | tf_op jit(solution)/shard_map/ppermute | solution.py:534
  (32 other events, 281.5 us)

commit v2 on v1

--- a/solution.py
+++ b/solution.py
@@ -19,6 +19,7 @@
 LANES = 128
 COLUMNS = 512
 ID_ROWS = 8
+DENSE_COST = 12000000000
 
 
 NT = (((1,), (1,)), ((), ()))
@@ -329,26 +330,45 @@
     )
 
 
-def row_gradients(here, xs, inner, d_pair, d_lc, proj, comp, hot_ids, cold_ids, narrow):
-    samples = xs.shape[1]
+def row_gradients(here, xs, inner, d_pair, d_lc, proj, comp, hot_ids, cold_ids, narrow, part, parts):
+    samples = xs.shape[1] // parts
     share = COLD_TABLES // narrow
-    vmem = pl.BlockSpec(memory_space=pltpu.VMEM)
+
+    def middle(count):
+        return pl.BlockSpec((count, samples, D), lambda i: (0, part, 0))
+
+    def last(count):
+        return pl.BlockSpec((count, samples), lambda i: (0, part))
+
+    def full(*shape):
+        zeros = (0,) * len(shape)
+        return pl.BlockSpec(shape, lambda i: zeros)
+
+    shapes = [(share * D + ID_ROWS, samples)] * narrow
+    shapes += [(HOT_TABLES, D, HOT_ROWS), (RANK + LC_OUT, TABLES)]
     return pl.pallas_call(
         functools.partial(rows_kernel, narrow),
-        in_specs=[pl.BlockSpec(memory_space=pltpu.SMEM)] + [vmem] * 8,
-        out_specs=[vmem] * (narrow + 2),
-        out_shape=[jax.ShapeDtypeStruct((share * D + ID_ROWS, samples), jnp.float32)] * narrow
-        + [
-            jax.ShapeDtypeStruct((HOT_TABLES, D, HOT_ROWS), jnp.float32),
-            jax.ShapeDtypeStruct((RANK + LC_OUT, TABLES), jnp.float32),
+        grid=(1,),
+        in_specs=[
+            pl.BlockSpec(memory_space=pltpu.SMEM),
+            middle(TABLES),
+            middle(RANK),
+            pl.BlockSpec((samples, TABLES * RANK), lambda i: (part, 0)),
+            middle(LC_OUT),
+            full(*proj.shape),
+            full(*comp.shape),
+            last(HOT_TABLES),
+            last(COLD_TABLES),
         ],
+        out_specs=[full(*shape) for shape in shapes],
+        out_shape=[jax.ShapeDtypeStruct(shape, jnp.float32) for shape in shapes],
         scratch_shapes=[
             pltpu.VMEM((TABLES, samples, D), jnp.bfloat16),
             pltpu.VMEM(((RANK + LC_OUT) * GROUP, TABLES * GROUP), jnp.float32),
         ],
         compiler_params=pltpu.CompilerParams(vmem_limit_bytes=VMEM),
         cost_estimate=pl.CostEstimate(
-            flops=8_000_000_000, bytes_accessed=12_000_000, transcendentals=0
+            flops=1, bytes_accessed=1, transcendentals=0
         ),
     )(here, xs, inner, d_pair, d_lc, proj, comp, hot_ids, cold_ids)
 
@@ -385,13 +405,15 @@
 
 def gate(values, after=()):
     values, after = list(values), list(after)
-    return pl.pallas_call(
+    return list(
+        pl.pallas_call(
         nothing,
         in_specs=[pl.BlockSpec(memory_space=pl.ANY)] * (len(values) + len(after)),
         out_specs=[pl.BlockSpec(memory_space=pl.ANY)] * len(values),
         out_shape=[jax.ShapeDtypeStruct(v.shape, v.dtype) for v in values],
         input_output_aliases={i: i for i in range(len(values))},
     )(*values, *after)
+    )
 
 
 def start(parts, labels):
@@ -472,7 +494,7 @@
         out_shape=[out] * 2,
         compiler_params=pltpu.CompilerParams(vmem_limit_bytes=VMEM),
         cost_estimate=pl.CostEstimate(
-            flops=1, bytes_accessed=1, transcendentals=0
+            flops=DENSE_COST, bytes_accessed=1, transcendentals=0
         ),
     )(core, *values, *values)
 
@@ -513,45 +535,35 @@
         wide,
         narrow,
     )
-    *cold_values, hot_local, sums = row_gradients(
-        here.reshape(1),
-        xs,
-        inner,
-        d_pair,
-        d_lc,
-        factor_machine_projection,
-        compress,
-        hot_index.T,
-        (cold_owner[:, :, 0] * COLD_ROWS_DEV + cold_row).T.astype(jnp.float32),
-        narrow,
-    )
-    grad_gain = gain_sum[:, 0]
-    grad_proj, compress_gradient = sums[:RANK].T, sums[RANK:]
+    cold_ids = (cold_owner[:, :, 0] * COLD_ROWS_DEV + cold_row).T.astype(jnp.float32)
+
+    def rows_of(part, d_pair):
+        *values, hot_sums, sums = row_gradients(
+            here.reshape(1),
+            xs,
+            inner,
+            d_pair,
+            d_lc,
+            factor_machine_projection,
+            compress,
+            hot_index.T,
+            cold_ids,
+            narrow,
+            part,
+            2,
+        )
+        return values, hot_sums, sums
 
     share = COLD_TABLES // narrow
+    low, high = narrow_bits
+    link_bits = jnp.stack([my_bit(*links[0]), my_bit(*links[-1])])
 
     def go_round(value, step):
         return lax.ppermute(value, "narrow", [(i, (i + step) % narrow) for i in range(narrow)])
-
-    got_values = [cold_values[0], go_round(cold_values[1], 1)]
-
-    hot_rows = hot_local.size // LANES
-    small = jnp.concatenate([grad_proj.reshape(-1), compress_gradient.reshape(-1), grad_gain])
-    small = jnp.pad(small, (0, -small.size % LANES)).reshape(-1, LANES)
-    shared = jnp.concatenate([hot_local.reshape(hot_rows, LANES), small], axis=0)
-    shared = jnp.pad(shared, ((0, -shared.shape[0] % (8 * devices)), (0, 0)))
-    hot_order = [core_bit] + links + narrow_bits
-    shared = shared.reshape([2] * len(hot_order) + [-1, LANES])
-    hot = (shared, hot_order)
 
     def halve(part, label):
         (part,) = finish(start([part], [label]), [label])
         return part
-
-    hot = halve(halve(hot, core_bit), links[0])
-
-    (mlp_got,) = gate([flip(mlp_send, *core_bit)], [cold_values[0]])
-    link_bits = jnp.stack([my_bit(*links[0]), my_bit(*links[-1])])
 
     def first_cuts(keep, got):
         a_send, a_keep, b_send, b_keep = combine(link_bits, keep, got)
@@ -564,12 +576,28 @@
     def unfold(parts, tail):
         return [(value.reshape([2] * len(dims) + tail), dims) for value, dims in parts]
 
+    early, hot_early, sums_early = rows_of(0, d_pair)
+    got_early = [go_round(value, step) for step, value in enumerate(early) if step]
+    (mlp_got,) = gate([flip(mlp_send, *core_bit)], early[:1])
     chunk = mlp_keep.shape[2]
     cuts = first_cuts(mlp_keep, mlp_got)
-    later = list(cold_values[2:])
-    sends = gate([cut[0] for cut in cuts] + later, [hot[0], got_values[1]])
-    cuts = [(send, cut[1], cut[2]) for send, cut in zip(sends, cuts)]
-    got_values += [go_round(value, step + 2) for step, value in enumerate(sends[2:])]
+    (d_pair_late,) = gate([d_pair], [cuts[0][0]])
+    late, hot_late, sums_late = rows_of(1, d_pair_late)
+
+    sums = sums_early + sums_late
+    grad_proj, compress_gradient = sums[:RANK].T, sums[RANK:]
+    hot_local = hot_early + hot_late
+    hot_rows = hot_local.size // LANES
+    small = jnp.concatenate([grad_proj.reshape(-1), compress_gradient.reshape(-1), gain_sum[:, 0]])
+    small = jnp.pad(small, (0, -small.size % LANES)).reshape(-1, LANES)
+    shared = jnp.concatenate([hot_local.reshape(hot_rows, LANES), small], axis=0)
+    shared = jnp.pad(shared, ((0, -shared.shape[0] % (8 * devices)), (0, 0)))
+    hot_order = [core_bit] + links + [low]
+    hot = (shared.reshape([2] * len(hot_order) + [-1, LANES]), hot_order)
+
+    late_sends = gate(late[1:], got_early)
+    got_late = [go_round(value, step + 1) for step, value in enumerate(late_sends)]
+    got_values = early[:1] + got_early + late[:1] + got_late
     mlp_parts = unfold(
         finish(cuts, [links[0], links[-1]]), [2] * len(narrow_bits) + [chunk // 2, COLUMNS]
     )
@@ -578,52 +606,45 @@
         labels = [links[turn], links[-1 - turn]]
         cuts = start(mlp_parts, labels)
         if turn == len(links) - 1:
-            (hot_cut,) = start([hot], narrow_bits[:1])
-            sends = gate([cut[0] for cut in cuts] + [hot_cut[0]] + got_values)
+            (hot_cut,) = start([hot], [core_bit])
+            sends = gate([cut[0] for cut in cuts] + [hot_cut[0]], late_sends)
             cuts = [(send, cut[1], cut[2]) for send, cut in zip(sends, cuts)]
-            (hot,) = finish([(sends[2], hot_cut[1], hot_cut[2])], narrow_bits[:1])
-            got_values = sends[3:]
+            (hot,) = finish([(sends[2], hot_cut[1], hot_cut[2])], [core_bit])
         mlp_parts = finish(cuts, labels)
 
     cold_keep, cold_send = add_rows(core, got_values, share, wide, COLD_ROWS_DEV)
-    low, high = narrow_bits
-    ready = start([hot, mlp_parts[0]], [high, low])
-    cold_send, *sends = gate([cold_send] + [cut[0] for cut in ready], [mlp_parts[1][0]])
+    labels = [low, low, links[0]]
+    ready = start(mlp_parts + [hot], labels)
+    cold_send, *sends = gate([cold_send] + [cut[0] for cut in ready])
     ready = [(send, cut[1], cut[2]) for send, cut in zip(sends, ready)]
-    hot, mlp_first = finish(ready, [high, low])
-    mlp_second = mlp_parts[1]
+    mlp_first, mlp_second, hot = finish(ready, labels)
+    for label in links[1:]:
+        hot = halve(hot, label)
     cuts = first_cuts(cold_keep, flip(cold_send, *core_bit))
     half = D // 2
     parts = []
     for turn in range(len(links)):
         labels = [links[turn], links[-1 - turn]]
-        moving = list(parts)
+        last = turn == len(links) - 1
         if turn == 0:
-            moving, labels = [mlp_second, mlp_first, hot], labels + [low, high, links[1]]
-        elif turn == len(links) - 1:
-            moving, labels = moving + [mlp_second], labels + [high]
-        first = cuts if turn == 0 else []
-        ready = first + start(moving, labels[len(first) :])
-        if turn == len(links) - 1:
+            labels = labels + [high, high, low]
+            *parts, mlp_first, mlp_second, hot = finish(
+                ordered(cuts + start([mlp_first, mlp_second, hot], labels[2:])), labels
+            )
+            parts = unfold(parts, [share, half, COLD_ROWS_DEV])
+        elif last:
+            ready = start(parts, labels)
             *sends, hot_value = gate([cut[0] for cut in ready] + [hot[0]])
             ready = [(send, cut[1], cut[2]) for send, cut in zip(sends, ready)]
-            hot_value = join(hot_value, high)
+            hot_value = hot_value + flip(hot_value, *high)
+            parts = finish(ready, labels)
         else:
-            ready = ordered(ready)
-        moved = finish(ready, labels)
-        parts = moved[:2]
-        if turn == 0:
-            parts = unfold(parts, [share, half, COLD_ROWS_DEV])
-            mlp_second, mlp_first, hot = moved[2:]
-            for label in links[2:]:
-                hot = halve(hot, label)
-        elif turn == len(links) - 1:
-            mlp_second = moved[2]
+            parts = finish(ordered(start(parts, labels)), labels)
     mlp_parts = [mlp_first, mlp_second]
 
     cold_grad = jnp.zeros((narrow, share, D, COLD_ROWS_DEV), jnp.float32)
     moving = jnp.concatenate([parts[0][0], parts[1][0]], axis=1)
-    joins = [narrow_bits[:1], links[:0:-1]] + [[]] * (narrow - 4) + [links[:1]]
+    joins = [[low], links[-1:]] + [[]] * (narrow - 4) + [links[-2::-1]]
     for step in range(narrow):
         cold_grad = lax.dynamic_update_index_in_dim(cold_grad, moving, (here - step) % narrow, 0)
         if step == narrow - 1:

time: 326 us -> 298 us (0.914)
  waiting for transfers between devices: 146 us -> 99.9 us
  starting transfers between devices: 38 us -> 49.6 us
  Pallas kernels: 82.7 us -> 88.3 us
    ppermute x24 -> x23, waiting for transfers between devices: 126 us -> 62.5 us  [flip(): lax.ppermute(value, axis, [(i, i ^ 1 << bit) for i in range(lax.axis_size...]
    ppermute x6 -> x9, waiting for transfers between devices: 19.6 us -> 37.3 us  [go_round(): lax.ppermute(value, 'narrow', [(i, (i + step) % narrow) for i in range(na...]
    ppermute x6 -> x9, starting transfers between devices: 7.35 us -> 18.9 us  [go_round(): lax.ppermute(value, 'narrow', [(i, (i + step) % narrow) for i in range(na...]
    pallas_call x1 -> x2, Pallas kernels: 23 us -> 28.2 us  [row_gradients(): pl.pallas_call(functools.partial(rows_kernel, narrow), grid=(1,), in_spec...]
    add x0 -> x3, other arithmetic: none -> 4.31 us  [the longest x1 2.05 us: local(): hot_local = hot_early + hot_late]
    unnamed x53 -> x73, local copies, waits for them, and re-layouts: 9.36 us -> 10.9 us
    squeeze x12 -> x11, local copies, waits for them, and re-layouts: 9.78 us -> 9.22 us  [split(): send = lax.dynamic_index_in_dim(value, 1 - me, dim, keepdims=False)]
    add x17 -> x16, other arithmetic: 17.1 us -> 16.8 us  [finish(): keep + flip(send, *label)]
  transfers between devices with their start and end apart: 30 -> 32, of which waited for: 14 -> 16; matrix products, arithmetic and copies ran while one was open for 12% -> 13% of each run, Pallas kernels for 13% -> 13%
where the time goes in v2:
time: 298 us; the launch traced here: 297 us
  waiting for transfers between devices  99.9 us (34%)
  Pallas kernels  88.3 us (30%)
  starting transfers between devices  49.6 us (17%)
  other arithmetic  29.1 us (10%)
  local copies, waits for them, and re-layouts  28.9 us (10%)
    ppermute x23, waiting for transfers between devices, flip(): lax.ppermute(value, axis, [(i, i ^ 1 << bit) for i in range(lax.axis_size...  62.5 us
    ppermute x9, waiting for transfers between devices, go_round(): lax.ppermute(value, 'narrow', [(i, (i + step) % narrow) for i in range(na...  37.3 us
    pallas_call x1, Pallas kernels, mlp(): pl.pallas_call(functools.partial(mlp_kernel, wide), grid_spec=pltpu.Prefe...  35.5 us
    ppermute x23, starting transfers between devices, flip(): lax.ppermute(value, axis, [(i, i ^ 1 << bit) for i in range(lax.axis_size...  30.7 us
    pallas_call x2, Pallas kernels, row_gradients(): pl.pallas_call(functools.partial(rows_kernel, narrow), grid=(1,), in_spec...  28.2 us
    ppermute x9, starting transfers between devices, go_round(): lax.ppermute(value, 'narrow', [(i, (i + step) % narrow) for i in range(na...  18.9 us
    add x16, other arithmetic, finish(): keep + flip(send, *label)  16.8 us
    pallas_call x2, Pallas kernels, combine(): pl.pallas_call(combine_kernel, grid_spec=pltpu.PrefetchScalarGridSpec(num...  15.5 us
  transfers between devices with their start and end apart: 32, of which 16 were waited for; matrix products, arithmetic and copies ran while one was open for 13% of the time, Pallas kernels for 13%

profile of v2, /device:TPU:0, one launch (start us, length us, event | category | flops | bytes accessed | tf_op | source)
XLA Modules:
  0.0 296.7 jit_solution(13066802634138666507)
XLA Ops:
  2.0 35.5 %shard_map.153 = (f32[4,4,256,512]{3,2,1,0:T(8,128)}, f32[4,4,256,512]{3,2,1,0:T(8,128)}, bf16[32,256,192]{2,1,0:T(8,128)(2,1)}, bf16[16,256,192]{2,1,0:T(8,128)...) custom-call(s32[1]{0:T(128)} %bitcast.2.core, bf16[32,192,256]{2,1,0:T(8,128)(2,1)} %bitcast.133, ...), custom_call_target="tpu_custom_call" | custom-call | flops 16000000000 | bytes 32000000 | tf_op jit(solution)/shard_map/pallas_call | solution.py:247
  38.6 14.1 %shard_map.154 = (f32[776,128]{1,0:T(8,128)}, f32[776,128]{1,0:T(8,128)}, f32[776,128]{1,0:T(8,128)}, f32[776,128]{1,0:T(8,128)}, f32[16,192,128]{2,1,0:T(8,128)}, /*index=5*/f32[24,32]{1,0:T(8,128)}) custom-call(s32[1]{0:T(128)} %bitcast.6.here, bf16[32,256,192]{2,1,0:T(8,128)(2,1)} %get-tuple-element.62.xs, bf16[16,256,192]{2,1,0:T(8,128)(2,1)} %get-tuple-element.63.inner, ...), custom_call_target="tpu_custom_call" | custom-call | flops 1 | bytes 1 | tf_op jit(solution)/shard_map/pallas_call | solution.py:349
  53.2 10.7 %shard_map.156 = (f32[2,4,128,512]{3,2,1,0:T(8,128)}, f32[2,4,128,512]{3,2,1,0:T(8,128)}, f32[2,4,128,512]{3,2,1,0:T(8,128)}, f32[2,4,128,512]{3,2,1,0:T(8,128)}) custom-call(s32[2]{0:T(128)} %pad_add_fusion.bits, f32[4,4,256,512]{3,2,1,0:T(8,128)} %get-tuple-element.60.refs_0_.refs_2_.refs_4_.refs_6_, ...), custom_call_target="tpu_custom_call" | custom-call | flops 2097152 | bytes 25165824 | tf_op jit(solution)/shard_map/pallas_call | solution.py:450
  63.9 2.6 collective-permute-start.2
  69.6 2.6 collective-permute-start.4
  73.6 14.1 %shard_map.158 = (f32[776,128]{1,0:T(8,128)}, f32[776,128]{1,0:T(8,128)}, f32[776,128]{1,0:T(8,128)}, f32[776,128]{1,0:T(8,128)}, f32[16,192,128]{2,1,0:T(8,128)}, /*index=5*/f32[24,32]{1,0:T(8,128)}) custom-call(s32[1]{0:T(128)} %bitcast.6.here, bf16[32,256,192]{2,1,0:T(8,128)(2,1)} %get-tuple-element.62.xs, bf16[16,256,192]{2,1,0:T(8,128)(2,1)} %get-tuple-element.63.inner, ...), custom_call_target="tpu_custom_call" | custom-call | flops 1 | bytes 1 | tf_op jit(solution)/shard_map/pallas_call | solution.py:349
  88.7 9.5 %collective-permute-done.4.refs_4_.refs_2_.refs_10_ = f32[776,128]{1,0:T(8,128)S(1)} collective-permute-done((f32[776,128]{1,0:T(8,128)}, f32[776,128]{1,0:T(8,128)S(1)}, u32[]{:S(2)}, u32[]{:S(2)}) %collective-permute-start.4) | collective-permute-done | bytes 397344 | tf_op jit(solution)/shard_map/ppermute | solution.py:562
  99.2 8.9 %collective-permute-start.7 = (f32[776,128]{1,0:T(8,128)}, f32[776,128]{1,0:T(8,128)S(1)}, u32[]{:S(2)}, u32[]{:S(2)}) collective-permute-start(f32[776,128]{1,0:T(8,128)} %get-tuple-element.82.refs_3_), channel_id=1, source_target_pairs={{0,1},{1,2},{2,3},{3,0},{4,5},{5,6},{6,7},{7,4},{8,9},{9,10},{10,1... | collective-permute-start | bytes 1191944 | tf_op jit(solution)/shard_map/ppermute | solution.py:562
  123.9 11.2 %collective-permute-done.8.refs_6_.refs_14_ = f32[776,128]{1,0:T(8,128)} collective-permute-done((f32[776,128]{1,0:T(8,128)}, f32[776,128]{1,0:T(8,128)}, u32[]{:S(2)}, u32[]{:S(2)}) %collective-permute-start.8) | collective-permute-done | bytes 397344 | tf_op jit(solution)/shard_map/ppermute | solution.py:562
  135.1 9.1 %shard_map.161 = (f32[4,4,192,256]{3,2,1,0:T(8,128)}, f32[4,4,192,256]{3,2,1,0:T(8,128)}) custom-call(s32[1]{0:T(128)} %bitcast.2.core, f32[776,128]{1,0:T(8,128)} %get-tuple-element.66.refs_1_.refs_0_.refs_8_, f32[776,128]{1,0:T(8,128)} %copy-done.27, f32[776,128]{1,0:T(8,128)} %copy-done.28, f32[776,128]{1,0:T(8,128)} %copy-done.29, ...), custom_call_target="tpu_custom_call" | custom-call | flops 12000000000 | bytes 1 | tf_op jit(solution)/shard_map/pallas_call | solution.py:482
  151.9 8.2 %collective-permute-start.12 = (f32[2,128,512]{2,1,0:T(8,128)}, f32[2,128,512]{2,1,0:T(8,128)}, u32[]{:S(2)}, u32[]{:S(2)}) collective-permute-start(f32[2,128,512]{2,1,0:T(8,128)} %get-tuple-element.90), channel_id=1, source_target_pairs={{0,1},{1,0},{2,3},{3,2},{4,5},{5,4},{6,7},{7,6},{8,9},{9,8},{10,11... | collective-permute-start | bytes 1572872 | tf_op jit(solution)/shard_map/ppermute | solution.py:381
  160.2 3.6 %collective-permute-done.15 = f32[2,2,208,128]{3,2,1,0:T(8,128)} collective-permute-done((f32[2,2,208,128]{3,2,1,0:T(8,128)}, f32[2,2,208,128]{3,2,1,0:T(8,128)}, u32[]{:S(2)}, u32[]{:S(2)}) %collective-permute-start.15) | collective-permute-done | bytes 426016 | tf_op jit(solution)/shard_map/ppermute | solution.py:381
  165.9 7.2 %collective-permute-done.12 = f32[2,128,512]{2,1,0:T(8,128)} collective-permute-done((f32[2,128,512]{2,1,0:T(8,128)}, f32[2,128,512]{2,1,0:T(8,128)}, u32[]{:S(2)}, u32[]{:S(2)}) %collective-permute-start.12) | collective-permute-done | bytes 524320 | tf_op jit(solution)/shard_map/ppermute | solution.py:381
  174.4 9.4 %collective-permute-done.14 = f32[2,128,512]{2,1,0:T(8,128)S(1)} collective-permute-done((f32[2,128,512]{2,1,0:T(8,128)}, f32[2,128,512]{2,1,0:T(8,128)S(1)}, u32[]{:S(2)}, u32[]{:S(2)}) %collective-permute-start.14) | collective-permute-done | bytes 524320 | tf_op jit(solution)/shard_map/ppermute | solution.py:381
  187.9 4.9 %shard_map.163 = (f32[2,4,96,256]{3,2,1,0:T(8,128)}, f32[2,4,96,256]{3,2,1,0:T(8,128)}, f32[2,4,96,256]{3,2,1,0:T(8,128)}, f32[2,4,96,256]{3,2,1,0:T(8,128)}) custom-call(s32[2]{0:T(128)} %pad_add_fusion.bits, f32[4,4,192,256]{3,2,1,0:T(8,128)} %get-tuple-element.91.refs_0_.refs_2_.refs_4_.refs_6_, f32[4,4,192,256]{3,2,1,0:T(8,128)} %copy-done, ...), custom_call_target="tpu_custom_call" | custom-call | flops 786432 | bytes 9437184 | tf_op jit(solution)/shard_map/pallas_call | solution.py:450
  196.5 2.2 collective-permute-start.18
  201.3 10.8 %collective-permute-done.20 = f32[2,4,96,256]{3,2,1,0:T(8,128)S(1)} collective-permute-done((f32[2,4,96,256]{3,2,1,0:T(8,128)}, f32[2,4,96,256]{3,2,1,0:T(8,128)S(1)}, u32[]{:S(2)}, u32[]{:S(2)}) %collective-permute-start.20) | collective-permute-done | bytes 786464 | tf_op jit(solution)/shard_map/ppermute | solution.py:381
  220.3 2.2 collective-permute-start.24
  228.8 3.3 %collective-permute-done.23 = f32[4,96,256]{2,1,0:T(8,128)S(1)} collective-permute-done((f32[4,96,256]{2,1,0:T(8,128)}, f32[4,96,256]{2,1,0:T(8,128)S(1)}, u32[]{:S(2)}, u32[]{:S(2)}) %collective-permute-start.23) | collective-permute-done | bytes 393248 | tf_op jit(solution)/shard_map/ppermute | solution.py:381
  237.3 13.6 %collective-permute-done.26 = f32[208,128]{1,0:T(8,128)S(1)} collective-permute-done((f32[208,128]{1,0:T(8,128)}, f32[208,128]{1,0:T(8,128)S(1)}, u32[]{:S(2)}, u32[]{:S(2)}) %collective-permute-start.26) | collective-permute-done | bytes 106528 | tf_op jit(solution)/shard_map/ppermute | solution.py:381
  256.6 4.5 %collective-permute-done.28 = f32[2,208,128]{2,1,0:T(8,128)S(1)} collective-permute-done((f32[2,208,128]{2,1,0:T(8,128)}, f32[2,208,128]{2,1,0:T(8,128)S(1)}, u32[]{:S(2)}, u32[]{:S(2)}) %collective-permute-start.28) | collective-permute-done | bytes 213024 | tf_op jit(solution)/shard_map/ppermute | solution.py:381
  262.9 8.3 %collective-permute-done.27.refs_0_ = f32[4,192,256]{2,1,0:T(8,128)S(1)} collective-permute-done((f32[4,192,256]{2,1,0:T(8,128)}, f32[4,192,256]{2,1,0:T(8,128)S(1)}, u32[]{:S(2)}, u32[]{:S(2)}) %collective-permute-start.27) | collective-permute-done | bytes 786464 | tf_op jit(solution)/shard_map/ppermute | solution.py:562
  274.0 6.6 %collective-permute-done.29 = f32[2,2,208,128]{3,2,1,0:T(8,128)S(1)} collective-permute-done((f32[2,2,208,128]{3,2,1,0:T(8,128)}, f32[2,2,208,128]{3,2,1,0:T(8,128)S(1)}, u32[]{:S(2)}, u32[]{:S(2)}) %collective-permute-start.29) | collective-permute-done | bytes 426016 | tf_op jit(solution)/shard_map/ppermute | solution.py:381
  282.7 6.8 %collective-permute-done.30.refs_1_ = f32[4,192,256]{2,1,0:T(8,128)S(1)} collective-permute-done((f32[4,192,256]{2,1,0:T(8,128)}, f32[4,192,256]{2,1,0:T(8,128)S(1)}, u32[]{:S(2)}, u32[]{:S(2)}) %collective-permute-start.30) | collective-permute-done | bytes 786464 | tf_op jit(solution)/shard_map/ppermute | solution.py:562
  (196 shorter events, 85.8 us)
Async XLA Ops:
  37.5 15.7 %collective-permute-start = (f32[4,4,256,512]{3,2,1,0:T(8,128)}, f32[4,4,256,512]{3,2,1,0:T(8,128)}, u32[]{:S(2)}, u32[]{:S(2)}) collective-permute-start(f32[4,4,256,512]{3,2,1,0:T(8,128)} %get-tuple-element.61), channel_id=1, source_target_pairs={{0,4},{4,0},{8,12},{12,8},{16,20},{20,16},{24,28},{28,24},{1,5},{5... | collective-permute-start | bytes 25165832 | tf_op jit(solution)/shard_map/ppermute | solution.py:381
  63.9 49.7 %collective-permute-start.2 = (f32[2,4,128,512]{3,2,1,0:T(8,128)}, f32[2,4,128,512]{3,2,1,0:T(8,128)S(1)}, u32[]{:S(2)}, u32[]{:S(2)}) collective-permute-start(f32[2,4,128,512]{3,2,1,0:T(8,128)} %get-tuple-element.70.refs_1_), channel_id=1, source_target_pairs={{0,8},{4,12},{8,0},{12,4},{16,24},{20,28},{24,16},{28,20},{1,9},{5... | collective-permute-start | bytes 6291464 | tf_op jit(solution)/shard_map/ppermute | solution.py:381
  66.5 51.1 %collective-permute-start.1 = (f32[2,4,128,512]{3,2,1,0:T(8,128)}, f32[2,4,128,512]{3,2,1,0:T(8,128)}, u32[]{:S(2)}, u32[]{:S(2)}) collective-permute-start(f32[2,4,128,512]{3,2,1,0:T(8,128)} %get-tuple-element.68), channel_id=1, source_target_pairs={{0,16},{4,20},{8,24},{12,28},{16,0},{20,4},{24,8},{28,12},{1,17},{... | collective-permute-start | bytes 6291464 | tf_op jit(solution)/shard_map/ppermute | solution.py:381
  68.0 20.7 %collective-permute-start.3 = (f32[776,128]{1,0:T(8,128)}, f32[776,128]{1,0:T(8,128)S(1)}, u32[]{:S(2)}, u32[]{:S(2)}) collective-permute-start(f32[776,128]{1,0:T(8,128)} %get-tuple-element.79), channel_id=1, source_target_pairs={{0,1},{1,2},{2,3},{3,0},{4,5},{5,6},{6,7},{7,4},{8,9},{9,10},{10,1... | collective-permute-start | bytes 1191944 | tf_op jit(solution)/shard_map/ppermute | solution.py:562
  69.6 28.7 %collective-permute-start.4 = (f32[776,128]{1,0:T(8,128)}, f32[776,128]{1,0:T(8,128)S(1)}, u32[]{:S(2)}, u32[]{:S(2)}) collective-permute-start(f32[776,128]{1,0:T(8,128)} %get-tuple-element.80), channel_id=1, source_target_pairs={{0,2},{1,3},{2,0},{3,1},{4,6},{5,7},{6,4},{7,5},{8,10},{9,11},{10,... | collective-permute-start | bytes 1191944 | tf_op jit(solution)/shard_map/ppermute | solution.py:562
  72.2 26.1 %collective-permute-start.5 = (f32[776,128]{1,0:T(8,128)}, f32[776,128]{1,0:T(8,128)S(1)}, u32[]{:S(2)}, u32[]{:S(2)}) collective-permute-start(f32[776,128]{1,0:T(8,128)} %get-tuple-element.81), channel_id=1, source_target_pairs={{0,3},{1,0},{2,1},{3,2},{4,7},{5,4},{6,5},{7,6},{8,11},{9,8},{10,9... | collective-permute-start | bytes 1191944 | tf_op jit(solution)/shard_map/ppermute | solution.py:562
  99.2 23.2 %collective-permute-start.7 = (f32[776,128]{1,0:T(8,128)}, f32[776,128]{1,0:T(8,128)S(1)}, u32[]{:S(2)}, u32[]{:S(2)}) collective-permute-start(f32[776,128]{1,0:T(8,128)} %get-tuple-element.82.refs_3_), channel_id=1, source_target_pairs={{0,1},{1,2},{2,3},{3,0},{4,5},{5,6},{6,7},{7,4},{8,9},{9,10},{10,1... | collective-permute-start | bytes 1191944 | tf_op jit(solution)/shard_map/ppermute | solution.py:562
  108.0 27.1 %collective-permute-start.8 = (f32[776,128]{1,0:T(8,128)}, f32[776,128]{1,0:T(8,128)}, u32[]{:S(2)}, u32[]{:S(2)}) collective-permute-start(f32[776,128]{1,0:T(8,128)} %get-tuple-element.83.refs_4_), channel_id=1, source_target_pairs={{0,2},{1,3},{2,0},{3,1},{4,6},{5,7},{6,4},{7,5},{8,10},{9,11},{10,... | collective-permute-start | bytes 1191944 | tf_op jit(solution)/shard_map/ppermute | solution.py:562
  109.7 25.3 %collective-permute-start.9 = (f32[776,128]{1,0:T(8,128)}, f32[776,128]{1,0:T(8,128)}, u32[]{:S(2)}, u32[]{:S(2)}) collective-permute-start(f32[776,128]{1,0:T(8,128)} %get-tuple-element.84.refs_5_), channel_id=1, source_target_pairs={{0,3},{1,0},{2,1},{3,2},{4,7},{5,4},{6,5},{7,6},{8,11},{9,8},{10,9... | collective-permute-start | bytes 1191944 | tf_op jit(solution)/shard_map/ppermute | solution.py:562
  121.7 22.4 %collective-permute-start.11 = (f32[2,2,2,208,128]{4,3,2,1,0:T(8,128)}, f32[2,2,2,208,128]{4,3,2,1,0:T(8,128)}, u32[]{:S(2)}, u32[]{:S(2)}) collective-permute-start(f32[2,2,2,208,128]{4,3,2,1,0:T(8,128)} %get-tuple-element.89), channel_id=1, source_target_pairs={{0,4},{4,0},{8,12},{12,8},{16,20},{20,16},{24,28},{28,24},{1,5},{5... | collective-permute-start | bytes 2555912 | tf_op jit(solution)/shard_map/ppermute | solution.py:381
  121.7 25.8 %collective-permute-start.6 = (f32[2,2,128,512]{3,2,1,0:T(8,128)}, f32[2,2,128,512]{3,2,1,0:T(8,128)S(1)}, u32[]{:S(2)}, u32[]{:S(2)}) collective-permute-start(f32[2,2,128,512]{3,2,1,0:T(8,128)} %get-tuple-element.85), channel_id=1, source_target_pairs={{0,8},{4,12},{8,0},{12,4},{16,24},{20,28},{24,16},{28,20},{1,9},{5... | collective-permute-start | bytes 3145736 | tf_op jit(solution)/shard_map/ppermute | solution.py:381
  122.3 26.3 %collective-permute-start.10 = (f32[2,2,128,512]{3,2,1,0:T(8,128)}, f32[2,2,128,512]{3,2,1,0:T(8,128)}, u32[]{:S(2)}, u32[]{:S(2)}) collective-permute-start(f32[2,2,128,512]{3,2,1,0:T(8,128)} %get-tuple-element.88), channel_id=1, source_target_pairs={{0,16},{4,20},{8,24},{12,28},{16,0},{20,4},{24,8},{28,12},{1,17},{... | collective-permute-start | bytes 3145736 | tf_op jit(solution)/shard_map/ppermute | solution.py:381
  151.2 35.0 %collective-permute-start.13 = (f32[4,4,192,256]{3,2,1,0:T(8,128)}, f32[4,4,192,256]{3,2,1,0:T(8,128)S(1)}, u32[]{:S(2)}, u32[]{:S(2)}) collective-permute-start(f32[4,4,192,256]{3,2,1,0:T(8,128)} %get-tuple-element.92), channel_id=1, source_target_pairs={{0,4},{4,0},{8,12},{12,8},{16,20},{20,16},{24,28},{28,24},{1,5},{5... | collective-permute-start | bytes 9437192 | tf_op jit(solution)/shard_map/ppermute | solution.py:381
  151.9 21.2 %collective-permute-start.12 = (f32[2,128,512]{2,1,0:T(8,128)}, f32[2,128,512]{2,1,0:T(8,128)}, u32[]{:S(2)}, u32[]{:S(2)}) collective-permute-start(f32[2,128,512]{2,1,0:T(8,128)} %get-tuple-element.90), channel_id=1, source_target_pairs={{0,1},{1,0},{2,3},{3,2},{4,5},{5,4},{6,7},{7,6},{8,9},{9,8},{10,11... | collective-permute-start | bytes 1572872 | tf_op jit(solution)/shard_map/ppermute | solution.py:381
  160.1 23.7 %collective-permute-start.14 = (f32[2,128,512]{2,1,0:T(8,128)}, f32[2,128,512]{2,1,0:T(8,128)S(1)}, u32[]{:S(2)}, u32[]{:S(2)}) collective-permute-start(f32[2,128,512]{2,1,0:T(8,128)} %get-tuple-element.95), channel_id=1, source_target_pairs={{0,1},{1,0},{2,3},{3,2},{4,5},{5,4},{6,7},{7,6},{8,9},{9,8},{10,11... | collective-permute-start | bytes 1572872 | tf_op jit(solution)/shard_map/ppermute | solution.py:381
  165.0 20.5 %collective-permute-start.16 = (f32[2,208,128]{2,1,0:T(8,128)S(1)}, f32[2,208,128]{2,1,0:T(8,128)S(1)}, u32[]{:S(2)}, u32[]{:S(2)}) collective-permute-start(f32[2,208,128]{2,1,0:T(8,128)S(1)} %dynamic-slice_bitcast_fusion.10), channel_id=1, source_target_pairs={{0,16},{4,20},{8,24},{12,28},{16,0},{20,4},{24,8},{28,12},{1,17},{... | collective-permute-start | bytes 638984 | tf_op jit(solution)/shard_map/ppermute | solution.py:381
  192.7 19.4 %collective-permute-start.20 = (f32[2,4,96,256]{3,2,1,0:T(8,128)}, f32[2,4,96,256]{3,2,1,0:T(8,128)S(1)}, u32[]{:S(2)}, u32[]{:S(2)}) collective-permute-start(f32[2,4,96,256]{3,2,1,0:T(8,128)} %get-tuple-element.102), channel_id=1, source_target_pairs={{0,16},{4,20},{8,24},{12,28},{16,0},{20,4},{24,8},{28,12},{1,17},{... | collective-permute-start | bytes 2359304 | tf_op jit(solution)/shard_map/ppermute | solution.py:381
  193.3 21.0 %collective-permute-start.19 = (f32[2,4,96,256]{3,2,1,0:T(8,128)}, f32[2,4,96,256]{3,2,1,0:T(8,128)S(1)}, u32[]{:S(2)}, u32[]{:S(2)}) collective-permute-start(f32[2,4,96,256]{3,2,1,0:T(8,128)} %get-tuple-element.100), channel_id=1, source_target_pairs={{0,8},{4,12},{8,0},{12,4},{16,24},{20,28},{24,16},{28,20},{1,9},{5... | collective-permute-start | bytes 2359304 | tf_op jit(solution)/shard_map/ppermute | solution.py:381
  196.5 22.0 %collective-permute-start.18 = (f32[128,512]{1,0:T(8,128)}, f32[128,512]{1,0:T(8,128)}, u32[]{:S(2)}, u32[]{:S(2)}) collective-permute-start(f32[128,512]{1,0:T(8,128)} %get-tuple-element.98), channel_id=1, source_target_pairs={{0,2},{1,3},{2,0},{3,1},{4,6},{5,7},{6,4},{7,5},{8,10},{9,11},{10,... | collective-permute-start | bytes 786440 | tf_op jit(solution)/shard_map/ppermute | solution.py:381
  198.8 25.2 %collective-permute-start.17 = (f32[128,512]{1,0:T(8,128)}, f32[128,512]{1,0:T(8,128)}, u32[]{:S(2)}, u32[]{:S(2)}) collective-permute-start(f32[128,512]{1,0:T(8,128)} %get-tuple-element.97), channel_id=1, source_target_pairs={{0,2},{1,3},{2,0},{3,1},{4,6},{5,7},{6,4},{7,5},{8,10},{9,11},{10,... | collective-permute-start | bytes 786440 | tf_op jit(solution)/shard_map/ppermute | solution.py:381
  233.1 20.1 %collective-permute-start.25 = (f32[4,192,256]{2,1,0:T(8,128)}, f32[4,192,256]{2,1,0:T(8,128)S(1)}, u32[]{:S(2)}, u32[]{:S(2)}) collective-permute-start(f32[4,192,256]{2,1,0:T(8,128)} %get-tuple-element.107), channel_id=1, source_target_pairs={{0,1},{1,2},{2,3},{3,0},{4,5},{5,6},{6,7},{7,4},{8,9},{9,10},{10,1... | collective-permute-start | bytes 2359304 | tf_op jit(solution)/shard_map/ppermute | solution.py:562
  234.2 16.7 %collective-permute-start.26 = (f32[208,128]{1,0:T(8,128)}, f32[208,128]{1,0:T(8,128)S(1)}, u32[]{:S(2)}, u32[]{:S(2)}) collective-permute-start(f32[208,128]{1,0:T(8,128)} %get-tuple-element.108), channel_id=1, source_target_pairs={{0,1},{1,0},{2,3},{3,2},{4,5},{5,4},{6,7},{7,6},{8,9},{9,8},{10,11... | collective-permute-start | bytes 319496 | tf_op jit(solution)/shard_map/ppermute | solution.py:381
  254.3 16.9 %collective-permute-start.27 = (f32[4,192,256]{2,1,0:T(8,128)}, f32[4,192,256]{2,1,0:T(8,128)S(1)}, u32[]{:S(2)}, u32[]{:S(2)}) collective-permute-start(f32[4,192,256]{2,1,0:T(8,128)} %get-tuple-element.109), channel_id=1, source_target_pairs={{0,1},{1,2},{2,3},{3,0},{4,5},{5,6},{6,7},{7,4},{8,9},{9,10},{10,1... | collective-permute-start | bytes 2359304 | tf_op jit(solution)/shard_map/ppermute | solution.py:562
  273.8 15.7 %collective-permute-start.30 = (f32[4,192,256]{2,1,0:T(8,128)}, f32[4,192,256]{2,1,0:T(8,128)S(1)}, u32[]{:S(2)}, u32[]{:S(2)}) collective-permute-start(f32[4,192,256]{2,1,0:T(8,128)} %get-tuple-element.112), channel_id=1, source_target_pairs={{0,1},{1,2},{2,3},{3,0},{4,5},{5,6},{6,7},{7,4},{8,9},{9,10},{10,1... | collective-permute-start | bytes 2359304 | tf_op jit(solution)/shard_map/ppermute | solution.py:562
  (44 other events, 349.2 us)

commit v3 on v2

--- a/solution.py
+++ b/solution.py
@@ -19,6 +19,7 @@
 LANES = 128
 COLUMNS = 512
 ID_ROWS = 8
+SENDS = 2
 DENSE_COST = 12000000000
 
 
@@ -429,56 +430,69 @@
     return [(send, cut[1], cut[2]) for send, cut in zip(sends, cuts)]
 
 
-def combine_kernel(bits, *refs):
-    sums = [refs[2 * i][...] + refs[2 * i + 1][...] for i in range(4)]
-    for value, out in zip(sums, refs[8:]):
-        out[...] = value
+def combine_kernel(cuts, bits, *refs):
+    ins, outs = refs[: 8 * cuts], refs[8 * cuts :]
+    for i, out in enumerate(outs):
+        rows = out.shape[2] // cuts
+        for u in range(cuts):
+            keep, got = ins[2 * (cuts * i + u)], ins[2 * (cuts * i + u) + 1]
+            out[:, :, rows * u : rows * (u + 1), :] = keep[...] + got[...]
 
 
 def combine(bits, keep, got):
     blocks, n, rows, columns = keep.shape
     half = blocks // 2
-    shape = (1, n, rows // 2, columns)
-
-    def spec(piece, other):
+    cuts = max(1, len(got) // 2)
+    shape = (1, n, rows // (2 * cuts), columns)
+
+    def spec(piece, other, at):
         if piece == 0:
-            return pl.BlockSpec(shape, lambda i, b: (2 * i + (b[0] ^ other), 0, 0, 0))
-        return pl.BlockSpec(shape, lambda i, b: (half * (b[1] ^ other) + i, 0, 1, 0))
-
-    specs = [spec(piece, other) for piece in (0, 1) for other in (1, 0)]
+            return pl.BlockSpec(shape, lambda i, b: (2 * i + (b[0] ^ other), 0, at, 0))
+        return pl.BlockSpec(shape, lambda i, b: (half * (b[1] ^ other) + i, 0, at, 0))
+
+    specs, operands = [], []
+    for piece in (0, 1):
+        for other in (1, 0):
+            for at in range(piece * cuts, (piece + 1) * cuts):
+                specs += [spec(piece, other, at), spec(piece, other, 0 if len(got) > 1 else at)]
+                operands += [keep, got[at] if len(got) > 1 else got[0]]
     out = jax.ShapeDtypeStruct((half, n, rows // 2, columns), keep.dtype)
     return pl.pallas_call(
-        combine_kernel,
+        functools.partial(combine_kernel, cuts),
         grid_spec=pltpu.PrefetchScalarGridSpec(
             num_scalar_prefetch=1,
             grid=(half,),
-            in_specs=[s for s in specs for _ in range(2)],
-            out_specs=[pl.BlockSpec(shape, lambda i, b: (i, 0, 0, 0))] * 4,
+            in_specs=specs,
+            out_specs=[pl.BlockSpec((1, n, rows // 2, columns), lambda i, b: (i, 0, 0, 0))] * 4,
         ),
         out_shape=[out] * 4,
         compiler_params=pltpu.CompilerParams(vmem_limit_bytes=VMEM),
         cost_estimate=pl.CostEstimate(
             flops=keep.size, bytes_accessed=12 * keep.size, transcendentals=0
         ),
-    )(bits, *[keep, got] * 4)
+    )(bits, *operands)
 
 
 def add_rows_kernel(rows, parts, core, *refs):
-    ids, values, (keep, send) = refs[:parts], refs[parts : 2 * parts], refs[-2:]
+    ids, values, keep, sends = refs[:parts], refs[parts : 2 * parts], refs[2 * parts], refs[2 * parts + 1 :]
     table = pl.program_id(0)
     numbers = jnp.concatenate([r[pl.ds(table, 1)] for r in ids], axis=1).astype(jnp.int32)
     owners, at = lax.div(numbers, rows), lax.rem(numbers, rows)
     values = jnp.concatenate([r[...].astype(jnp.bfloat16) for r in values], axis=1)
     onehot = ones_where(iota((rows, numbers.shape[1]), 0) == at)
-    for which, out in ((1 - core[0], send), (core[0], keep)):
-        for b in range(out.shape[0]):
-            out[b, 0] = mm(values * ones_where(owners == 2 * b + which), onehot, NT)
+    for which, outs in ((1 - core[0], sends), (core[0], [keep])):
+        for b in range(keep.shape[0]):
+            sums = mm(values * ones_where(owners == 2 * b + which), onehot, NT)
+            size = D // len(outs)
+            for i, out in enumerate(outs):
+                out[b, 0] = sums[size * i : size * (i + 1)]
 
 
 def add_rows(core, values, tables, blocks, rows):
     samples = values[0].shape[1]
     parts = len(values)
     out = jax.ShapeDtypeStruct((blocks // 2, tables, D, rows), jnp.float32)
+    piece = jax.ShapeDtypeStruct((blocks // 2, tables, D // SENDS, rows), jnp.float32)
     return pl.pallas_call(
         functools.partial(add_rows_kernel, rows, parts),
         grid_spec=pltpu.PrefetchScalarGridSpec(
@@ -489,9 +503,10 @@
             ]
             * parts
             + [pl.BlockSpec((D, samples), lambda t, c: (t, 0))] * parts,
-            out_specs=[pl.BlockSpec((blocks // 2, 1, D, rows), lambda t, c: (0, t, 0, 0))] * 2,
+            out_specs=[pl.BlockSpec((blocks // 2, 1, D, rows), lambda t, c: (0, t, 0, 0))]
+            + [pl.BlockSpec((blocks // 2, 1, D // SENDS, rows), lambda t, c: (0, t, 0, 0))] * SENDS,
         ),
-        out_shape=[out] * 2,
+        out_shape=[out] + [piece] * SENDS,
         compiler_params=pltpu.CompilerParams(vmem_limit_bytes=VMEM),
         cost_estimate=pl.CostEstimate(
             flops=DENSE_COST, bytes_accessed=1, transcendentals=0
@@ -580,7 +595,7 @@
     got_early = [go_round(value, step) for step, value in enumerate(early) if step]
     (mlp_got,) = gate([flip(mlp_send, *core_bit)], early[:1])
     chunk = mlp_keep.shape[2]
-    cuts = first_cuts(mlp_keep, mlp_got)
+    cuts = first_cuts(mlp_keep, [mlp_got])
     (d_pair_late,) = gate([d_pair], [cuts[0][0]])
     late, hot_late, sums_late = rows_of(1, d_pair_late)
 
@@ -612,26 +627,31 @@
             (hot,) = finish([(sends[2], hot_cut[1], hot_cut[2])], [core_bit])
         mlp_parts = finish(cuts, labels)
 
-    cold_keep, cold_send = add_rows(core, got_values, share, wide, COLD_ROWS_DEV)
-    labels = [low, low, links[0]]
-    ready = start(mlp_parts + [hot], labels)
-    cold_send, *sends = gate([cold_send] + [cut[0] for cut in ready])
-    ready = [(send, cut[1], cut[2]) for send, cut in zip(sends, ready)]
-    mlp_first, mlp_second, hot = finish(ready, labels)
+    cold_keep, *cold_sends = add_rows(core, got_values, share, wide, COLD_ROWS_DEV)
+    labels = [low, links[0]]
+    both = start(mlp_parts, [low, low])
+    mlp_dims = both[0][2]
+    mlp_cut = [jnp.concatenate([cut[i] for cut in both], axis=len(mlp_dims)) for i in range(2)]
+    ready = [(*mlp_cut, mlp_dims)] + start([hot], labels[1:])
+    sends = gate(cold_sends + [cut[0] for cut in ready])
+    cold_sends = sends[:SENDS]
+    ready = [(send, cut[1], cut[2]) for send, cut in zip(sends[SENDS:], ready)]
+    mlp_part, hot = finish(ready, labels)
     for label in links[1:]:
         hot = halve(hot, label)
-    cuts = first_cuts(cold_keep, flip(cold_send, *core_bit))
+    cuts = first_cuts(cold_keep, [flip(send, *core_bit) for send in cold_sends])
     half = D // 2
     parts = []
     for turn in range(len(links)):
         labels = [links[turn], links[-1 - turn]]
         last = turn == len(links) - 1
         if turn == 0:
-            labels = labels + [high, high, low]
-            *parts, mlp_first, mlp_second, hot = finish(
-                ordered(cuts + start([mlp_first, mlp_second, hot], labels[2:])), labels
-            )
+            labels = labels + [low]
+            ready = ordered(cuts + start([hot], labels[2:]))
+            *parts, hot = finish(ready, labels)
             parts = unfold(parts, [share, half, COLD_ROWS_DEV])
+            ready = ordered(start([mlp_part], [high]), [cut[0] for cut in ready])
+            (mlp_part,) = finish(ready, [high])
         elif last:
             ready = start(parts, labels)
             *sends, hot_value = gate([cut[0] for cut in ready] + [hot[0]])
@@ -640,7 +660,6 @@
             parts = finish(ready, labels)
         else:
             parts = finish(ordered(start(parts, labels)), labels)
-    mlp_parts = [mlp_first, mlp_second]
 
     cold_grad = jnp.zeros((narrow, share, D, COLD_ROWS_DEV), jnp.float32)
     moving = jnp.concatenate([parts[0][0], parts[1][0]], axis=1)
@@ -649,7 +668,7 @@
         cold_grad = lax.dynamic_update_index_in_dim(cold_grad, moving, (here - step) % narrow, 0)
         if step == narrow - 1:
             break
-        after = [] if step else [value for value, _ in mlp_parts]
+        after = [] if step else [mlp_part[0]]
         moving, hot_value = gate([moving, hot_value], after)
         moving = go_round(moving, 1)
         for label in joins[step]:
@@ -666,7 +685,7 @@
     compress_gradient = small[n_proj : n_proj + n_compress].reshape(LC_OUT, TABLES)
     grad_gain = small[n_proj + n_compress : n_proj + n_compress + D]
 
-    done = jnp.concatenate([value for value, _ in mlp_parts], axis=0)
+    done = mlp_part[0]
     own_second, own_first = w_first.shape[1] // devices, TABLES * RANK // devices
     cut = own_second * FM_OUT * D // COLUMNS
 

time: 298 us -> 293 us (0.983)
  starting transfers between devices: 49.6 us -> 35 us
  waiting for transfers between devices: 99.9 us -> 111 us
    ppermute x23 -> x22, starting transfers between devices: 30.7 us -> 18.5 us  [flip(): lax.ppermute(value, axis, [(i, i ^ 1 << bit) for i in range(lax.axis_size...]
    ppermute x9, waiting for transfers between devices: 37.3 us -> 48.1 us  [go_round(): lax.ppermute(value, 'narrow', [(i, (i + step) % narrow) for i in range(na...]
    squeeze x11 -> x8, local copies, waits for them, and re-layouts: 9.22 us -> 6.5 us  [split(): send = lax.dynamic_index_in_dim(value, 1 - me, dim, keepdims=False)]
    add x16 -> x14, other arithmetic: 16.8 us -> 15.6 us  [finish(): keep + flip(send, *label)]
    unnamed x73 -> x59, local copies, waits for them, and re-layouts: 10.9 us -> 10.1 us
    ppermute x23 -> x22, waiting for transfers between devices: 62.5 us -> 63.2 us  [flip(): lax.ppermute(value, axis, [(i, i ^ 1 << bit) for i in range(lax.axis_size...]
  transfers between devices with their start and end apart: 32 -> 31, of which waited for: 16 -> 15; matrix products, arithmetic and copies ran while one was open for 13% -> 13% of each run, Pallas kernels for 13% -> 14%
where the time goes in v3:
time: 293 us; the launch traced here: 292 us
  waiting for transfers between devices  111 us (38%)
  Pallas kernels  88.4 us (30%)
  starting transfers between devices  35 us (12%)
  other arithmetic  29 us (10%)
  local copies, waits for them, and re-layouts  27.3 us (9%)
    ppermute x22, waiting for transfers between devices, flip(): lax.ppermute(value, axis, [(i, i ^ 1 << bit) for i in range(lax.axis_size...  63.2 us
    ppermute x9, waiting for transfers between devices, go_round(): lax.ppermute(value, 'narrow', [(i, (i + step) % narrow) for i in range(na...  48.1 us
    pallas_call x1, Pallas kernels, mlp(): pl.pallas_call(functools.partial(mlp_kernel, wide), grid_spec=pltpu.Prefe...  35.5 us
    pallas_call x2, Pallas kernels, row_gradients(): pl.pallas_call(functools.partial(rows_kernel, narrow), grid=(1,), in_spec...  28.2 us
    ppermute x22, starting transfers between devices, flip(): lax.ppermute(value, axis, [(i, i ^ 1 << bit) for i in range(lax.axis_size...  18.5 us
    ppermute x9, starting transfers between devices, go_round(): lax.ppermute(value, 'narrow', [(i, (i + step) % narrow) for i in range(na...  16.4 us
    add x14, other arithmetic, finish(): keep + flip(send, *label)  15.6 us
    pallas_call x2, Pallas kernels, combine(): pl.pallas_call(functools.partial(combine_kernel, cuts), grid_spec=pltpu.P...  15.6 us
  transfers between devices with their start and end apart: 31, of which 15 were waited for; matrix products, arithmetic and copies ran while one was open for 13% of the time, Pallas kernels for 14%

profile of v3, /device:TPU:0, one launch (start us, length us, event | category | flops | bytes accessed | tf_op | source)
XLA Modules:
  0.0 291.9 jit_solution(8233485703422752863)
XLA Ops:
  2.0 35.5 %shard_map.153 = (f32[4,4,256,512]{3,2,1,0:T(8,128)}, f32[4,4,256,512]{3,2,1,0:T(8,128)}, bf16[32,256,192]{2,1,0:T(8,128)(2,1)}, bf16[16,256,192]{2,1,0:T(8,128)...) custom-call(s32[1]{0:T(128)} %bitcast.2.core, bf16[32,192,256]{2,1,0:T(8,128)(2,1)} %bitcast.129, ...), custom_call_target="tpu_custom_call" | custom-call | flops 16000000000 | bytes 32000000 | tf_op jit(solution)/shard_map/pallas_call | solution.py:248
  38.6 14.1 %shard_map.154 = (f32[776,128]{1,0:T(8,128)}, f32[776,128]{1,0:T(8,128)}, f32[776,128]{1,0:T(8,128)}, f32[776,128]{1,0:T(8,128)}, f32[16,192,128]{2,1,0:T(8,128)}, /*index=5*/f32[24,32]{1,0:T(8,128)}) custom-call(s32[1]{0:T(128)} %bitcast.6.here, bf16[32,256,192]{2,1,0:T(8,128)(2,1)} %get-tuple-element.61.xs, bf16[16,256,192]{2,1,0:T(8,128)(2,1)} %get-tuple-element.62.inner, ...), custom_call_target="tpu_custom_call" | custom-call | flops 1 | bytes 1 | tf_op jit(solution)/shard_map/pallas_call | solution.py:350
  53.3 10.6 %shard_map.156 = (f32[2,4,128,512]{3,2,1,0:T(8,128)}, f32[2,4,128,512]{3,2,1,0:T(8,128)}, f32[2,4,128,512]{3,2,1,0:T(8,128)}, f32[2,4,128,512]{3,2,1,0:T(8,128)}) custom-call(s32[2]{0:T(128)} %pad_add_fusion.bits, f32[4,4,256,512]{3,2,1,0:T(8,128)} %get-tuple-element.59.refs_0_.refs_2_.refs_4_.refs_6_, ...), custom_call_target="tpu_custom_call" | custom-call | flops 2097152 | bytes 25165824 | tf_op jit(solution)/shard_map/pallas_call | solution.py:460
  63.9 2.6 collective-permute-start.1
  69.6 2.6 collective-permute-start.4
  73.7 14.1 %shard_map.158 = (f32[776,128]{1,0:T(8,128)}, f32[776,128]{1,0:T(8,128)}, f32[776,128]{1,0:T(8,128)}, f32[776,128]{1,0:T(8,128)}, f32[16,192,128]{2,1,0:T(8,128)}, /*index=5*/f32[24,32]{1,0:T(8,128)}) custom-call(s32[1]{0:T(128)} %bitcast.6.here, bf16[32,256,192]{2,1,0:T(8,128)(2,1)} %get-tuple-element.61.xs, bf16[16,256,192]{2,1,0:T(8,128)(2,1)} %get-tuple-element.62.inner, ...), custom_call_target="tpu_custom_call" | custom-call | flops 1 | bytes 1 | tf_op jit(solution)/shard_map/pallas_call | solution.py:350
  88.8 9.5 %collective-permute-done.4.refs_4_.refs_2_.refs_10_ = f32[776,128]{1,0:T(8,128)S(1)} collective-permute-done((f32[776,128]{1,0:T(8,128)}, f32[776,128]{1,0:T(8,128)S(1)}, u32[]{:S(2)}, u32[]{:S(2)}) %collective-permute-start.4) | collective-permute-done | bytes 397344 | tf_op jit(solution)/shard_map/ppermute | solution.py:577
  99.2 10.0 %collective-permute-start.10 = (f32[776,128]{1,0:T(8,128)}, f32[776,128]{1,0:T(8,128)S(1)}, u32[]{:S(2)}, u32[]{:S(2)}) collective-permute-start(f32[776,128]{1,0:T(8,128)} %get-tuple-element.83.refs_5_), channel_id=1, source_target_pairs={{0,3},{1,0},{2,1},{3,2},{4,7},{5,4},{6,5},{7,6},{8,11},{9,8},{10,9... | collective-permute-start | bytes 1191944 | tf_op jit(solution)/shard_map/ppermute | solution.py:577
  114.4 2.2 add.143
  123.7 4.4 %collective-permute-done.8.refs_5_.refs_13_ = f32[776,128]{1,0:T(8,128)S(1)} collective-permute-done((f32[776,128]{1,0:T(8,128)}, f32[776,128]{1,0:T(8,128)S(1)}, u32[]{:S(2)}, u32[]{:S(2)}) %collective-permute-start.8) | collective-permute-done | bytes 397344 | tf_op jit(solution)/shard_map/ppermute | solution.py:577
  128.2 16.3 %collective-permute-done.9.refs_6_.refs_14_ = f32[776,128]{1,0:T(8,128)S(1)} collective-permute-done((f32[776,128]{1,0:T(8,128)}, f32[776,128]{1,0:T(8,128)S(1)}, u32[]{:S(2)}, u32[]{:S(2)}) %collective-permute-start.9) | collective-permute-done | bytes 397344 | tf_op jit(solution)/shard_map/ppermute | solution.py:577
  145.2 9.1 %shard_map.161 = (f32[4,4,192,256]{3,2,1,0:T(8,128)}, f32[4,4,96,256]{3,2,1,0:T(8,128)}, f32[4,4,96,256]{3,2,1,0:T(8,128)}) custom-call(s32[1]{0:T(128)} %bitcast.2.core, f32[776,128]{1,0:T(8,128)} %get-tuple-element.65.refs_1_.refs_0_.refs_8_, f32[776,128]{1,0:T(8,128)} %copy-done.18, f32[776,128]{1,0:T(8,128)} %copy-done.19, f32[776,128]{1,0:T(8,128)} %copy-done.20, ...), custom_call_target="tpu_custom_call" | custom-call | flops 12000000000 | bytes 1 | tf_op jit(solution)/shard_map/pallas_call | solution.py:496
  163.7 2.1 collective-permute-start.12
  165.8 9.3 %collective-permute-done.15 = f32[2,2,208,128]{3,2,1,0:T(8,128)S(1)} collective-permute-done((f32[2,2,208,128]{3,2,1,0:T(8,128)}, f32[2,2,208,128]{3,2,1,0:T(8,128)S(1)}, u32[]{:S(2)}, u32[]{:S(2)}) %collective-permute-start.15) | collective-permute-done | bytes 426016 | tf_op jit(solution)/shard_map/ppermute | solution.py:382
  175.7 5.9 %collective-permute-done.16 = f32[2,208,128]{2,1,0:T(8,128)S(1)} collective-permute-done((f32[2,208,128]{2,1,0:T(8,128)S(1)}, f32[2,208,128]{2,1,0:T(8,128)S(1)}, u32[]{:S(2)}, u32[]{:S(2)}) %collective-permute-start.16) | collective-permute-done | bytes 213024 | tf_op jit(solution)/shard_map/ppermute | solution.py:382
  184.0 5.0 %shard_map.163 = (f32[2,4,96,256]{3,2,1,0:T(8,128)}, f32[2,4,96,256]{3,2,1,0:T(8,128)}, f32[2,4,96,256]{3,2,1,0:T(8,128)}, f32[2,4,96,256]{3,2,1,0:T(8,128)}) custom-call(s32[2]{0:T(128)} %pad_add_fusion.bits, f32[4,4,192,256]{3,2,1,0:T(8,128)} %get-tuple-element.91.refs_0_.refs_2_.refs_4_.refs_6_, f32[4,4,96,256]{3,2,1,0:T(8,128)} %copy-done.4, ...), custom_call_target="tpu_custom_call" | custom-call | flops 786432 | bytes 9437184 | tf_op jit(solution)/shard_map/pallas_call | solution.py:460
  191.7 2.1 collective-permute-start.20
  197.9 9.3 %collective-permute-done.19 = f32[2,4,96,256]{3,2,1,0:T(8,128)} collective-permute-done((f32[2,4,96,256]{3,2,1,0:T(8,128)}, f32[2,4,96,256]{3,2,1,0:T(8,128)}, u32[]{:S(2)}, u32[]{:S(2)}) %collective-permute-start.19) | collective-permute-done | bytes 786464 | tf_op jit(solution)/shard_map/ppermute | solution.py:382
  212.4 9.4 %collective-permute-done.17 = f32[256,512]{1,0:T(8,128)} collective-permute-done((f32[256,512]{1,0:T(8,128)}, f32[256,512]{1,0:T(8,128)}, u32[]{:S(2)}, u32[]{:S(2)}) %collective-permute-start.17) | collective-permute-done | bytes 524320 | tf_op jit(solution)/shard_map/ppermute | solution.py:382
  229.4 15.9 %collective-permute-done.25 = f32[208,128]{1,0:T(8,128)S(1)} collective-permute-done((f32[208,128]{1,0:T(8,128)}, f32[208,128]{1,0:T(8,128)S(1)}, u32[]{:S(2)}, u32[]{:S(2)}) %collective-permute-start.25) | collective-permute-done | bytes 106528 | tf_op jit(solution)/shard_map/ppermute | solution.py:382
  250.1 4.6 %collective-permute-done.27 = f32[2,208,128]{2,1,0:T(8,128)S(1)} collective-permute-done((f32[2,208,128]{2,1,0:T(8,128)}, f32[2,208,128]{2,1,0:T(8,128)S(1)}, u32[]{:S(2)}, u32[]{:S(2)}) %collective-permute-start.27) | collective-permute-done | bytes 213024 | tf_op jit(solution)/shard_map/ppermute | solution.py:382
  256.4 9.4 %collective-permute-done.26.refs_0_ = f32[4,192,256]{2,1,0:T(8,128)S(1)} collective-permute-done((f32[4,192,256]{2,1,0:T(8,128)}, f32[4,192,256]{2,1,0:T(8,128)S(1)}, u32[]{:S(2)}, u32[]{:S(2)}) %collective-permute-start.26) | collective-permute-done | bytes 786464 | tf_op jit(solution)/shard_map/ppermute | solution.py:577
  268.4 6.9 %collective-permute-done.28 = f32[2,2,208,128]{3,2,1,0:T(8,128)S(1)} collective-permute-done((f32[2,2,208,128]{3,2,1,0:T(8,128)}, f32[2,2,208,128]{3,2,1,0:T(8,128)S(1)}, u32[]{:S(2)}, u32[]{:S(2)}) %collective-permute-start.28) | collective-permute-done | bytes 426016 | tf_op jit(solution)/shard_map/ppermute | solution.py:382
  277.3 7.4 %collective-permute-done.29.refs_1_ = f32[4,192,256]{2,1,0:T(8,128)S(1)} collective-permute-done((f32[4,192,256]{2,1,0:T(8,128)}, f32[4,192,256]{2,1,0:T(8,128)S(1)}, u32[]{:S(2)}, u32[]{:S(2)}) %collective-permute-start.29) | collective-permute-done | bytes 786464 | tf_op jit(solution)/shard_map/ppermute | solution.py:577
  (180 shorter events, 72.4 us)
Async XLA Ops:
  37.5 15.8 %collective-permute-start = (f32[4,4,256,512]{3,2,1,0:T(8,128)}, f32[4,4,256,512]{3,2,1,0:T(8,128)}, u32[]{:S(2)}, u32[]{:S(2)}) collective-permute-start(f32[4,4,256,512]{3,2,1,0:T(8,128)} %get-tuple-element.60), channel_id=1, source_target_pairs={{0,4},{4,0},{8,12},{12,8},{16,20},{20,16},{24,28},{28,24},{1,5},{5... | collective-permute-start | bytes 25165832 | tf_op jit(solution)/shard_map/ppermute | solution.py:382
  63.9 49.2 %collective-permute-start.1 = (f32[2,4,128,512]{3,2,1,0:T(8,128)}, f32[2,4,128,512]{3,2,1,0:T(8,128)}, u32[]{:S(2)}, u32[]{:S(2)}) collective-permute-start(f32[2,4,128,512]{3,2,1,0:T(8,128)} %get-tuple-element.67.refs_1_), channel_id=1, source_target_pairs={{0,8},{4,12},{8,0},{12,4},{16,24},{20,28},{24,16},{28,20},{1,9},{5... | collective-permute-start | bytes 6291464 | tf_op jit(solution)/shard_map/ppermute | solution.py:382
  66.5 50.1 %collective-permute-start.2 = (f32[2,4,128,512]{3,2,1,0:T(8,128)}, f32[2,4,128,512]{3,2,1,0:T(8,128)S(1)}, u32[]{:S(2)}, u32[]{:S(2)}) collective-permute-start(f32[2,4,128,512]{3,2,1,0:T(8,128)} %get-tuple-element.69), channel_id=1, source_target_pairs={{0,16},{4,20},{8,24},{12,28},{16,0},{20,4},{24,8},{28,12},{1,17},{... | collective-permute-start | bytes 6291464 | tf_op jit(solution)/shard_map/ppermute | solution.py:382
  68.0 20.7 %collective-permute-start.3 = (f32[776,128]{1,0:T(8,128)}, f32[776,128]{1,0:T(8,128)S(1)}, u32[]{:S(2)}, u32[]{:S(2)}) collective-permute-start(f32[776,128]{1,0:T(8,128)} %get-tuple-element.78), channel_id=1, source_target_pairs={{0,1},{1,2},{2,3},{3,0},{4,5},{5,6},{6,7},{7,4},{8,9},{9,10},{10,1... | collective-permute-start | bytes 1191944 | tf_op jit(solution)/shard_map/ppermute | solution.py:577
  69.6 28.7 %collective-permute-start.4 = (f32[776,128]{1,0:T(8,128)}, f32[776,128]{1,0:T(8,128)S(1)}, u32[]{:S(2)}, u32[]{:S(2)}) collective-permute-start(f32[776,128]{1,0:T(8,128)} %get-tuple-element.79), channel_id=1, source_target_pairs={{0,2},{1,3},{2,0},{3,1},{4,6},{5,7},{6,4},{7,5},{8,10},{9,11},{10,... | collective-permute-start | bytes 1191944 | tf_op jit(solution)/shard_map/ppermute | solution.py:577
  72.2 26.1 %collective-permute-start.5 = (f32[776,128]{1,0:T(8,128)}, f32[776,128]{1,0:T(8,128)S(1)}, u32[]{:S(2)}, u32[]{:S(2)}) collective-permute-start(f32[776,128]{1,0:T(8,128)} %get-tuple-element.80), channel_id=1, source_target_pairs={{0,3},{1,0},{2,1},{3,2},{4,7},{5,4},{6,5},{7,6},{8,11},{9,8},{10,9... | collective-permute-start | bytes 1191944 | tf_op jit(solution)/shard_map/ppermute | solution.py:577
  99.2 23.0 %collective-permute-start.10 = (f32[776,128]{1,0:T(8,128)}, f32[776,128]{1,0:T(8,128)S(1)}, u32[]{:S(2)}, u32[]{:S(2)}) collective-permute-start(f32[776,128]{1,0:T(8,128)} %get-tuple-element.83.refs_5_), channel_id=1, source_target_pairs={{0,3},{1,0},{2,1},{3,2},{4,7},{5,4},{6,5},{7,6},{8,11},{9,8},{10,9... | collective-permute-start | bytes 1191944 | tf_op jit(solution)/shard_map/ppermute | solution.py:577
  109.2 18.9 %collective-permute-start.8 = (f32[776,128]{1,0:T(8,128)}, f32[776,128]{1,0:T(8,128)S(1)}, u32[]{:S(2)}, u32[]{:S(2)}) collective-permute-start(f32[776,128]{1,0:T(8,128)} %get-tuple-element.81.refs_3_), channel_id=1, source_target_pairs={{0,1},{1,2},{2,3},{3,0},{4,5},{5,6},{6,7},{7,4},{8,9},{9,10},{10,1... | collective-permute-start | bytes 1191944 | tf_op jit(solution)/shard_map/ppermute | solution.py:577
  109.2 35.3 %collective-permute-start.9 = (f32[776,128]{1,0:T(8,128)}, f32[776,128]{1,0:T(8,128)S(1)}, u32[]{:S(2)}, u32[]{:S(2)}) collective-permute-start(f32[776,128]{1,0:T(8,128)} %get-tuple-element.82.refs_4_), channel_id=1, source_target_pairs={{0,2},{1,3},{2,0},{3,1},{4,6},{5,7},{6,4},{7,5},{8,10},{9,11},{10,... | collective-permute-start | bytes 1191944 | tf_op jit(solution)/shard_map/ppermute | solution.py:577
  121.7 32.7 %collective-permute-start.11 = (f32[2,2,2,208,128]{4,3,2,1,0:T(8,128)}, f32[2,2,2,208,128]{4,3,2,1,0:T(8,128)}, u32[]{:S(2)}, u32[]{:S(2)}) collective-permute-start(f32[2,2,2,208,128]{4,3,2,1,0:T(8,128)} %get-tuple-element.89), channel_id=1, source_target_pairs={{0,4},{4,0},{8,12},{12,8},{16,20},{20,16},{24,28},{28,24},{1,5},{5... | collective-permute-start | bytes 2555912 | tf_op jit(solution)/shard_map/ppermute | solution.py:382
  121.7 35.1 %collective-permute-start.6 = (f32[2,2,128,512]{3,2,1,0:T(8,128)}, f32[2,2,128,512]{3,2,1,0:T(8,128)}, u32[]{:S(2)}, u32[]{:S(2)}) collective-permute-start(f32[2,2,128,512]{3,2,1,0:T(8,128)} %get-tuple-element.84), channel_id=1, source_target_pairs={{0,16},{4,20},{8,24},{12,28},{16,0},{20,4},{24,8},{28,12},{1,17},{... | collective-permute-start | bytes 3145736 | tf_op jit(solution)/shard_map/ppermute | solution.py:382
  122.2 37.0 %collective-permute-start.7 = (f32[2,2,128,512]{3,2,1,0:T(8,128)}, f32[2,2,128,512]{3,2,1,0:T(8,128)}, u32[]{:S(2)}, u32[]{:S(2)}) collective-permute-start(f32[2,2,128,512]{3,2,1,0:T(8,128)} %get-tuple-element.85), channel_id=1, source_target_pairs={{0,8},{4,12},{8,0},{12,4},{16,24},{20,28},{24,16},{28,20},{1,9},{5... | collective-permute-start | bytes 3145736 | tf_op jit(solution)/shard_map/ppermute | solution.py:382
  162.6 19.7 %collective-permute-start.13 = (f32[4,4,96,256]{3,2,1,0:T(8,128)}, f32[4,4,96,256]{3,2,1,0:T(8,128)S(1)}, u32[]{:S(2)}, u32[]{:S(2)}) collective-permute-start(f32[4,4,96,256]{3,2,1,0:T(8,128)} %get-tuple-element.92), channel_id=1, source_target_pairs={{0,4},{4,0},{8,12},{12,8},{16,20},{20,16},{24,28},{28,24},{1,5},{5... | collective-permute-start | bytes 4718600 | tf_op jit(solution)/shard_map/ppermute | solution.py:382
  162.6 19.7 %collective-permute-start.14 = (f32[4,4,96,256]{3,2,1,0:T(8,128)}, f32[4,4,96,256]{3,2,1,0:T(8,128)S(1)}, u32[]{:S(2)}, u32[]{:S(2)}) collective-permute-start(f32[4,4,96,256]{3,2,1,0:T(8,128)} %get-tuple-element.93), channel_id=1, source_target_pairs={{0,4},{4,0},{8,12},{12,8},{16,20},{20,16},{24,28},{28,24},{1,5},{5... | collective-permute-start | bytes 4718600 | tf_op jit(solution)/shard_map/ppermute | solution.py:382
  163.7 26.5 %collective-permute-start.12 = (f32[2,256,512]{2,1,0:T(8,128)}, f32[2,256,512]{2,1,0:T(8,128)}, u32[]{:S(2)}, u32[]{:S(2)}) collective-permute-start(f32[2,256,512]{2,1,0:T(8,128)} %get-tuple-element.90), channel_id=1, source_target_pairs={{0,1},{1,0},{2,3},{3,2},{4,5},{5,4},{6,7},{7,6},{8,9},{9,8},{10,11... | collective-permute-start | bytes 3145736 | tf_op jit(solution)/shard_map/ppermute | solution.py:382
  189.0 18.3 %collective-permute-start.19 = (f32[2,4,96,256]{3,2,1,0:T(8,128)}, f32[2,4,96,256]{3,2,1,0:T(8,128)}, u32[]{:S(2)}, u32[]{:S(2)}) collective-permute-start(f32[2,4,96,256]{3,2,1,0:T(8,128)} %get-tuple-element.98.refs_2_), channel_id=1, source_target_pairs={{0,16},{4,20},{8,24},{12,28},{16,0},{20,4},{24,8},{28,12},{1,17},{... | collective-permute-start | bytes 2359304 | tf_op jit(solution)/shard_map/ppermute | solution.py:382
  189.6 19.0 %collective-permute-start.18 = (f32[2,4,96,256]{3,2,1,0:T(8,128)}, f32[2,4,96,256]{3,2,1,0:T(8,128)}, u32[]{:S(2)}, u32[]{:S(2)}) collective-permute-start(f32[2,4,96,256]{3,2,1,0:T(8,128)} %get-tuple-element.97.refs_1_), channel_id=1, source_target_pairs={{0,8},{4,12},{8,0},{12,4},{16,24},{20,28},{24,16},{28,20},{1,9},{5... | collective-permute-start | bytes 2359304 | tf_op jit(solution)/shard_map/ppermute | solution.py:382
  194.7 27.1 %collective-permute-start.17 = (f32[256,512]{1,0:T(8,128)}, f32[256,512]{1,0:T(8,128)}, u32[]{:S(2)}, u32[]{:S(2)}) collective-permute-start(f32[256,512]{1,0:T(8,128)} %shard_map.165), channel_id=1, source_target_pairs={{0,2},{1,3},{2,0},{3,1},{4,6},{5,7},{6,4},{7,5},{8,10},{9,11},{10,... | collective-permute-start | bytes 1572872 | tf_op jit(solution)/shard_map/ppermute | solution.py:382
  211.4 14.0 %collective-permute-start.21 = (f32[4,96,256]{2,1,0:T(8,128)}, f32[4,96,256]{2,1,0:T(8,128)S(1)}, u32[]{:S(2)}, u32[]{:S(2)}) collective-permute-start(f32[4,96,256]{2,1,0:T(8,128)} %get-tuple-element.102), channel_id=1, source_target_pairs={{0,16},{4,20},{8,24},{12,28},{16,0},{20,4},{24,8},{28,12},{1,17},{... | collective-permute-start | bytes 1179656 | tf_op jit(solution)/shard_map/ppermute | solution.py:382
  211.8 13.5 %collective-permute-start.22 = (f32[4,96,256]{2,1,0:T(8,128)}, f32[4,96,256]{2,1,0:T(8,128)S(1)}, u32[]{:S(2)}, u32[]{:S(2)}) collective-permute-start(f32[4,96,256]{2,1,0:T(8,128)} %get-tuple-element.103), channel_id=1, source_target_pairs={{0,8},{4,12},{8,0},{12,4},{16,24},{20,28},{24,16},{28,20},{1,9},{5... | collective-permute-start | bytes 1179656 | tf_op jit(solution)/shard_map/ppermute | solution.py:382
  226.4 20.7 %collective-permute-start.24 = (f32[4,192,256]{2,1,0:T(8,128)}, f32[4,192,256]{2,1,0:T(8,128)S(1)}, u32[]{:S(2)}, u32[]{:S(2)}) collective-permute-start(f32[4,192,256]{2,1,0:T(8,128)} %get-tuple-element.105), channel_id=1, source_target_pairs={{0,1},{1,2},{2,3},{3,0},{4,5},{5,6},{6,7},{7,4},{8,9},{9,10},{10,1... | collective-permute-start | bytes 2359304 | tf_op jit(solution)/shard_map/ppermute | solution.py:577
  226.4 19.0 %collective-permute-start.25 = (f32[208,128]{1,0:T(8,128)}, f32[208,128]{1,0:T(8,128)S(1)}, u32[]{:S(2)}, u32[]{:S(2)}) collective-permute-start(f32[208,128]{1,0:T(8,128)} %get-tuple-element.106), channel_id=1, source_target_pairs={{0,1},{1,0},{2,3},{3,2},{4,5},{5,4},{6,7},{7,6},{8,9},{9,8},{10,11... | collective-permute-start | bytes 319496 | tf_op jit(solution)/shard_map/ppermute | solution.py:382
  248.2 17.5 %collective-permute-start.26 = (f32[4,192,256]{2,1,0:T(8,128)}, f32[4,192,256]{2,1,0:T(8,128)S(1)}, u32[]{:S(2)}, u32[]{:S(2)}) collective-permute-start(f32[4,192,256]{2,1,0:T(8,128)} %get-tuple-element.107), channel_id=1, source_target_pairs={{0,1},{1,2},{2,3},{3,0},{4,5},{5,6},{6,7},{7,4},{8,9},{9,10},{10,1... | collective-permute-start | bytes 2359304 | tf_op jit(solution)/shard_map/ppermute | solution.py:577
  268.4 16.3 %collective-permute-start.29 = (f32[4,192,256]{2,1,0:T(8,128)}, f32[4,192,256]{2,1,0:T(8,128)S(1)}, u32[]{:S(2)}, u32[]{:S(2)}) collective-permute-start(f32[4,192,256]{2,1,0:T(8,128)} %get-tuple-element.110), channel_id=1, source_target_pairs={{0,1},{1,2},{2,3},{3,0},{4,5},{5,6},{6,7},{7,4},{8,9},{9,10},{10,1... | collective-permute-start | bytes 2359304 | tf_op jit(solution)/shard_map/ppermute | solution.py:577
  (37 other events, 310.5 us)

commit v4 on v3

--- a/solution.py
+++ b/solution.py
@@ -94,8 +94,8 @@
     x,
     up,
     proj,
-    w_first,
-    w_second,
+    w_first_in,
+    w_second_in,
     comp,
     gain,
     keep,
@@ -113,6 +113,9 @@
     lc_out,
     d_fm,
     d_pre,
+    w_first,
+    w_second,
+    arrived,
 ):
     step = pl.program_id(0)
     samples = x.shape[2]
@@ -121,6 +124,10 @@
 
     @pl.when(step == 0)
     def _():
+        first_copy = pltpu.make_async_copy(w_first_in, w_first, arrived.at[0])
+        second_copy = pltpu.make_async_copy(w_second_in, w_second, arrived.at[1])
+        first_copy.start()
+        second_copy.start()
         unit = eye(samples)
         for n in range(TABLES):
             xs[n] = mm(unit, x[n], NT).astype(jnp.bfloat16)
@@ -149,7 +156,9 @@
                 ).astype(jnp.bfloat16)
             return carry
 
-        lax.fori_loop(0, groups, group, 0, unroll=2)
+        lax.fori_loop(0, groups, group, 0, unroll=4)
+        first_copy.wait()
+        second_copy.wait()
         pairs = flat.shape[1]
         block = 256
         unit_b = eye(block)
@@ -250,7 +259,9 @@
         grid_spec=pltpu.PrefetchScalarGridSpec(
             num_scalar_prefetch=1,
             grid=(half,),
-            in_specs=[whole(a.shape) for a in (x, up, proj, w_first, w_second, comp, gain)],
+            in_specs=[whole(a.shape) for a in (x, up, proj)]
+            + [pl.BlockSpec(memory_space=pl.ANY)] * 2
+            + [whole(a.shape) for a in (comp, gain)],
             out_specs=[by_step(sums)] * 2 + [whole(r.shape) for r in rest],
             scratch_shapes=[
                 pltpu.VMEM((samples, pairs), bf16),
@@ -261,6 +272,9 @@
                 pltpu.VMEM((LC_OUT, D, samples), f32),
                 pltpu.VMEM((samples, outs), bf16),
                 pltpu.VMEM((samples, hidden_size), bf16),
+                pltpu.VMEM(w_first.shape, bf16),
+                pltpu.VMEM(w_second.shape, bf16),
+                pltpu.SemaphoreType.DMA((2,)),
             ],
         ),
         out_shape=[sums, sums] + rest,

time: 293 us -> 290 us (0.990)
  Pallas kernels: 88.4 us -> 85.3 us
    pallas_call x1, Pallas kernels: 35.5 us -> 32.4 us  [mlp(): pl.pallas_call(functools.partial(mlp_kernel, wide), grid_spec=pltpu.Prefe...]
  transfers between devices with their start and end apart: 31 -> 31, of which waited for: 15 -> 15; matrix products, arithmetic and copies ran while one was open for 13% -> 13% of each run, Pallas kernels for 14% -> 15%
where the time goes in v4:
time: 290 us; the launch traced here: 289 us
  waiting for transfers between devices  111 us (38%)
  Pallas kernels  85.3 us (29%)
  starting transfers between devices  35.1 us (12%)
  other arithmetic  29 us (10%)
  local copies, waits for them, and re-layouts  27.3 us (9%)
    ppermute x22, waiting for transfers between devices, flip(): lax.ppermute(value, axis, [(i, i ^ 1 << bit) for i in range(lax.axis_size...  63 us
    ppermute x9, waiting for transfers between devices, go_round(): lax.ppermute(value, 'narrow', [(i, (i + step) % narrow) for i in range(na...  48.1 us
    pallas_call x1, Pallas kernels, mlp(): pl.pallas_call(functools.partial(mlp_kernel, wide), grid_spec=pltpu.Prefe...  32.4 us
    pallas_call x2, Pallas kernels, row_gradients(): pl.pallas_call(functools.partial(rows_kernel, narrow), grid=(1,), in_spec...  28.2 us
    ppermute x22, starting transfers between devices, flip(): lax.ppermute(value, axis, [(i, i ^ 1 << bit) for i in range(lax.axis_size...  18.7 us
    ppermute x9, starting transfers between devices, go_round(): lax.ppermute(value, 'narrow', [(i, (i + step) % narrow) for i in range(na...  16.4 us
    add x14, other arithmetic, finish(): keep + flip(send, *label)  15.6 us
    pallas_call x2, Pallas kernels, combine(): pl.pallas_call(functools.partial(combine_kernel, cuts), grid_spec=pltpu.P...  15.6 us
  transfers between devices with their start and end apart: 31, of which 15 were waited for; matrix products, arithmetic and copies ran while one was open for 13% of the time, Pallas kernels for 15%

profile of v4, /device:TPU:0, one launch (start us, length us, event | category | flops | bytes accessed | tf_op | source)
XLA Modules:
  0.0 288.8 jit_solution(8344247348128412632)
XLA Ops:
  2.0 32.4 %shard_map.153 = (f32[4,4,256,512]{3,2,1,0:T(8,128)}, f32[4,4,256,512]{3,2,1,0:T(8,128)}, bf16[32,256,192]{2,1,0:T(8,128)(2,1)}, bf16[16,256,192]{2,1,0:T(8,128)...) custom-call(s32[1]{0:T(128)} %bitcast.2.core, bf16[32,192,256]{2,1,0:T(8,128)(2,1)} %bitcast.129, ...), custom_call_target="tpu_custom_call" | custom-call | flops 16000000000 | bytes 32000000 | tf_op jit(solution)/shard_map/pallas_call | solution.py:257
  35.5 14.1 %shard_map.154 = (f32[776,128]{1,0:T(8,128)}, f32[776,128]{1,0:T(8,128)}, f32[776,128]{1,0:T(8,128)}, f32[776,128]{1,0:T(8,128)}, f32[16,192,128]{2,1,0:T(8,128)}, /*index=5*/f32[24,32]{1,0:T(8,128)}) custom-call(s32[1]{0:T(128)} %bitcast.6.here, bf16[32,256,192]{2,1,0:T(8,128)(2,1)} %get-tuple-element.61.xs, bf16[16,256,192]{2,1,0:T(8,128)(2,1)} %get-tuple-element.62.inner, ...), custom_call_target="tpu_custom_call" | custom-call | flops 1 | bytes 1 | tf_op jit(solution)/shard_map/pallas_call | solution.py:364
  50.3 10.6 %shard_map.156 = (f32[2,4,128,512]{3,2,1,0:T(8,128)}, f32[2,4,128,512]{3,2,1,0:T(8,128)}, f32[2,4,128,512]{3,2,1,0:T(8,128)}, f32[2,4,128,512]{3,2,1,0:T(8,128)}) custom-call(s32[2]{0:T(128)} %pad_add_fusion.bits, f32[4,4,256,512]{3,2,1,0:T(8,128)} %get-tuple-element.59.refs_0_.refs_2_.refs_4_.refs_6_, ...), custom_call_target="tpu_custom_call" | custom-call | flops 2097152 | bytes 25165824 | tf_op jit(solution)/shard_map/pallas_call | solution.py:474
  60.9 2.6 collective-permute-start.1
  66.6 2.6 collective-permute-start.4
  70.6 14.1 %shard_map.158 = (f32[776,128]{1,0:T(8,128)}, f32[776,128]{1,0:T(8,128)}, f32[776,128]{1,0:T(8,128)}, f32[776,128]{1,0:T(8,128)}, f32[16,192,128]{2,1,0:T(8,128)}, /*index=5*/f32[24,32]{1,0:T(8,128)}) custom-call(s32[1]{0:T(128)} %bitcast.6.here, bf16[32,256,192]{2,1,0:T(8,128)(2,1)} %get-tuple-element.61.xs, bf16[16,256,192]{2,1,0:T(8,128)(2,1)} %get-tuple-element.62.inner, ...), custom_call_target="tpu_custom_call" | custom-call | flops 1 | bytes 1 | tf_op jit(solution)/shard_map/pallas_call | solution.py:364
  85.7 9.5 %collective-permute-done.4.refs_4_.refs_2_.refs_10_ = f32[776,128]{1,0:T(8,128)S(1)} collective-permute-done((f32[776,128]{1,0:T(8,128)}, f32[776,128]{1,0:T(8,128)S(1)}, u32[]{:S(2)}, u32[]{:S(2)}) %collective-permute-start.4) | collective-permute-done | bytes 397344 | tf_op jit(solution)/shard_map/ppermute | solution.py:591
  96.2 10.0 %collective-permute-start.10 = (f32[776,128]{1,0:T(8,128)}, f32[776,128]{1,0:T(8,128)S(1)}, u32[]{:S(2)}, u32[]{:S(2)}) collective-permute-start(f32[776,128]{1,0:T(8,128)} %get-tuple-element.83.refs_5_), channel_id=1, source_target_pairs={{0,3},{1,0},{2,1},{3,2},{4,7},{5,4},{6,5},{7,6},{8,11},{9,8},{10,9... | collective-permute-start | bytes 1191944 | tf_op jit(solution)/shard_map/ppermute | solution.py:591
  111.3 2.2 add.143
  120.7 4.4 %collective-permute-done.8.refs_5_.refs_13_ = f32[776,128]{1,0:T(8,128)S(1)} collective-permute-done((f32[776,128]{1,0:T(8,128)}, f32[776,128]{1,0:T(8,128)S(1)}, u32[]{:S(2)}, u32[]{:S(2)}) %collective-permute-start.8) | collective-permute-done | bytes 397344 | tf_op jit(solution)/shard_map/ppermute | solution.py:591
  125.1 16.3 %collective-permute-done.9.refs_6_.refs_14_ = f32[776,128]{1,0:T(8,128)S(1)} collective-permute-done((f32[776,128]{1,0:T(8,128)}, f32[776,128]{1,0:T(8,128)S(1)}, u32[]{:S(2)}, u32[]{:S(2)}) %collective-permute-start.9) | collective-permute-done | bytes 397344 | tf_op jit(solution)/shard_map/ppermute | solution.py:591
  142.2 9.1 %shard_map.161 = (f32[4,4,192,256]{3,2,1,0:T(8,128)}, f32[4,4,96,256]{3,2,1,0:T(8,128)}, f32[4,4,96,256]{3,2,1,0:T(8,128)}) custom-call(s32[1]{0:T(128)} %bitcast.2.core, f32[776,128]{1,0:T(8,128)} %get-tuple-element.65.refs_1_.refs_0_.refs_8_, f32[776,128]{1,0:T(8,128)} %copy-done.18, f32[776,128]{1,0:T(8,128)} %copy-done.19, f32[776,128]{1,0:T(8,128)} %copy-done.20, ...), custom_call_target="tpu_custom_call" | custom-call | flops 12000000000 | bytes 1 | tf_op jit(solution)/shard_map/pallas_call | solution.py:510
  160.6 2.1 collective-permute-start.12
  162.7 9.3 %collective-permute-done.15 = f32[2,2,208,128]{3,2,1,0:T(8,128)S(1)} collective-permute-done((f32[2,2,208,128]{3,2,1,0:T(8,128)}, f32[2,2,208,128]{3,2,1,0:T(8,128)S(1)}, u32[]{:S(2)}, u32[]{:S(2)}) %collective-permute-start.15) | collective-permute-done | bytes 426016 | tf_op jit(solution)/shard_map/ppermute | solution.py:396
  172.7 5.9 %collective-permute-done.16 = f32[2,208,128]{2,1,0:T(8,128)S(1)} collective-permute-done((f32[2,208,128]{2,1,0:T(8,128)S(1)}, f32[2,208,128]{2,1,0:T(8,128)S(1)}, u32[]{:S(2)}, u32[]{:S(2)}) %collective-permute-start.16) | collective-permute-done | bytes 213024 | tf_op jit(solution)/shard_map/ppermute | solution.py:396
  181.0 5.0 %shard_map.163 = (f32[2,4,96,256]{3,2,1,0:T(8,128)}, f32[2,4,96,256]{3,2,1,0:T(8,128)}, f32[2,4,96,256]{3,2,1,0:T(8,128)}, f32[2,4,96,256]{3,2,1,0:T(8,128)}) custom-call(s32[2]{0:T(128)} %pad_add_fusion.bits, f32[4,4,192,256]{3,2,1,0:T(8,128)} %get-tuple-element.91.refs_0_.refs_2_.refs_4_.refs_6_, f32[4,4,96,256]{3,2,1,0:T(8,128)} %copy-done.4, ...), custom_call_target="tpu_custom_call" | custom-call | flops 786432 | bytes 9437184 | tf_op jit(solution)/shard_map/pallas_call | solution.py:474
  188.7 2.1 collective-permute-start.20
  194.9 9.4 %collective-permute-done.19 = f32[2,4,96,256]{3,2,1,0:T(8,128)} collective-permute-done((f32[2,4,96,256]{3,2,1,0:T(8,128)}, f32[2,4,96,256]{3,2,1,0:T(8,128)}, u32[]{:S(2)}, u32[]{:S(2)}) %collective-permute-start.19) | collective-permute-done | bytes 786464 | tf_op jit(solution)/shard_map/ppermute | solution.py:396
  209.3 9.4 %collective-permute-done.17 = f32[256,512]{1,0:T(8,128)} collective-permute-done((f32[256,512]{1,0:T(8,128)}, f32[256,512]{1,0:T(8,128)}, u32[]{:S(2)}, u32[]{:S(2)}) %collective-permute-start.17) | collective-permute-done | bytes 524320 | tf_op jit(solution)/shard_map/ppermute | solution.py:396
  226.3 15.9 %collective-permute-done.25 = f32[208,128]{1,0:T(8,128)S(1)} collective-permute-done((f32[208,128]{1,0:T(8,128)}, f32[208,128]{1,0:T(8,128)S(1)}, u32[]{:S(2)}, u32[]{:S(2)}) %collective-permute-start.25) | collective-permute-done | bytes 106528 | tf_op jit(solution)/shard_map/ppermute | solution.py:396
  247.0 4.5 %collective-permute-done.27 = f32[2,208,128]{2,1,0:T(8,128)S(1)} collective-permute-done((f32[2,208,128]{2,1,0:T(8,128)}, f32[2,208,128]{2,1,0:T(8,128)S(1)}, u32[]{:S(2)}, u32[]{:S(2)}) %collective-permute-start.27) | collective-permute-done | bytes 213024 | tf_op jit(solution)/shard_map/ppermute | solution.py:396
  253.3 9.3 %collective-permute-done.26.refs_0_ = f32[4,192,256]{2,1,0:T(8,128)S(1)} collective-permute-done((f32[4,192,256]{2,1,0:T(8,128)}, f32[4,192,256]{2,1,0:T(8,128)S(1)}, u32[]{:S(2)}, u32[]{:S(2)}) %collective-permute-start.26) | collective-permute-done | bytes 786464 | tf_op jit(solution)/shard_map/ppermute | solution.py:591
  265.3 6.9 %collective-permute-done.28 = f32[2,2,208,128]{3,2,1,0:T(8,128)S(1)} collective-permute-done((f32[2,2,208,128]{3,2,1,0:T(8,128)}, f32[2,2,208,128]{3,2,1,0:T(8,128)S(1)}, u32[]{:S(2)}, u32[]{:S(2)}) %collective-permute-start.28) | collective-permute-done | bytes 426016 | tf_op jit(solution)/shard_map/ppermute | solution.py:396
  274.2 7.4 %collective-permute-done.29.refs_1_ = f32[4,192,256]{2,1,0:T(8,128)S(1)} collective-permute-done((f32[4,192,256]{2,1,0:T(8,128)}, f32[4,192,256]{2,1,0:T(8,128)S(1)}, u32[]{:S(2)}, u32[]{:S(2)}) %collective-permute-start.29) | collective-permute-done | bytes 786464 | tf_op jit(solution)/shard_map/ppermute | solution.py:591
  (180 shorter events, 72.5 us)
Async XLA Ops:
  34.4 15.9 %collective-permute-start = (f32[4,4,256,512]{3,2,1,0:T(8,128)}, f32[4,4,256,512]{3,2,1,0:T(8,128)}, u32[]{:S(2)}, u32[]{:S(2)}) collective-permute-start(f32[4,4,256,512]{3,2,1,0:T(8,128)} %get-tuple-element.60), channel_id=1, source_target_pairs={{0,4},{4,0},{8,12},{12,8},{16,20},{20,16},{24,28},{28,24},{1,5},{5... | collective-permute-start | bytes 25165832 | tf_op jit(solution)/shard_map/ppermute | solution.py:396
  60.9 49.2 %collective-permute-start.1 = (f32[2,4,128,512]{3,2,1,0:T(8,128)}, f32[2,4,128,512]{3,2,1,0:T(8,128)}, u32[]{:S(2)}, u32[]{:S(2)}) collective-permute-start(f32[2,4,128,512]{3,2,1,0:T(8,128)} %get-tuple-element.67.refs_1_), channel_id=1, source_target_pairs={{0,8},{4,12},{8,0},{12,4},{16,24},{20,28},{24,16},{28,20},{1,9},{5... | collective-permute-start | bytes 6291464 | tf_op jit(solution)/shard_map/ppermute | solution.py:396
  63.5 50.1 %collective-permute-start.2 = (f32[2,4,128,512]{3,2,1,0:T(8,128)}, f32[2,4,128,512]{3,2,1,0:T(8,128)S(1)}, u32[]{:S(2)}, u32[]{:S(2)}) collective-permute-start(f32[2,4,128,512]{3,2,1,0:T(8,128)} %get-tuple-element.69), channel_id=1, source_target_pairs={{0,16},{4,20},{8,24},{12,28},{16,0},{20,4},{24,8},{28,12},{1,17},{... | collective-permute-start | bytes 6291464 | tf_op jit(solution)/shard_map/ppermute | solution.py:396
  65.0 20.7 %collective-permute-start.3 = (f32[776,128]{1,0:T(8,128)}, f32[776,128]{1,0:T(8,128)S(1)}, u32[]{:S(2)}, u32[]{:S(2)}) collective-permute-start(f32[776,128]{1,0:T(8,128)} %get-tuple-element.78), channel_id=1, source_target_pairs={{0,1},{1,2},{2,3},{3,0},{4,5},{5,6},{6,7},{7,4},{8,9},{9,10},{10,1... | collective-permute-start | bytes 1191944 | tf_op jit(solution)/shard_map/ppermute | solution.py:591
  66.6 28.7 %collective-permute-start.4 = (f32[776,128]{1,0:T(8,128)}, f32[776,128]{1,0:T(8,128)S(1)}, u32[]{:S(2)}, u32[]{:S(2)}) collective-permute-start(f32[776,128]{1,0:T(8,128)} %get-tuple-element.79), channel_id=1, source_target_pairs={{0,2},{1,3},{2,0},{3,1},{4,6},{5,7},{6,4},{7,5},{8,10},{9,11},{10,... | collective-permute-start | bytes 1191944 | tf_op jit(solution)/shard_map/ppermute | solution.py:591
  69.2 26.1 %collective-permute-start.5 = (f32[776,128]{1,0:T(8,128)}, f32[776,128]{1,0:T(8,128)S(1)}, u32[]{:S(2)}, u32[]{:S(2)}) collective-permute-start(f32[776,128]{1,0:T(8,128)} %get-tuple-element.80), channel_id=1, source_target_pairs={{0,3},{1,0},{2,1},{3,2},{4,7},{5,4},{6,5},{7,6},{8,11},{9,8},{10,9... | collective-permute-start | bytes 1191944 | tf_op jit(solution)/shard_map/ppermute | solution.py:591
  96.2 23.0 %collective-permute-start.10 = (f32[776,128]{1,0:T(8,128)}, f32[776,128]{1,0:T(8,128)S(1)}, u32[]{:S(2)}, u32[]{:S(2)}) collective-permute-start(f32[776,128]{1,0:T(8,128)} %get-tuple-element.83.refs_5_), channel_id=1, source_target_pairs={{0,3},{1,0},{2,1},{3,2},{4,7},{5,4},{6,5},{7,6},{8,11},{9,8},{10,9... | collective-permute-start | bytes 1191944 | tf_op jit(solution)/shard_map/ppermute | solution.py:591
  106.2 18.9 %collective-permute-start.8 = (f32[776,128]{1,0:T(8,128)}, f32[776,128]{1,0:T(8,128)S(1)}, u32[]{:S(2)}, u32[]{:S(2)}) collective-permute-start(f32[776,128]{1,0:T(8,128)} %get-tuple-element.81.refs_3_), channel_id=1, source_target_pairs={{0,1},{1,2},{2,3},{3,0},{4,5},{5,6},{6,7},{7,4},{8,9},{9,10},{10,1... | collective-permute-start | bytes 1191944 | tf_op jit(solution)/shard_map/ppermute | solution.py:591
  106.2 35.3 %collective-permute-start.9 = (f32[776,128]{1,0:T(8,128)}, f32[776,128]{1,0:T(8,128)S(1)}, u32[]{:S(2)}, u32[]{:S(2)}) collective-permute-start(f32[776,128]{1,0:T(8,128)} %get-tuple-element.82.refs_4_), channel_id=1, source_target_pairs={{0,2},{1,3},{2,0},{3,1},{4,6},{5,7},{6,4},{7,5},{8,10},{9,11},{10,... | collective-permute-start | bytes 1191944 | tf_op jit(solution)/shard_map/ppermute | solution.py:591
  118.6 32.7 %collective-permute-start.11 = (f32[2,2,2,208,128]{4,3,2,1,0:T(8,128)}, f32[2,2,2,208,128]{4,3,2,1,0:T(8,128)}, u32[]{:S(2)}, u32[]{:S(2)}) collective-permute-start(f32[2,2,2,208,128]{4,3,2,1,0:T(8,128)} %get-tuple-element.89), channel_id=1, source_target_pairs={{0,4},{4,0},{8,12},{12,8},{16,20},{20,16},{24,28},{28,24},{1,5},{5... | collective-permute-start | bytes 2555912 | tf_op jit(solution)/shard_map/ppermute | solution.py:396
  118.7 35.1 %collective-permute-start.6 = (f32[2,2,128,512]{3,2,1,0:T(8,128)}, f32[2,2,128,512]{3,2,1,0:T(8,128)}, u32[]{:S(2)}, u32[]{:S(2)}) collective-permute-start(f32[2,2,128,512]{3,2,1,0:T(8,128)} %get-tuple-element.84), channel_id=1, source_target_pairs={{0,16},{4,20},{8,24},{12,28},{16,0},{20,4},{24,8},{28,12},{1,17},{... | collective-permute-start | bytes 3145736 | tf_op jit(solution)/shard_map/ppermute | solution.py:396
  119.2 37.0 %collective-permute-start.7 = (f32[2,2,128,512]{3,2,1,0:T(8,128)}, f32[2,2,128,512]{3,2,1,0:T(8,128)}, u32[]{:S(2)}, u32[]{:S(2)}) collective-permute-start(f32[2,2,128,512]{3,2,1,0:T(8,128)} %get-tuple-element.85), channel_id=1, source_target_pairs={{0,8},{4,12},{8,0},{12,4},{16,24},{20,28},{24,16},{28,20},{1,9},{5... | collective-permute-start | bytes 3145736 | tf_op jit(solution)/shard_map/ppermute | solution.py:396
  159.6 19.7 %collective-permute-start.13 = (f32[4,4,96,256]{3,2,1,0:T(8,128)}, f32[4,4,96,256]{3,2,1,0:T(8,128)S(1)}, u32[]{:S(2)}, u32[]{:S(2)}) collective-permute-start(f32[4,4,96,256]{3,2,1,0:T(8,128)} %get-tuple-element.92), channel_id=1, source_target_pairs={{0,4},{4,0},{8,12},{12,8},{16,20},{20,16},{24,28},{28,24},{1,5},{5... | collective-permute-start | bytes 4718600 | tf_op jit(solution)/shard_map/ppermute | solution.py:396
  159.6 19.7 %collective-permute-start.14 = (f32[4,4,96,256]{3,2,1,0:T(8,128)}, f32[4,4,96,256]{3,2,1,0:T(8,128)S(1)}, u32[]{:S(2)}, u32[]{:S(2)}) collective-permute-start(f32[4,4,96,256]{3,2,1,0:T(8,128)} %get-tuple-element.93), channel_id=1, source_target_pairs={{0,4},{4,0},{8,12},{12,8},{16,20},{20,16},{24,28},{28,24},{1,5},{5... | collective-permute-start | bytes 4718600 | tf_op jit(solution)/shard_map/ppermute | solution.py:396
  160.6 26.5 %collective-permute-start.12 = (f32[2,256,512]{2,1,0:T(8,128)}, f32[2,256,512]{2,1,0:T(8,128)}, u32[]{:S(2)}, u32[]{:S(2)}) collective-permute-start(f32[2,256,512]{2,1,0:T(8,128)} %get-tuple-element.90), channel_id=1, source_target_pairs={{0,1},{1,0},{2,3},{3,2},{4,5},{5,4},{6,7},{7,6},{8,9},{9,8},{10,11... | collective-permute-start | bytes 3145736 | tf_op jit(solution)/shard_map/ppermute | solution.py:396
  186.0 18.3 %collective-permute-start.19 = (f32[2,4,96,256]{3,2,1,0:T(8,128)}, f32[2,4,96,256]{3,2,1,0:T(8,128)}, u32[]{:S(2)}, u32[]{:S(2)}) collective-permute-start(f32[2,4,96,256]{3,2,1,0:T(8,128)} %get-tuple-element.98.refs_2_), channel_id=1, source_target_pairs={{0,16},{4,20},{8,24},{12,28},{16,0},{20,4},{24,8},{28,12},{1,17},{... | collective-permute-start | bytes 2359304 | tf_op jit(solution)/shard_map/ppermute | solution.py:396
  186.5 18.9 %collective-permute-start.18 = (f32[2,4,96,256]{3,2,1,0:T(8,128)}, f32[2,4,96,256]{3,2,1,0:T(8,128)}, u32[]{:S(2)}, u32[]{:S(2)}) collective-permute-start(f32[2,4,96,256]{3,2,1,0:T(8,128)} %get-tuple-element.97.refs_1_), channel_id=1, source_target_pairs={{0,8},{4,12},{8,0},{12,4},{16,24},{20,28},{24,16},{28,20},{1,9},{5... | collective-permute-start | bytes 2359304 | tf_op jit(solution)/shard_map/ppermute | solution.py:396
  191.6 27.1 %collective-permute-start.17 = (f32[256,512]{1,0:T(8,128)}, f32[256,512]{1,0:T(8,128)}, u32[]{:S(2)}, u32[]{:S(2)}) collective-permute-start(f32[256,512]{1,0:T(8,128)} %shard_map.165), channel_id=1, source_target_pairs={{0,2},{1,3},{2,0},{3,1},{4,6},{5,7},{6,4},{7,5},{8,10},{9,11},{10,... | collective-permute-start | bytes 1572872 | tf_op jit(solution)/shard_map/ppermute | solution.py:396
  208.3 13.9 %collective-permute-start.21 = (f32[4,96,256]{2,1,0:T(8,128)}, f32[4,96,256]{2,1,0:T(8,128)S(1)}, u32[]{:S(2)}, u32[]{:S(2)}) collective-permute-start(f32[4,96,256]{2,1,0:T(8,128)} %get-tuple-element.102), channel_id=1, source_target_pairs={{0,16},{4,20},{8,24},{12,28},{16,0},{20,4},{24,8},{28,12},{1,17},{... | collective-permute-start | bytes 1179656 | tf_op jit(solution)/shard_map/ppermute | solution.py:396
  208.8 13.5 %collective-permute-start.22 = (f32[4,96,256]{2,1,0:T(8,128)}, f32[4,96,256]{2,1,0:T(8,128)S(1)}, u32[]{:S(2)}, u32[]{:S(2)}) collective-permute-start(f32[4,96,256]{2,1,0:T(8,128)} %get-tuple-element.103), channel_id=1, source_target_pairs={{0,8},{4,12},{8,0},{12,4},{16,24},{20,28},{24,16},{28,20},{1,9},{5... | collective-permute-start | bytes 1179656 | tf_op jit(solution)/shard_map/ppermute | solution.py:396
  223.3 20.7 %collective-permute-start.24 = (f32[4,192,256]{2,1,0:T(8,128)}, f32[4,192,256]{2,1,0:T(8,128)S(1)}, u32[]{:S(2)}, u32[]{:S(2)}) collective-permute-start(f32[4,192,256]{2,1,0:T(8,128)} %get-tuple-element.105), channel_id=1, source_target_pairs={{0,1},{1,2},{2,3},{3,0},{4,5},{5,6},{6,7},{7,4},{8,9},{9,10},{10,1... | collective-permute-start | bytes 2359304 | tf_op jit(solution)/shard_map/ppermute | solution.py:591
  223.3 18.9 %collective-permute-start.25 = (f32[208,128]{1,0:T(8,128)}, f32[208,128]{1,0:T(8,128)S(1)}, u32[]{:S(2)}, u32[]{:S(2)}) collective-permute-start(f32[208,128]{1,0:T(8,128)} %get-tuple-element.106), channel_id=1, source_target_pairs={{0,1},{1,0},{2,3},{3,2},{4,5},{5,4},{6,7},{7,6},{8,9},{9,8},{10,11... | collective-permute-start | bytes 319496 | tf_op jit(solution)/shard_map/ppermute | solution.py:396
  245.2 17.5 %collective-permute-start.26 = (f32[4,192,256]{2,1,0:T(8,128)}, f32[4,192,256]{2,1,0:T(8,128)S(1)}, u32[]{:S(2)}, u32[]{:S(2)}) collective-permute-start(f32[4,192,256]{2,1,0:T(8,128)} %get-tuple-element.107), channel_id=1, source_target_pairs={{0,1},{1,2},{2,3},{3,0},{4,5},{5,6},{6,7},{7,4},{8,9},{9,10},{10,1... | collective-permute-start | bytes 2359304 | tf_op jit(solution)/shard_map/ppermute | solution.py:591
  265.3 16.3 %collective-permute-start.29 = (f32[4,192,256]{2,1,0:T(8,128)}, f32[4,192,256]{2,1,0:T(8,128)S(1)}, u32[]{:S(2)}, u32[]{:S(2)}) collective-permute-start(f32[4,192,256]{2,1,0:T(8,128)} %get-tuple-element.110), channel_id=1, source_target_pairs={{0,1},{1,2},{2,3},{3,0},{4,5},{5,6},{6,7},{7,4},{8,9},{9,10},{10,1... | collective-permute-start | bytes 2359304 | tf_op jit(solution)/shard_map/ppermute | solution.py:591
  (37 other events, 304.3 us)

commit v5 on v4

--- a/solution.py
+++ b/solution.py
@@ -92,7 +92,7 @@
     wide,
     core,
     x,
-    up,
+    up_in,
     proj,
     w_first_in,
     w_second_in,
@@ -115,6 +115,7 @@
     d_pre,
     w_first,
     w_second,
+    up,
     arrived,
 ):
     step = pl.program_id(0)
@@ -128,6 +129,8 @@
         second_copy = pltpu.make_async_copy(w_second_in, w_second, arrived.at[1])
         first_copy.start()
         second_copy.start()
+        up_copy = pltpu.make_async_copy(up_in, up, arrived.at[2])
+        up_copy.start()
         unit = eye(samples)
         for n in range(TABLES):
             xs[n] = mm(unit, x[n], NT).astype(jnp.bfloat16)
@@ -159,6 +162,7 @@
         lax.fori_loop(0, groups, group, 0, unroll=4)
         first_copy.wait()
         second_copy.wait()
+        up_copy.wait()
         pairs = flat.shape[1]
         block = 256
         unit_b = eye(block)
@@ -259,7 +263,7 @@
         grid_spec=pltpu.PrefetchScalarGridSpec(
             num_scalar_prefetch=1,
             grid=(half,),
-            in_specs=[whole(a.shape) for a in (x, up, proj)]
+            in_specs=[whole(x.shape), pl.BlockSpec(memory_space=pl.ANY), whole(proj.shape)]
             + [pl.BlockSpec(memory_space=pl.ANY)] * 2
             + [whole(a.shape) for a in (comp, gain)],
             out_specs=[by_step(sums)] * 2 + [whole(r.shape) for r in rest],
@@ -274,7 +278,8 @@
                 pltpu.VMEM((samples, hidden_size), bf16),
                 pltpu.VMEM(w_first.shape, bf16),
                 pltpu.VMEM(w_second.shape, bf16),
-                pltpu.SemaphoreType.DMA((2,)),
+                pltpu.VMEM(up.shape, bf16),
+                pltpu.SemaphoreType.DMA((3,)),
             ],
         ),
         out_shape=[sums, sums] + rest,
@@ -316,7 +321,7 @@
         totals[...] += mm(jnp.concatenate([d_inner, d_lc_g], axis=0), xg, NT)
         return carry
 
-    lax.fori_loop(0, samples // GROUP, group, 0, unroll=2)
+    lax.fori_loop(0, samples // GROUP, group, 0, unroll=4)
     unit = eye(D)
     for step in range(narrow):
         target = lax.rem(here[0] + step, narrow)

time: 290 us -> 289 us (level)
  transfers between devices with their start and end apart: 31 -> 31, of which waited for: 15 -> 15; matrix products, arithmetic and copies ran while one was open for 13% -> 13% of each run, Pallas kernels for 15% -> 14%
where the time goes in v5:
time: 289 us; the launch traced here: 288 us
  waiting for transfers between devices  112 us (39%)
  Pallas kernels  83.7 us (29%)
  starting transfers between devices  35.3 us (12%)
  other arithmetic  29 us (10%)
  local copies, waits for them, and re-layouts  27.3 us (9%)
    ppermute x22, waiting for transfers between devices, flip(): lax.ppermute(value, axis, [(i, i ^ 1 << bit) for i in range(lax.axis_size...  63.3 us
    ppermute x9, waiting for transfers between devices, go_round(): lax.ppermute(value, 'narrow', [(i, (i + step) % narrow) for i in range(na...  48.7 us
    pallas_call x1, Pallas kernels, mlp(): pl.pallas_call(functools.partial(mlp_kernel, wide), grid_spec=pltpu.Prefe...  31.9 us
    pallas_call x2, Pallas kernels, row_gradients(): pl.pallas_call(functools.partial(rows_kernel, narrow), grid=(1,), in_spec...  27.3 us
    ppermute x22, starting transfers between devices, flip(): lax.ppermute(value, axis, [(i, i ^ 1 << bit) for i in range(lax.axis_size...  18.9 us
    ppermute x9, starting transfers between devices, go_round(): lax.ppermute(value, 'narrow', [(i, (i + step) % narrow) for i in range(na...  16.4 us
    add x14, other arithmetic, finish(): keep + flip(send, *label)  15.6 us
    pallas_call x2, Pallas kernels, combine(): pl.pallas_call(functools.partial(combine_kernel, cuts), grid_spec=pltpu.P...  15.6 us
  transfers between devices with their start and end apart: 31, of which 15 were waited for; matrix products, arithmetic and copies ran while one was open for 13% of the time, Pallas kernels for 14%

profile of v5, /device:TPU:0, one launch (start us, length us, event | category | flops | bytes accessed | tf_op | source)
XLA Modules:
  0.0 288.4 jit_solution(12521919364727905351)
XLA Ops:
  2.0 31.9 %shard_map.153 = (f32[4,4,256,512]{3,2,1,0:T(8,128)}, f32[4,4,256,512]{3,2,1,0:T(8,128)}, bf16[32,256,192]{2,1,0:T(8,128)(2,1)}, bf16[16,256,192]{2,1,0:T(8,128)...) custom-call(s32[1]{0:T(128)} %bitcast.2.core, bf16[32,192,256]{2,1,0:T(8,128)(2,1)} %bitcast.129, ...), custom_call_target="tpu_custom_call" | custom-call | flops 16000000000 | bytes 32000000 | tf_op jit(solution)/shard_map/pallas_call | solution.py:261
  35.1 13.6 %shard_map.154 = (f32[776,128]{1,0:T(8,128)}, f32[776,128]{1,0:T(8,128)}, f32[776,128]{1,0:T(8,128)}, f32[776,128]{1,0:T(8,128)}, f32[16,192,128]{2,1,0:T(8,128)}, /*index=5*/f32[24,32]{1,0:T(8,128)}) custom-call(s32[1]{0:T(128)} %bitcast.6.here, bf16[32,256,192]{2,1,0:T(8,128)(2,1)} %get-tuple-element.61.xs, bf16[16,256,192]{2,1,0:T(8,128)(2,1)} %get-tuple-element.62.inner, ...), custom_call_target="tpu_custom_call" | custom-call | flops 1 | bytes 1 | tf_op jit(solution)/shard_map/pallas_call | solution.py:369
  49.4 10.6 %shard_map.156 = (f32[2,4,128,512]{3,2,1,0:T(8,128)}, f32[2,4,128,512]{3,2,1,0:T(8,128)}, f32[2,4,128,512]{3,2,1,0:T(8,128)}, f32[2,4,128,512]{3,2,1,0:T(8,128)}) custom-call(s32[2]{0:T(128)} %pad_add_fusion.bits, f32[4,4,256,512]{3,2,1,0:T(8,128)} %get-tuple-element.59.refs_0_.refs_2_.refs_4_.refs_6_, ...), custom_call_target="tpu_custom_call" | custom-call | flops 2097152 | bytes 25165824 | tf_op jit(solution)/shard_map/pallas_call | solution.py:479
  60.0 2.6 collective-permute-start.1
  65.7 2.6 collective-permute-start.4
  69.8 13.7 %shard_map.158 = (f32[776,128]{1,0:T(8,128)}, f32[776,128]{1,0:T(8,128)}, f32[776,128]{1,0:T(8,128)}, f32[776,128]{1,0:T(8,128)}, f32[16,192,128]{2,1,0:T(8,128)}, /*index=5*/f32[24,32]{1,0:T(8,128)}) custom-call(s32[1]{0:T(128)} %bitcast.6.here, bf16[32,256,192]{2,1,0:T(8,128)(2,1)} %get-tuple-element.61.xs, bf16[16,256,192]{2,1,0:T(8,128)(2,1)} %get-tuple-element.62.inner, ...), custom_call_target="tpu_custom_call" | custom-call | flops 1 | bytes 1 | tf_op jit(solution)/shard_map/pallas_call | solution.py:369
  84.4 10.0 %collective-permute-done.4.refs_4_.refs_2_.refs_10_ = f32[776,128]{1,0:T(8,128)S(1)} collective-permute-done((f32[776,128]{1,0:T(8,128)}, f32[776,128]{1,0:T(8,128)S(1)}, u32[]{:S(2)}, u32[]{:S(2)}) %collective-permute-start.4) | collective-permute-done | bytes 397344 | tf_op jit(solution)/shard_map/ppermute | solution.py:596
  95.3 10.0 %collective-permute-start.10 = (f32[776,128]{1,0:T(8,128)}, f32[776,128]{1,0:T(8,128)S(1)}, u32[]{:S(2)}, u32[]{:S(2)}) collective-permute-start(f32[776,128]{1,0:T(8,128)} %get-tuple-element.83.refs_5_), channel_id=1, source_target_pairs={{0,3},{1,0},{2,1},{3,2},{4,7},{5,4},{6,5},{7,6},{8,11},{9,8},{10,9... | collective-permute-start | bytes 1191944 | tf_op jit(solution)/shard_map/ppermute | solution.py:596
  110.4 2.2 add.143
  119.8 4.4 %collective-permute-done.8.refs_5_.refs_13_ = f32[776,128]{1,0:T(8,128)S(1)} collective-permute-done((f32[776,128]{1,0:T(8,128)}, f32[776,128]{1,0:T(8,128)S(1)}, u32[]{:S(2)}, u32[]{:S(2)}) %collective-permute-start.8) | collective-permute-done | bytes 397344 | tf_op jit(solution)/shard_map/ppermute | solution.py:596
  124.2 16.3 %collective-permute-done.9.refs_6_.refs_14_ = f32[776,128]{1,0:T(8,128)S(1)} collective-permute-done((f32[776,128]{1,0:T(8,128)}, f32[776,128]{1,0:T(8,128)S(1)}, u32[]{:S(2)}, u32[]{:S(2)}) %collective-permute-start.9) | collective-permute-done | bytes 397344 | tf_op jit(solution)/shard_map/ppermute | solution.py:596
  141.3 8.9 %shard_map.161 = (f32[4,4,192,256]{3,2,1,0:T(8,128)}, f32[4,4,96,256]{3,2,1,0:T(8,128)}, f32[4,4,96,256]{3,2,1,0:T(8,128)}) custom-call(s32[1]{0:T(128)} %bitcast.2.core, f32[776,128]{1,0:T(8,128)} %get-tuple-element.65.refs_1_.refs_0_.refs_8_, f32[776,128]{1,0:T(8,128)} %copy-done.18, f32[776,128]{1,0:T(8,128)} %copy-done.19, f32[776,128]{1,0:T(8,128)} %copy-done.20, ...), custom_call_target="tpu_custom_call" | custom-call | flops 12000000000 | bytes 1 | tf_op jit(solution)/shard_map/pallas_call | solution.py:515
  159.5 2.3 collective-permute-start.12
  161.8 9.1 %collective-permute-done.15 = f32[2,2,208,128]{3,2,1,0:T(8,128)S(1)} collective-permute-done((f32[2,2,208,128]{3,2,1,0:T(8,128)}, f32[2,2,208,128]{3,2,1,0:T(8,128)S(1)}, u32[]{:S(2)}, u32[]{:S(2)}) %collective-permute-start.15) | collective-permute-done | bytes 426016 | tf_op jit(solution)/shard_map/ppermute | solution.py:401
  171.6 5.9 %collective-permute-done.16 = f32[2,208,128]{2,1,0:T(8,128)S(1)} collective-permute-done((f32[2,208,128]{2,1,0:T(8,128)S(1)}, f32[2,208,128]{2,1,0:T(8,128)S(1)}, u32[]{:S(2)}, u32[]{:S(2)}) %collective-permute-start.16) | collective-permute-done | bytes 213024 | tf_op jit(solution)/shard_map/ppermute | solution.py:401
  179.9 5.0 %shard_map.163 = (f32[2,4,96,256]{3,2,1,0:T(8,128)}, f32[2,4,96,256]{3,2,1,0:T(8,128)}, f32[2,4,96,256]{3,2,1,0:T(8,128)}, f32[2,4,96,256]{3,2,1,0:T(8,128)}) custom-call(s32[2]{0:T(128)} %pad_add_fusion.bits, f32[4,4,192,256]{3,2,1,0:T(8,128)} %get-tuple-element.91.refs_0_.refs_2_.refs_4_.refs_6_, f32[4,4,96,256]{3,2,1,0:T(8,128)} %copy-done.4, ...), custom_call_target="tpu_custom_call" | custom-call | flops 786432 | bytes 9437184 | tf_op jit(solution)/shard_map/pallas_call | solution.py:479
  187.6 2.4 collective-permute-start.20
  194.0 9.1 %collective-permute-done.19 = f32[2,4,96,256]{3,2,1,0:T(8,128)} collective-permute-done((f32[2,4,96,256]{3,2,1,0:T(8,128)}, f32[2,4,96,256]{3,2,1,0:T(8,128)}, u32[]{:S(2)}, u32[]{:S(2)}) %collective-permute-start.19) | collective-permute-done | bytes 786464 | tf_op jit(solution)/shard_map/ppermute | solution.py:401
  208.3 9.6 %collective-permute-done.17 = f32[256,512]{1,0:T(8,128)} collective-permute-done((f32[256,512]{1,0:T(8,128)}, f32[256,512]{1,0:T(8,128)}, u32[]{:S(2)}, u32[]{:S(2)}) %collective-permute-start.17) | collective-permute-done | bytes 524320 | tf_op jit(solution)/shard_map/ppermute | solution.py:401
  225.4 16.2 %collective-permute-done.25 = f32[208,128]{1,0:T(8,128)S(1)} collective-permute-done((f32[208,128]{1,0:T(8,128)}, f32[208,128]{1,0:T(8,128)S(1)}, u32[]{:S(2)}, u32[]{:S(2)}) %collective-permute-start.25) | collective-permute-done | bytes 106528 | tf_op jit(solution)/shard_map/ppermute | solution.py:401
  246.3 4.5 %collective-permute-done.27 = f32[2,208,128]{2,1,0:T(8,128)S(1)} collective-permute-done((f32[2,208,128]{2,1,0:T(8,128)}, f32[2,208,128]{2,1,0:T(8,128)S(1)}, u32[]{:S(2)}, u32[]{:S(2)}) %collective-permute-start.27) | collective-permute-done | bytes 213024 | tf_op jit(solution)/shard_map/ppermute | solution.py:401
  252.6 9.5 %collective-permute-done.26.refs_0_ = f32[4,192,256]{2,1,0:T(8,128)S(1)} collective-permute-done((f32[4,192,256]{2,1,0:T(8,128)}, f32[4,192,256]{2,1,0:T(8,128)S(1)}, u32[]{:S(2)}, u32[]{:S(2)}) %collective-permute-start.26) | collective-permute-done | bytes 786464 | tf_op jit(solution)/shard_map/ppermute | solution.py:596
  264.7 6.9 %collective-permute-done.28 = f32[2,2,208,128]{3,2,1,0:T(8,128)S(1)} collective-permute-done((f32[2,2,208,128]{3,2,1,0:T(8,128)}, f32[2,2,208,128]{3,2,1,0:T(8,128)S(1)}, u32[]{:S(2)}, u32[]{:S(2)}) %collective-permute-start.28) | collective-permute-done | bytes 426016 | tf_op jit(solution)/shard_map/ppermute | solution.py:401
  273.6 7.6 %collective-permute-done.29.refs_1_ = f32[4,192,256]{2,1,0:T(8,128)S(1)} collective-permute-done((f32[4,192,256]{2,1,0:T(8,128)}, f32[4,192,256]{2,1,0:T(8,128)S(1)}, u32[]{:S(2)}, u32[]{:S(2)}) %collective-permute-start.29) | collective-permute-done | bytes 786464 | tf_op jit(solution)/shard_map/ppermute | solution.py:596
  (180 shorter events, 72.4 us)
Async XLA Ops:
  33.9 15.4 %collective-permute-start = (f32[4,4,256,512]{3,2,1,0:T(8,128)}, f32[4,4,256,512]{3,2,1,0:T(8,128)}, u32[]{:S(2)}, u32[]{:S(2)}) collective-permute-start(f32[4,4,256,512]{3,2,1,0:T(8,128)} %get-tuple-element.60), channel_id=1, source_target_pairs={{0,4},{4,0},{8,12},{12,8},{16,20},{20,16},{24,28},{28,24},{1,5},{5... | collective-permute-start | bytes 25165832 | tf_op jit(solution)/shard_map/ppermute | solution.py:401
  60.0 49.2 %collective-permute-start.1 = (f32[2,4,128,512]{3,2,1,0:T(8,128)}, f32[2,4,128,512]{3,2,1,0:T(8,128)}, u32[]{:S(2)}, u32[]{:S(2)}) collective-permute-start(f32[2,4,128,512]{3,2,1,0:T(8,128)} %get-tuple-element.67.refs_1_), channel_id=1, source_target_pairs={{0,8},{4,12},{8,0},{12,4},{16,24},{20,28},{24,16},{28,20},{1,9},{5... | collective-permute-start | bytes 6291464 | tf_op jit(solution)/shard_map/ppermute | solution.py:401
  62.6 50.1 %collective-permute-start.2 = (f32[2,4,128,512]{3,2,1,0:T(8,128)}, f32[2,4,128,512]{3,2,1,0:T(8,128)S(1)}, u32[]{:S(2)}, u32[]{:S(2)}) collective-permute-start(f32[2,4,128,512]{3,2,1,0:T(8,128)} %get-tuple-element.69), channel_id=1, source_target_pairs={{0,16},{4,20},{8,24},{12,28},{16,0},{20,4},{24,8},{28,12},{1,17},{... | collective-permute-start | bytes 6291464 | tf_op jit(solution)/shard_map/ppermute | solution.py:401
  64.1 20.3 %collective-permute-start.3 = (f32[776,128]{1,0:T(8,128)}, f32[776,128]{1,0:T(8,128)S(1)}, u32[]{:S(2)}, u32[]{:S(2)}) collective-permute-start(f32[776,128]{1,0:T(8,128)} %get-tuple-element.78), channel_id=1, source_target_pairs={{0,1},{1,2},{2,3},{3,0},{4,5},{5,6},{6,7},{7,4},{8,9},{9,10},{10,1... | collective-permute-start | bytes 1191944 | tf_op jit(solution)/shard_map/ppermute | solution.py:596
  65.7 28.7 %collective-permute-start.4 = (f32[776,128]{1,0:T(8,128)}, f32[776,128]{1,0:T(8,128)S(1)}, u32[]{:S(2)}, u32[]{:S(2)}) collective-permute-start(f32[776,128]{1,0:T(8,128)} %get-tuple-element.79), channel_id=1, source_target_pairs={{0,2},{1,3},{2,0},{3,1},{4,6},{5,7},{6,4},{7,5},{8,10},{9,11},{10,... | collective-permute-start | bytes 1191944 | tf_op jit(solution)/shard_map/ppermute | solution.py:596
  68.3 26.1 %collective-permute-start.5 = (f32[776,128]{1,0:T(8,128)}, f32[776,128]{1,0:T(8,128)S(1)}, u32[]{:S(2)}, u32[]{:S(2)}) collective-permute-start(f32[776,128]{1,0:T(8,128)} %get-tuple-element.80), channel_id=1, source_target_pairs={{0,3},{1,0},{2,1},{3,2},{4,7},{5,4},{6,5},{7,6},{8,11},{9,8},{10,9... | collective-permute-start | bytes 1191944 | tf_op jit(solution)/shard_map/ppermute | solution.py:596
  95.3 23.0 %collective-permute-start.10 = (f32[776,128]{1,0:T(8,128)}, f32[776,128]{1,0:T(8,128)S(1)}, u32[]{:S(2)}, u32[]{:S(2)}) collective-permute-start(f32[776,128]{1,0:T(8,128)} %get-tuple-element.83.refs_5_), channel_id=1, source_target_pairs={{0,3},{1,0},{2,1},{3,2},{4,7},{5,4},{6,5},{7,6},{8,11},{9,8},{10,9... | collective-permute-start | bytes 1191944 | tf_op jit(solution)/shard_map/ppermute | solution.py:596
  105.3 18.9 %collective-permute-start.8 = (f32[776,128]{1,0:T(8,128)}, f32[776,128]{1,0:T(8,128)S(1)}, u32[]{:S(2)}, u32[]{:S(2)}) collective-permute-start(f32[776,128]{1,0:T(8,128)} %get-tuple-element.81.refs_3_), channel_id=1, source_target_pairs={{0,1},{1,2},{2,3},{3,0},{4,5},{5,6},{6,7},{7,4},{8,9},{9,10},{10,1... | collective-permute-start | bytes 1191944 | tf_op jit(solution)/shard_map/ppermute | solution.py:596
  105.3 35.3 %collective-permute-start.9 = (f32[776,128]{1,0:T(8,128)}, f32[776,128]{1,0:T(8,128)S(1)}, u32[]{:S(2)}, u32[]{:S(2)}) collective-permute-start(f32[776,128]{1,0:T(8,128)} %get-tuple-element.82.refs_4_), channel_id=1, source_target_pairs={{0,2},{1,3},{2,0},{3,1},{4,6},{5,7},{6,4},{7,5},{8,10},{9,11},{10,... | collective-permute-start | bytes 1191944 | tf_op jit(solution)/shard_map/ppermute | solution.py:596
  117.8 32.4 %collective-permute-start.11 = (f32[2,2,2,208,128]{4,3,2,1,0:T(8,128)}, f32[2,2,2,208,128]{4,3,2,1,0:T(8,128)}, u32[]{:S(2)}, u32[]{:S(2)}) collective-permute-start(f32[2,2,2,208,128]{4,3,2,1,0:T(8,128)} %get-tuple-element.89), channel_id=1, source_target_pairs={{0,4},{4,0},{8,12},{12,8},{16,20},{20,16},{24,28},{28,24},{1,5},{5... | collective-permute-start | bytes 2555912 | tf_op jit(solution)/shard_map/ppermute | solution.py:401
  117.8 34.9 %collective-permute-start.6 = (f32[2,2,128,512]{3,2,1,0:T(8,128)}, f32[2,2,128,512]{3,2,1,0:T(8,128)}, u32[]{:S(2)}, u32[]{:S(2)}) collective-permute-start(f32[2,2,128,512]{3,2,1,0:T(8,128)} %get-tuple-element.84), channel_id=1, source_target_pairs={{0,16},{4,20},{8,24},{12,28},{16,0},{20,4},{24,8},{28,12},{1,17},{... | collective-permute-start | bytes 3145736 | tf_op jit(solution)/shard_map/ppermute | solution.py:401
  118.3 36.8 %collective-permute-start.7 = (f32[2,2,128,512]{3,2,1,0:T(8,128)}, f32[2,2,128,512]{3,2,1,0:T(8,128)}, u32[]{:S(2)}, u32[]{:S(2)}) collective-permute-start(f32[2,2,128,512]{3,2,1,0:T(8,128)} %get-tuple-element.85), channel_id=1, source_target_pairs={{0,8},{4,12},{8,0},{12,4},{16,24},{20,28},{24,16},{28,20},{1,9},{5... | collective-permute-start | bytes 3145736 | tf_op jit(solution)/shard_map/ppermute | solution.py:401
  158.5 19.7 %collective-permute-start.13 = (f32[4,4,96,256]{3,2,1,0:T(8,128)}, f32[4,4,96,256]{3,2,1,0:T(8,128)S(1)}, u32[]{:S(2)}, u32[]{:S(2)}) collective-permute-start(f32[4,4,96,256]{3,2,1,0:T(8,128)} %get-tuple-element.92), channel_id=1, source_target_pairs={{0,4},{4,0},{8,12},{12,8},{16,20},{20,16},{24,28},{28,24},{1,5},{5... | collective-permute-start | bytes 4718600 | tf_op jit(solution)/shard_map/ppermute | solution.py:401
  158.5 19.7 %collective-permute-start.14 = (f32[4,4,96,256]{3,2,1,0:T(8,128)}, f32[4,4,96,256]{3,2,1,0:T(8,128)S(1)}, u32[]{:S(2)}, u32[]{:S(2)}) collective-permute-start(f32[4,4,96,256]{3,2,1,0:T(8,128)} %get-tuple-element.93), channel_id=1, source_target_pairs={{0,4},{4,0},{8,12},{12,8},{16,20},{20,16},{24,28},{28,24},{1,5},{5... | collective-permute-start | bytes 4718600 | tf_op jit(solution)/shard_map/ppermute | solution.py:401
  159.5 26.4 %collective-permute-start.12 = (f32[2,256,512]{2,1,0:T(8,128)}, f32[2,256,512]{2,1,0:T(8,128)}, u32[]{:S(2)}, u32[]{:S(2)}) collective-permute-start(f32[2,256,512]{2,1,0:T(8,128)} %get-tuple-element.90), channel_id=1, source_target_pairs={{0,1},{1,0},{2,3},{3,2},{4,5},{5,4},{6,7},{7,6},{8,9},{9,8},{10,11... | collective-permute-start | bytes 3145736 | tf_op jit(solution)/shard_map/ppermute | solution.py:401
  184.9 18.3 %collective-permute-start.19 = (f32[2,4,96,256]{3,2,1,0:T(8,128)}, f32[2,4,96,256]{3,2,1,0:T(8,128)}, u32[]{:S(2)}, u32[]{:S(2)}) collective-permute-start(f32[2,4,96,256]{3,2,1,0:T(8,128)} %get-tuple-element.98.refs_2_), channel_id=1, source_target_pairs={{0,16},{4,20},{8,24},{12,28},{16,0},{20,4},{24,8},{28,12},{1,17},{... | collective-permute-start | bytes 2359304 | tf_op jit(solution)/shard_map/ppermute | solution.py:401
  185.4 18.9 %collective-permute-start.18 = (f32[2,4,96,256]{3,2,1,0:T(8,128)}, f32[2,4,96,256]{3,2,1,0:T(8,128)}, u32[]{:S(2)}, u32[]{:S(2)}) collective-permute-start(f32[2,4,96,256]{3,2,1,0:T(8,128)} %get-tuple-element.97.refs_1_), channel_id=1, source_target_pairs={{0,8},{4,12},{8,0},{12,4},{16,24},{20,28},{24,16},{28,20},{1,9},{5... | collective-permute-start | bytes 2359304 | tf_op jit(solution)/shard_map/ppermute | solution.py:401
  190.8 27.1 %collective-permute-start.17 = (f32[256,512]{1,0:T(8,128)}, f32[256,512]{1,0:T(8,128)}, u32[]{:S(2)}, u32[]{:S(2)}) collective-permute-start(f32[256,512]{1,0:T(8,128)} %shard_map.165), channel_id=1, source_target_pairs={{0,2},{1,3},{2,0},{3,1},{4,6},{5,7},{6,4},{7,5},{8,10},{9,11},{10,... | collective-permute-start | bytes 1572872 | tf_op jit(solution)/shard_map/ppermute | solution.py:401
  207.2 14.1 %collective-permute-start.21 = (f32[4,96,256]{2,1,0:T(8,128)}, f32[4,96,256]{2,1,0:T(8,128)S(1)}, u32[]{:S(2)}, u32[]{:S(2)}) collective-permute-start(f32[4,96,256]{2,1,0:T(8,128)} %get-tuple-element.102), channel_id=1, source_target_pairs={{0,16},{4,20},{8,24},{12,28},{16,0},{20,4},{24,8},{28,12},{1,17},{... | collective-permute-start | bytes 1179656 | tf_op jit(solution)/shard_map/ppermute | solution.py:401
  207.7 13.6 %collective-permute-start.22 = (f32[4,96,256]{2,1,0:T(8,128)}, f32[4,96,256]{2,1,0:T(8,128)S(1)}, u32[]{:S(2)}, u32[]{:S(2)}) collective-permute-start(f32[4,96,256]{2,1,0:T(8,128)} %get-tuple-element.103), channel_id=1, source_target_pairs={{0,8},{4,12},{8,0},{12,4},{16,24},{20,28},{24,16},{28,20},{1,9},{5... | collective-permute-start | bytes 1179656 | tf_op jit(solution)/shard_map/ppermute | solution.py:401
  222.4 20.9 %collective-permute-start.24 = (f32[4,192,256]{2,1,0:T(8,128)}, f32[4,192,256]{2,1,0:T(8,128)S(1)}, u32[]{:S(2)}, u32[]{:S(2)}) collective-permute-start(f32[4,192,256]{2,1,0:T(8,128)} %get-tuple-element.105), channel_id=1, source_target_pairs={{0,1},{1,2},{2,3},{3,0},{4,5},{5,6},{6,7},{7,4},{8,9},{9,10},{10,1... | collective-permute-start | bytes 2359304 | tf_op jit(solution)/shard_map/ppermute | solution.py:596
  222.4 19.3 %collective-permute-start.25 = (f32[208,128]{1,0:T(8,128)}, f32[208,128]{1,0:T(8,128)S(1)}, u32[]{:S(2)}, u32[]{:S(2)}) collective-permute-start(f32[208,128]{1,0:T(8,128)} %get-tuple-element.106), channel_id=1, source_target_pairs={{0,1},{1,0},{2,3},{3,2},{4,5},{5,4},{6,7},{7,6},{8,9},{9,8},{10,11... | collective-permute-start | bytes 319496 | tf_op jit(solution)/shard_map/ppermute | solution.py:401
  244.4 17.7 %collective-permute-start.26 = (f32[4,192,256]{2,1,0:T(8,128)}, f32[4,192,256]{2,1,0:T(8,128)S(1)}, u32[]{:S(2)}, u32[]{:S(2)}) collective-permute-start(f32[4,192,256]{2,1,0:T(8,128)} %get-tuple-element.107), channel_id=1, source_target_pairs={{0,1},{1,2},{2,3},{3,0},{4,5},{5,6},{6,7},{7,4},{8,9},{9,10},{10,1... | collective-permute-start | bytes 2359304 | tf_op jit(solution)/shard_map/ppermute | solution.py:596
  264.7 16.5 %collective-permute-start.29 = (f32[4,192,256]{2,1,0:T(8,128)}, f32[4,192,256]{2,1,0:T(8,128)S(1)}, u32[]{:S(2)}, u32[]{:S(2)}) collective-permute-start(f32[4,192,256]{2,1,0:T(8,128)} %get-tuple-element.110), channel_id=1, source_target_pairs={{0,1},{1,2},{2,3},{3,0},{4,5},{5,6},{6,7},{7,4},{8,9},{9,10},{10,1... | collective-permute-start | bytes 2359304 | tf_op jit(solution)/shard_map/ppermute | solution.py:596
  (37 other events, 304.3 us)
